TPU v7x, 32 devices: a whole 2x2x4 slice. The times are simulated.
32 devices in a mesh: slab: 2 (over y), tile: 4 (over z), gz: 2 (over x), rep: 2 (over core).
Axes of the slice: x: 2, y: 2, z: 4, core: 2. Of those that a mesh axis runs over, the one named last changes fastest.
Arguments:
- fixed_image: bfloat16 [16, 256, 512], P(('slab', 'gz'), 'tile', 'rep'), parts along dimension 0, may hold values from -6 to 6
- moving_image: bfloat16 [16, 256, 512], P(('slab', 'gz'), 'tile', 'rep'), parts along dimension 0, may hold values from -6 to 6
- source_tile: int32 [8, 2, 8, 1], P('slab', 'rep'), parts along dimension 0, may hold values from 0 to 3; in each aligned block of 8 rows (0 to 7, 8 to 15, ..., all dimensions but the last counted through in order) at most 4 rows name the same one
- block_shifts: int32 [8, 2, 8, 2], P(('slab', 'tile'), 'rep'), parts along dimension 0, may hold values from 0 to 63
Outputs:
- spline_grad: float32 [3, 2, 16, 32], P(None, 'slab', 'tile', 'rep'), parts along dimension 1
There are 2 independent parts, one for each index of `slab`. A program takes and returns all parts, laid end to end along the dimension named above; each array names one. Nothing has to cross between parts.
Inputs may be any that keep to these rules, and one draw needn't show every extreme that they name: `source_tile`: among the 8 blocks of one device (one index pair of the first two dimensions) no tile is named more than 4 times; in every draw some device names one tile exactly 4 times.
All inputs are finite; a program needn't handle non-finite values.
Results may differ from a plain program's by a relative error of at most 0.00085.
Values may be sent and summed in bfloat16 or wider, within the bound.
No kernel may reach another device: no remote copies, remote signals or barrier semaphores. Data moves between devices by JAX's collectives and lax.ppermute only.
A program may use at most 64 MiB of HBM per device.

v0:
```python
import jax
import jax.numpy as jnp
from jax import lax
from jax.sharding import PartitionSpec as P

BLK_Y = 16
BLK_X = 128
RAD = 2
SPACING = 16


den_floor = 1e-05


def with_halo(array, sides, width):
    for axis, dim in sides:
        count, length = (lax.axis_size(axis), array.shape[dim])
        up = [(i, (i + 1) % count) for i in range(count - 1)]
        down = [(j, i) for i, j in up]
        last = lax.slice_in_dim(array, length - width, length, axis=dim)
        first = lax.slice_in_dim(array, 0, width, axis=dim)
        before = lax.ppermute(last, axis, up)
        after = lax.ppermute(first, axis, down)
        array = jnp.concatenate([before, array, after], axis=dim)
    return array


def window_sum(extended, radius):
    result = extended
    for axis_id in range(3):
        length = result.shape[axis_id] - 2 * radius
        summed = lax.slice_in_dim(result, 0, length, axis=axis_id)
        for offset in range(1, 2 * radius + 1):
            summed = summed + lax.slice_in_dim(result, offset, offset + length, axis=axis_id)
        result = summed
    return result


def window_terms(ext_fixed, ext_warp, radius):
    volume = float((2 * radius + 1) ** 3)
    sum_fixed = window_sum(ext_fixed, radius)
    sum_warp = window_sum(ext_warp, radius)
    sum_fixed_sq = window_sum(ext_fixed * ext_fixed, radius)
    sum_warp_sq = window_sum(ext_warp * ext_warp, radius)
    sum_product = window_sum(ext_fixed * ext_warp, radius)
    cross_term = sum_product - sum_fixed * sum_warp / volume
    fixed_var = sum_fixed_sq - sum_fixed * sum_fixed / volume
    warp_var = sum_warp_sq - sum_warp * sum_warp / volume
    denominator = fixed_var * warp_var + den_floor
    term_a = 2.0 * cross_term / denominator
    term_b = -cross_term * cross_term * fixed_var / (denominator * denominator)
    term_c = -(term_a * sum_fixed + 2.0 * term_b * sum_warp) / volume
    return (term_a, term_b, term_c)


def slopes(extended, margin, extent):
    result = []
    for axis_id in range(3):
        ahead = [margin, margin, margin]
        behind = [margin, margin, margin]
        ahead[axis_id] += 1
        behind[axis_id] -= 1
        upper = lax.slice(
            extended,
            tuple(ahead),
            (ahead[0] + extent[0], ahead[1] + extent[1], ahead[2] + extent[2]),
        )
        lower = lax.slice(
            extended,
            tuple(behind),
            (behind[0] + extent[0], behind[1] + extent[1], behind[2] + extent[2]),
        )
        result.append(0.5 * (upper - lower))
    return result


def spline_table(first_pos, length, first_col, columns):
    places = first_pos + jnp.arange(length, dtype=jnp.int32)
    knots = places // SPACING
    within = (places - knots * SPACING).astype(jnp.float32) / SPACING
    squares = within * within
    cubes = squares * within
    weights = (
        (1.0 - within) ** 3 / 6.0,
        (3.0 * cubes - 6.0 * squares + 4.0) / 6.0,
        (-3.0 * cubes + 3.0 * squares + 3.0 * within + 1.0) / 6.0,
        cubes / 6.0,
    )
    targets = first_col + jnp.arange(columns, dtype=jnp.int32)
    table = jnp.zeros((length, columns), jnp.float32)
    for offset in range(4):
        table = table + jnp.where(
            targets[None, :] == (knots + offset - 1)[:, None], weights[offset][:, None], 0.0
        )
    return table


def contract(pieces, table_z, table_y, table_x):
    highest = lax.Precision.HIGHEST
    along_x = jnp.einsum("czyx,xk->czyk", pieces, table_x, precision=highest)
    along_y = jnp.einsum("czyk,yj->czjk", along_x, table_y, precision=highest)
    return jnp.einsum("czjk,zl->cljk", along_y, table_z, precision=highest)


def roll_block(block, amounts):
    return jnp.roll(jnp.roll(block, amounts[0], axis=1), amounts[1], axis=2)


def fold_rims(extended, axis_id, owned):
    middle = lax.slice_in_dim(extended, 4, owned + 4, axis=axis_id)
    leading = lax.slice_in_dim(extended, 0, 2, axis=axis_id)
    trailing = lax.slice_in_dim(extended, owned + 6, owned + 8, axis=axis_id)
    lead_pad = [(0, 0), (0, 0), (0, 0), (0, 0)]
    trail_pad = [(0, 0), (0, 0), (0, 0), (0, 0)]
    lead_pad[axis_id] = (0, owned - 2)
    trail_pad[axis_id] = (owned - 2, 0)
    return middle + jnp.pad(leading, lead_pad) + jnp.pad(trailing, trail_pad)


def body(fixed_image, moving_image, source_tile, block_shifts):
    depth, height, width = fixed_image.shape
    yblocks = height // BLK_Y
    xblocks = width // BLK_X
    block_count = yblocks * xblocks
    tile_lists = source_tile[:, 0, :, 0]
    my_tile = lax.axis_index("tile")
    own_list = lax.dynamic_index_in_dim(tile_lists, my_tile, 0, keepdims=False)
    row_steps = jnp.arange(BLK_Y, dtype=jnp.int32)
    initial = jnp.zeros((block_count, depth, BLK_Y, BLK_X), jnp.bfloat16)
    piece = lax.all_gather(moving_image, "tile", axis=1, tiled=True)
    length = piece.shape[1]
    held_blocks = []
    for block_id in range(block_count):
        row_block = block_id // xblocks
        col_block = block_id % xblocks
        wanted = own_list[block_id] * height + row_block * BLK_Y + row_steps
        usable = (wanted >= 0) & (wanted < length)
        columns_part = lax.slice_in_dim(piece, col_block * BLK_X, (col_block + 1) * BLK_X, axis=2)
        taken = jnp.take(columns_part, jnp.clip(wanted, 0, length - 1), axis=1)
        held_blocks.append(jnp.where(usable[None, :, None], taken, initial[block_id]))
    blocks = jnp.stack(held_blocks)
    rolled = jax.vmap(roll_block)(blocks, block_shifts[0, 0])
    warped = (
        rolled.reshape(yblocks, xblocks, depth, BLK_Y, BLK_X)
        .transpose(2, 0, 3, 1, 4)
        .reshape(depth, height, width)
    )
    image_pair = jnp.stack((fixed_image, warped))
    fixed_own = fixed_image.astype(jnp.float32)
    warp_own = warped.astype(jnp.float32)
    extended = with_halo(image_pair, (("tile", 2), ("gz", 1), ("rep", 3)), RAD).astype(jnp.float32)
    term_a, term_b, term_c = window_terms(extended[0], extended[1], RAD)
    terms_ext = with_halo(
        jnp.stack((term_a, term_b, term_c)).astype(jnp.bfloat16),
        (("tile", 2), ("gz", 1), ("rep", 3)),
        RAD,
    ).astype(jnp.float32)
    box_a = window_sum(terms_ext[0], RAD)
    box_b = window_sum(terms_ext[1], RAD)
    box_c = window_sum(terms_ext[2], RAD)
    margin = RAD
    gain = -(fixed_own * box_a + 2.0 * warp_own * box_b + box_c)
    slope_z, slope_y, slope_x = slopes(extended[1], margin, (depth, height, width))
    pieces = jnp.stack((gain * slope_z, gain * slope_y, gain * slope_x))
    depth_total = depth * lax.axis_size("gz")
    depth_knots = (depth_total + SPACING - 1) // SPACING
    table_z = spline_table(lax.axis_index("gz") * depth, depth, 0, depth_knots)
    row_knots = height // SPACING
    table_y = spline_table(my_tile * height, height, my_tile * row_knots - 2, row_knots + 4)
    col_knots = width // SPACING
    rep_index = lax.axis_index("rep")
    table_x = spline_table(rep_index * width, width, rep_index * col_knots - 2, col_knots + 4)
    local_grad = contract(pieces, table_z, table_y, table_x)
    spread = with_halo(local_grad, (("tile", 2), ("rep", 3)), 2)
    owned_grad = fold_rims(fold_rims(spread, 2, row_knots), 3, col_knots)
    return lax.psum(owned_grad, "gz")


def solution(mesh):
    return jax.shard_map(
        body,
        mesh=mesh,
        in_specs=(
            P(("slab", "gz"), "tile", "rep"),
            P(("slab", "gz"), "tile", "rep"),
            P("slab", "rep", None, None),
            P(("slab", "tile"), "rep", None, None),
        ),
        out_specs=P(None, "slab", "tile", "rep"),
        check_vma=False,
    )
```

profile of v0, /device:TPU:0, one launch (start us, length us, event | category | flops | bytes accessed | tf_op | source)
XLA Modules:
  0.0 109.7 jit_solution(7598929801452606011)
XLA Ops:
  0.0 0.7 copy-done
  0.7 0.7 fusion.184
  6.7 1.0 copy.20
  7.7 17.4 %all_gather.3 = bf16[4,256,256]{2,0,1:T(4,128)(2,1)S(1)} all-gather(bf16[4,64,256]{2,0,1:T(4,128)(2,1)S(1)} %copy.20), channel_id=1, replica_groups=mesh['slab'=2,'tile'=4,'gz'=2,'rep'=2] {'tile'}, dimensions={1}, use_global_device_ids=true | all-gather | bytes 655360 | tf_op jit(solution)/shard_map/all_gather | solution.py:130
  25.1 0.2 fusion.179
  25.3 0.6 gather_fusion.2
  25.9 0.6 gather_fusion.4
  26.5 0.6 gather_fusion.3
  27.0 0.6 gather_fusion.5
  27.6 0.6 gather_fusion.6
  28.2 0.6 gather_fusion.7
  28.8 0.6 gather_fusion.8
  29.4 0.6 gather_fusion.9
  31.2 0.7 gather_fusion
  32.0 1.9 %copy.22 = bf16[8,4,16,256]{2,1,0,3:T(4,128)(2,1)S(1)} copy(bf16[8,4,16,256]{3,1,2,0:T(4,128)(2,1)S(1)} %pad_maximum_fusion.5) | data formatting | bytes 524288 | tf_op jit(solution)/shard_map/vmap(jit(_roll_dynamic))/concatenate | solution.py:106
  33.9 1.8 %gather_fusion.1 = bf16[8,4,16,128]{2,1,3,0:T(4,128)(2,1)S(1)} fusion(bf16[8,4,16,256]{2,1,0,3:T(4,128)(2,1)S(1)} %copy.22, s32[8]{0:T(128)S(1)} %get-tuple-element.44), kind=kCustom, calls=%fused_computation.9 | custom fusion | bytes 262272 | tf_op jit(solution)/shard_map/vmap(jit(_roll_dynamic))/gather | solution.py:106
  35.7 0.6 copy.23
  36.4 1.3 %collective-permute-start.1 = (bf16[2,4,2,256]{3,2,1,0:T(2,128)(2,1)S(1)}, bf16[2,4,2,256]{3,2,1,0:T(2,128)(2,1)S(1)}, u32[]{:S(2)}, u32[]{:S(2)}) collective-permute-start(bf16[2,4,2,256]{3,2,1,0:T(2,128)(2,1)S(1)} %get-tuple-element.39), channel_id=1, source_target_pairs={{4,0},{8,4},{12,8},{5,1},{9,5},{13,9},{6,2},{10,6},{14,10},{7,3},{... | collective-permute-start | bytes 24584 | tf_op jit(solution)/shard_map/ppermute | solution.py:23
  37.7 4.7 %collective-permute-start = (bf16[2,4,2,256]{3,2,1,0:T(2,128)(2,1)S(1)}, bf16[2,4,2,256]{3,2,1,0:T(2,128)(2,1)S(1)}, u32[]{:S(2)}, u32[]{:S(2)}) collective-permute-start(bf16[2,4,2,256]{3,2,1,0:T(2,128)(2,1)S(1)} %get-tuple-element.38), channel_id=1, source_target_pairs={{0,4},{4,8},{8,12},{1,5},{5,9},{9,13},{2,6},{6,10},{10,14},{3,7},{... | collective-permute-start | bytes 24584 | tf_op jit(solution)/shard_map/ppermute | solution.py:22
  42.6 1.1 %collective-permute-done = bf16[2,4,2,256]{3,2,1,0:T(2,128)(2,1)S(1)} collective-permute-done((bf16[2,4,2,256]{3,2,1,0:T(2,128)(2,1)S(1)}, bf16[2,4,2,256]{3,2,1,0:T(2,128)(2,1)S(1)}, u32[]{:S(2)}, u32[]{:S(2)}) %collective-permute-start) | collective-permute-done | bytes 8224 | tf_op jit(solution)/shard_map/ppermute | solution.py:22
  43.9 1.3 %collective-permute-start.3 = (bf16[2,2,68,256]{3,2,1,0:T(8,128)(2,1)S(1)}, bf16[2,2,68,256]{3,2,1,0:T(8,128)(2,1)S(1)}, u32[]{:S(2)}, u32[]{:S(2)}) collective-permute-start(bf16[2,2,68,256]{3,2,1,0:T(8,128)(2,1)S(1)} %get-tuple-element.37), channel_id=1, source_target_pairs={{2,0},{3,1},{6,4},{7,5},{10,8},{11,9},{14,12},{15,13},{18,16},{19,... | collective-permute-start | bytes 417800 | tf_op jit(solution)/shard_map/ppermute | solution.py:23
  45.2 4.6 %collective-permute-start.2 = (bf16[2,2,68,256]{3,2,1,0:T(8,128)(2,1)S(1)}, bf16[2,2,68,256]{3,2,1,0:T(8,128)(2,1)S(1)}, u32[]{:S(2)}, u32[]{:S(2)}) collective-permute-start(bf16[2,2,68,256]{3,2,1,0:T(8,128)(2,1)S(1)} %get-tuple-element.36), channel_id=1, source_target_pairs={{0,2},{1,3},{4,6},{5,7},{8,10},{9,11},{12,14},{13,15},{16,18},{17,... | collective-permute-start | bytes 417800 | tf_op jit(solution)/shard_map/ppermute | solution.py:22
  49.8 1.1 %collective-permute-done.3 = bf16[2,2,68,256]{3,2,1,0:T(8,128)(2,1)S(1)} collective-permute-done((bf16[2,2,68,256]{3,2,1,0:T(8,128)(2,1)S(1)}, bf16[2,2,68,256]{3,2,1,0:T(8,128)(2,1)S(1)}, u32[]{:S(2)}, u32[]{:S(2)}) %collective-permute-start.3) | collective-permute-done | bytes 139296 | tf_op jit(solution)/shard_map/ppermute | solution.py:23
  50.9 1.5 %collective-permute-done.2 = bf16[2,2,68,256]{3,2,1,0:T(8,128)(2,1)S(1)} collective-permute-done((bf16[2,2,68,256]{3,2,1,0:T(8,128)(2,1)S(1)}, bf16[2,2,68,256]{3,2,1,0:T(8,128)(2,1)S(1)}, u32[]{:S(2)}, u32[]{:S(2)}) %collective-permute-start.2) | collective-permute-done | bytes 139296 | tf_op jit(solution)/shard_map/ppermute | solution.py:22
  52.6 1.3 %collective-permute-start.5 = (bf16[2,8,68,2]{3,2,1,0:T(8,128)(2,1)S(1)}, bf16[2,8,68,2]{3,2,1,0:T(8,128)(2,1)S(1)}, u32[]{:S(2)}, u32[]{:S(2)}) collective-permute-start(bf16[2,8,68,2]{3,2,1,0:T(8,128)(2,1)S(1)} %get-tuple-element.29), channel_id=1, source_target_pairs={{1,0},{3,2},{5,4},{7,6},{9,8},{11,10},{13,12},{15,14},{17,16},{19,... | collective-permute-start | bytes 13064 | tf_op jit(solution)/shard_map/ppermute | solution.py:23
  53.9 3.1 %collective-permute-start.4 = (bf16[2,8,68,2]{3,2,1,0:T(8,128)(2,1)S(1)}, bf16[2,8,68,2]{3,2,1,0:T(8,128)(2,1)S(1)}, u32[]{:S(2)}, u32[]{:S(2)}) collective-permute-start(bf16[2,8,68,2]{3,2,1,0:T(8,128)(2,1)S(1)} %get-tuple-element.28), channel_id=1, source_target_pairs={{0,1},{2,3},{4,5},{6,7},{8,9},{10,11},{12,13},{14,15},{16,17},{18,... | collective-permute-start | bytes 13064 | tf_op jit(solution)/shard_map/ppermute | solution.py:22
  57.0 1.1 %collective-permute-done.4 = bf16[2,8,68,2]{3,2,1,0:T(8,128)(2,1)S(1)} collective-permute-done((bf16[2,8,68,2]{3,2,1,0:T(8,128)(2,1)S(1)}, bf16[2,8,68,2]{3,2,1,0:T(8,128)(2,1)S(1)}, u32[]{:S(2)}, u32[]{:S(2)}) %collective-permute-start.4) | collective-permute-done | bytes 4384 | tf_op jit(solution)/shard_map/ppermute | solution.py:22
  58.2 0.6 maximum_convert_fusion.1
  58.8 0.2 fusion
  59.2 0.2 slice_add_fusion.44
  59.4 0.2 slice_add_fusion.60
  59.7 0.2 slice_add_fusion.48
  59.8 0.2 slice_add_fusion.56
  60.2 1.4 %convert_bitcast_fusion.1 = (bf16[1,4,64,256]{3,2,1,0:T(8,128)(2,1)S(1)}, f32[4,64,256]{2,1,0:T(8,128)S(1)}, f32[4,64,256]{2,1,0:T(8,128)S(1)}, f32[4,64,256]{2,...) fusion(f32[4,64,260]{2,1,0:T(8,128)S(1)} %slice_add_fusion.44, ...), kind=kLoop, calls=%fused_computation.160 | loop fusion | flops 2228224 | bytes 7995392 | tf_op jit(solution)/shard_map/stack | solution.py:154
  61.8 1.3 %collective-permute-start.7 = (bf16[3,4,2,256]{3,2,1,0:T(2,128)(2,1)S(1)}, bf16[3,4,2,256]{3,2,1,0:T(2,128)(2,1)S(1)}, u32[]{:S(2)}, u32[]{:S(2)}) collective-permute-start(bf16[3,4,2,256]{3,2,1,0:T(2,128)(2,1)S(1)} %get-tuple-element.35), channel_id=1, source_target_pairs={{4,0},{8,4},{12,8},{5,1},{9,5},{13,9},{6,2},{10,6},{14,10},{7,3},{... | collective-permute-start | bytes 36872 | tf_op jit(solution)/shard_map/ppermute | solution.py:23
  63.1 4.8 %collective-permute-start.6 = (bf16[3,4,2,256]{3,2,1,0:T(2,128)(2,1)S(1)}, bf16[3,4,2,256]{3,2,1,0:T(2,128)(2,1)S(1)}, u32[]{:S(2)}, u32[]{:S(2)}) collective-permute-start(bf16[3,4,2,256]{3,2,1,0:T(2,128)(2,1)S(1)} %get-tuple-element.34), channel_id=1, source_target_pairs={{0,4},{4,8},{8,12},{1,5},{5,9},{9,13},{2,6},{6,10},{10,14},{3,7},{... | collective-permute-start | bytes 36872 | tf_op jit(solution)/shard_map/ppermute | solution.py:22
  68.0 0.2 mul.379
  68.2 1.1 %collective-permute-done.6 = bf16[3,4,2,256]{3,2,1,0:T(2,128)(2,1)S(1)} collective-permute-done((bf16[3,4,2,256]{3,2,1,0:T(2,128)(2,1)S(1)}, bf16[3,4,2,256]{3,2,1,0:T(2,128)(2,1)S(1)}, u32[]{:S(2)}, u32[]{:S(2)}) %collective-permute-start.6) | collective-permute-done | bytes 12320 | tf_op jit(solution)/shard_map/ppermute | solution.py:22
  69.3 0.2 pad_maximum_fusion.2
  69.5 1.3 %collective-permute-start.9 = (bf16[3,2,68,256]{3,2,1,0:T(8,128)(2,1)S(1)}, bf16[3,2,68,256]{3,2,1,0:T(8,128)(2,1)S(1)}, u32[]{:S(2)}, u32[]{:S(2)}) collective-permute-start(bf16[3,2,68,256]{3,2,1,0:T(8,128)(2,1)S(1)} %get-tuple-element.33), channel_id=1, source_target_pairs={{2,0},{3,1},{6,4},{7,5},{10,8},{11,9},{14,12},{15,13},{18,16},{19,... | collective-permute-start | bytes 626696 | tf_op jit(solution)/shard_map/ppermute | solution.py:23
  70.8 4.6 %collective-permute-start.8 = (bf16[3,2,68,256]{3,2,1,0:T(8,128)(2,1)S(1)}, bf16[3,2,68,256]{3,2,1,0:T(8,128)(2,1)S(1)}, u32[]{:S(2)}, u32[]{:S(2)}) collective-permute-start(bf16[3,2,68,256]{3,2,1,0:T(8,128)(2,1)S(1)} %get-tuple-element.32), channel_id=1, source_target_pairs={{0,2},{1,3},{4,6},{5,7},{8,10},{9,11},{12,14},{13,15},{16,18},{17,... | collective-permute-start | bytes 626696 | tf_op jit(solution)/shard_map/ppermute | solution.py:22
  75.5 2.9 %collective-permute-done.9 = bf16[3,2,68,256]{3,2,1,0:T(8,128)(2,1)S(1)} collective-permute-done((bf16[3,2,68,256]{3,2,1,0:T(8,128)(2,1)S(1)}, bf16[3,2,68,256]{3,2,1,0:T(8,128)(2,1)S(1)}, u32[]{:S(2)}, u32[]{:S(2)}) %collective-permute-start.9) | collective-permute-done | bytes 208928 | tf_op jit(solution)/shard_map/ppermute | solution.py:23
  78.4 1.2 %collective-permute-done.8 = bf16[3,2,68,256]{3,2,1,0:T(8,128)(2,1)S(1)} collective-permute-done((bf16[3,2,68,256]{3,2,1,0:T(8,128)(2,1)S(1)}, bf16[3,2,68,256]{3,2,1,0:T(8,128)(2,1)S(1)}, u32[]{:S(2)}, u32[]{:S(2)}) %collective-permute-start.8) | collective-permute-done | bytes 208928 | tf_op jit(solution)/shard_map/ppermute | solution.py:22
  79.6 0.2 pad_maximum_fusion
  79.8 0.2 fusion.177
  80.0 1.3 %collective-permute-start.11 = (bf16[3,8,68,2]{3,2,1,0:T(8,128)(2,1)S(1)}, bf16[3,8,68,2]{3,2,1,0:T(8,128)(2,1)S(1)}, u32[]{:S(2)}, u32[]{:S(2)}) collective-permute-start(bf16[3,8,68,2]{3,2,1,0:T(8,128)(2,1)S(1)} %get-tuple-element.27), channel_id=1, source_target_pairs={{1,0},{3,2},{5,4},{7,6},{9,8},{11,10},{13,12},{15,14},{17,16},{19,... | collective-permute-start | bytes 19592 | tf_op jit(solution)/shard_map/ppermute | solution.py:23
  81.3 3.3 %collective-permute-start.10 = (bf16[3,8,68,2]{3,2,1,0:T(8,128)(2,1)S(1)}, bf16[3,8,68,2]{3,2,1,0:T(8,128)(2,1)S(1)}, u32[]{:S(2)}, u32[]{:S(2)}) collective-permute-start(bf16[3,8,68,2]{3,2,1,0:T(8,128)(2,1)S(1)} %get-tuple-element.26), channel_id=1, source_target_pairs={{0,1},{2,3},{4,5},{6,7},{8,9},{10,11},{12,13},{14,15},{16,17},{18,... | collective-permute-start | bytes 19592 | tf_op jit(solution)/shard_map/ppermute | solution.py:22
  84.7 1.1 %collective-permute-done.10 = bf16[3,8,68,2]{3,2,1,0:T(8,128)(2,1)S(1)} collective-permute-done((bf16[3,8,68,2]{3,2,1,0:T(8,128)(2,1)S(1)}, bf16[3,8,68,2]{3,2,1,0:T(8,128)(2,1)S(1)}, u32[]{:S(2)}, u32[]{:S(2)}) %collective-permute-start.10) | collective-permute-done | bytes 6560 | tf_op jit(solution)/shard_map/ppermute | solution.py:22
  85.8 0.9 maximum_convert_fusion
  86.7 0.2 fusion.10
  86.9 0.2 slice_add_fusion.32
  87.1 0.2 slice_add_fusion.36
  87.4 1.0 fusion.23
  88.5 0.3 fusion.20
  88.8 1.1 fusion.2
  89.9 0.9 convolution_bitcast_fusion
  90.7 0.3 fusion.35
  91.0 1.3 %collective-permute-start.13 = (f32[3,1,2,20]{3,2,1,0:T(2,128)S(1)}, f32[3,1,2,20]{3,2,1,0:T(2,128)S(1)}, u32[]{:S(2)}, u32[]{:S(2)}) collective-permute-start(f32[3,1,2,20]{3,2,1,0:T(2,128)S(1)} %get-tuple-element.43), channel_id=1, source_target_pairs={{4,0},{8,4},{12,8},{5,1},{9,5},{13,9},{6,2},{10,6},{14,10},{7,3},{... | collective-permute-start | bytes 1448 | tf_op jit(solution)/shard_map/ppermute | solution.py:23
  92.3 4.6 %collective-permute-start.12 = (f32[3,1,2,20]{3,2,1,0:T(2,128)S(1)}, f32[3,1,2,20]{3,2,1,0:T(2,128)S(1)}, u32[]{:S(2)}, u32[]{:S(2)}) collective-permute-start(f32[3,1,2,20]{3,2,1,0:T(2,128)S(1)} %get-tuple-element.42), channel_id=1, source_target_pairs={{0,4},{4,8},{8,12},{1,5},{5,9},{9,13},{2,6},{6,10},{10,14},{3,7},{... | collective-permute-start | bytes 1448 | tf_op jit(solution)/shard_map/ppermute | solution.py:22
  96.9 1.3 %collective-permute-done.12 = f32[3,1,2,20]{3,2,1,0:T(2,128)S(1)} collective-permute-done((f32[3,1,2,20]{3,2,1,0:T(2,128)S(1)}, f32[3,1,2,20]{3,2,1,0:T(2,128)S(1)}, u32[]{:S(2)}, u32[]{:S(2)}) %collective-permute-start.12) | collective-permute-done | bytes 512 | tf_op jit(solution)/shard_map/ppermute | solution.py:22
  98.3 1.3 %collective-permute-start.15 = (f32[3,1,12,2]{3,2,1,0:T(8,128)S(1)}, f32[3,1,12,2]{3,2,1,0:T(8,128)S(1)}, u32[]{:S(2)}, u32[]{:S(2)}) collective-permute-start(f32[3,1,12,2]{3,2,1,0:T(8,128)S(1)} %get-tuple-element.41), channel_id=1, source_target_pairs={{1,0},{3,2},{5,4},{7,6},{9,8},{11,10},{13,12},{15,14},{17,16},{19,... | collective-permute-start | bytes 872 | tf_op jit(solution)/shard_map/ppermute | solution.py:23
  99.6 3.0 %collective-permute-start.14 = (f32[3,1,12,2]{3,2,1,0:T(8,128)S(1)}, f32[3,1,12,2]{3,2,1,0:T(8,128)S(1)}, u32[]{:S(2)}, u32[]{:S(2)}) collective-permute-start(f32[3,1,12,2]{3,2,1,0:T(8,128)S(1)} %get-tuple-element.40), channel_id=1, source_target_pairs={{0,1},{2,3},{4,5},{6,7},{8,9},{10,11},{12,13},{14,15},{16,17},{18,... | collective-permute-start | bytes 872 | tf_op jit(solution)/shard_map/ppermute | solution.py:22
  102.6 0.8 collective-permute-done.14
  103.7 6.0 %psum.7 = f32[3,1,4,16]{3,2,1,0:T(4,128)} all-reduce(f32[3,1,4,16]{3,2,1,0:T(4,128)S(1)} %fusion.60), channel_id=1, replica_groups=mesh['slab'=2,'tile'=4,'gz'=2,'rep'=2] {'gz'}, use_global_device_ids=true, to_apply=%region_0.2 | all-reduce | flops 192 | bytes 1536 | tf_op jit(solution)/shard_map/psum | solution.py:176
  (82 shorter events, 3.4 us)
Async XLA Ops:
  0.0 0.7 copy-start
  5.3 25.9 %copy-start.2 = (s32[1,1,8,2]{2,3,1,0:T(2,128)S(1)}, s32[1,1,8,2]{2,3,1,0:T(2,128)}, u32[]{:S(2)}) copy-start(s32[1,1,8,2]{2,3,1,0:T(2,128)} %param.9) | copy-start | bytes 196
  32.0 4.4 %copy-start.1 = (bf16[4,64,256]{2,1,0:T(8,128)(2,1)S(1)}, bf16[4,64,256]{2,1,0:T(8,128)(2,1)}, u32[]{:S(2)}) copy-start(bf16[4,64,256]{2,1,0:T(8,128)(2,1)} %param.6) | copy-start | bytes 393220
  36.4 6.2 %collective-permute-start.1 = (bf16[2,4,2,256]{3,2,1,0:T(2,128)(2,1)S(1)}, bf16[2,4,2,256]{3,2,1,0:T(2,128)(2,1)S(1)}, u32[]{:S(2)}, u32[]{:S(2)}) collective-permute-start(bf16[2,4,2,256]{3,2,1,0:T(2,128)(2,1)S(1)} %get-tuple-element.39), channel_id=1, source_target_pairs={{4,0},{8,4},{12,8},{5,1},{9,5},{13,9},{6,2},{10,6},{14,10},{7,3},{... | collective-permute-start | bytes 24584 | tf_op jit(solution)/shard_map/ppermute | solution.py:23
  37.7 6.0 %collective-permute-start = (bf16[2,4,2,256]{3,2,1,0:T(2,128)(2,1)S(1)}, bf16[2,4,2,256]{3,2,1,0:T(2,128)(2,1)S(1)}, u32[]{:S(2)}, u32[]{:S(2)}) collective-permute-start(bf16[2,4,2,256]{3,2,1,0:T(2,128)(2,1)S(1)} %get-tuple-element.38), channel_id=1, source_target_pairs={{0,4},{4,8},{8,12},{1,5},{5,9},{9,13},{2,6},{6,10},{10,14},{3,7},{... | collective-permute-start | bytes 24584 | tf_op jit(solution)/shard_map/ppermute | solution.py:22
  43.9 7.0 %collective-permute-start.3 = (bf16[2,2,68,256]{3,2,1,0:T(8,128)(2,1)S(1)}, bf16[2,2,68,256]{3,2,1,0:T(8,128)(2,1)S(1)}, u32[]{:S(2)}, u32[]{:S(2)}) collective-permute-start(bf16[2,2,68,256]{3,2,1,0:T(8,128)(2,1)S(1)} %get-tuple-element.37), channel_id=1, source_target_pairs={{2,0},{3,1},{6,4},{7,5},{10,8},{11,9},{14,12},{15,13},{18,16},{19,... | collective-permute-start | bytes 417800 | tf_op jit(solution)/shard_map/ppermute | solution.py:23
  45.2 7.2 %collective-permute-start.2 = (bf16[2,2,68,256]{3,2,1,0:T(8,128)(2,1)S(1)}, bf16[2,2,68,256]{3,2,1,0:T(8,128)(2,1)S(1)}, u32[]{:S(2)}, u32[]{:S(2)}) collective-permute-start(bf16[2,2,68,256]{3,2,1,0:T(8,128)(2,1)S(1)} %get-tuple-element.36), channel_id=1, source_target_pairs={{0,2},{1,3},{4,6},{5,7},{8,10},{9,11},{12,14},{13,15},{16,18},{17,... | collective-permute-start | bytes 417800 | tf_op jit(solution)/shard_map/ppermute | solution.py:22
  52.6 4.4 %collective-permute-start.5 = (bf16[2,8,68,2]{3,2,1,0:T(8,128)(2,1)S(1)}, bf16[2,8,68,2]{3,2,1,0:T(8,128)(2,1)S(1)}, u32[]{:S(2)}, u32[]{:S(2)}) collective-permute-start(bf16[2,8,68,2]{3,2,1,0:T(8,128)(2,1)S(1)} %get-tuple-element.29), channel_id=1, source_target_pairs={{1,0},{3,2},{5,4},{7,6},{9,8},{11,10},{13,12},{15,14},{17,16},{19,... | collective-permute-start | bytes 13064 | tf_op jit(solution)/shard_map/ppermute | solution.py:23
  53.9 4.2 %collective-permute-start.4 = (bf16[2,8,68,2]{3,2,1,0:T(8,128)(2,1)S(1)}, bf16[2,8,68,2]{3,2,1,0:T(8,128)(2,1)S(1)}, u32[]{:S(2)}, u32[]{:S(2)}) collective-permute-start(bf16[2,8,68,2]{3,2,1,0:T(8,128)(2,1)S(1)} %get-tuple-element.28), channel_id=1, source_target_pairs={{0,1},{2,3},{4,5},{6,7},{8,9},{10,11},{12,13},{14,15},{16,17},{18,... | collective-permute-start | bytes 13064 | tf_op jit(solution)/shard_map/ppermute | solution.py:22
  61.8 6.4 %collective-permute-start.7 = (bf16[3,4,2,256]{3,2,1,0:T(2,128)(2,1)S(1)}, bf16[3,4,2,256]{3,2,1,0:T(2,128)(2,1)S(1)}, u32[]{:S(2)}, u32[]{:S(2)}) collective-permute-start(bf16[3,4,2,256]{3,2,1,0:T(2,128)(2,1)S(1)} %get-tuple-element.35), channel_id=1, source_target_pairs={{4,0},{8,4},{12,8},{5,1},{9,5},{13,9},{6,2},{10,6},{14,10},{7,3},{... | collective-permute-start | bytes 36872 | tf_op jit(solution)/shard_map/ppermute | solution.py:23
  63.1 6.2 %collective-permute-start.6 = (bf16[3,4,2,256]{3,2,1,0:T(2,128)(2,1)S(1)}, bf16[3,4,2,256]{3,2,1,0:T(2,128)(2,1)S(1)}, u32[]{:S(2)}, u32[]{:S(2)}) collective-permute-start(bf16[3,4,2,256]{3,2,1,0:T(2,128)(2,1)S(1)} %get-tuple-element.34), channel_id=1, source_target_pairs={{0,4},{4,8},{8,12},{1,5},{5,9},{9,13},{2,6},{6,10},{10,14},{3,7},{... | collective-permute-start | bytes 36872 | tf_op jit(solution)/shard_map/ppermute | solution.py:22
  69.5 8.8 %collective-permute-start.9 = (bf16[3,2,68,256]{3,2,1,0:T(8,128)(2,1)S(1)}, bf16[3,2,68,256]{3,2,1,0:T(8,128)(2,1)S(1)}, u32[]{:S(2)}, u32[]{:S(2)}) collective-permute-start(bf16[3,2,68,256]{3,2,1,0:T(8,128)(2,1)S(1)} %get-tuple-element.33), channel_id=1, source_target_pairs={{2,0},{3,1},{6,4},{7,5},{10,8},{11,9},{14,12},{15,13},{18,16},{19,... | collective-permute-start | bytes 626696 | tf_op jit(solution)/shard_map/ppermute | solution.py:23
  70.8 8.7 %collective-permute-start.8 = (bf16[3,2,68,256]{3,2,1,0:T(8,128)(2,1)S(1)}, bf16[3,2,68,256]{3,2,1,0:T(8,128)(2,1)S(1)}, u32[]{:S(2)}, u32[]{:S(2)}) collective-permute-start(bf16[3,2,68,256]{3,2,1,0:T(8,128)(2,1)S(1)} %get-tuple-element.32), channel_id=1, source_target_pairs={{0,2},{1,3},{4,6},{5,7},{8,10},{9,11},{12,14},{13,15},{16,18},{17,... | collective-permute-start | bytes 626696 | tf_op jit(solution)/shard_map/ppermute | solution.py:22
  80.0 4.6 %collective-permute-start.11 = (bf16[3,8,68,2]{3,2,1,0:T(8,128)(2,1)S(1)}, bf16[3,8,68,2]{3,2,1,0:T(8,128)(2,1)S(1)}, u32[]{:S(2)}, u32[]{:S(2)}) collective-permute-start(bf16[3,8,68,2]{3,2,1,0:T(8,128)(2,1)S(1)} %get-tuple-element.27), channel_id=1, source_target_pairs={{1,0},{3,2},{5,4},{7,6},{9,8},{11,10},{13,12},{15,14},{17,16},{19,... | collective-permute-start | bytes 19592 | tf_op jit(solution)/shard_map/ppermute | solution.py:23
  81.3 4.5 %collective-permute-start.10 = (bf16[3,8,68,2]{3,2,1,0:T(8,128)(2,1)S(1)}, bf16[3,8,68,2]{3,2,1,0:T(8,128)(2,1)S(1)}, u32[]{:S(2)}, u32[]{:S(2)}) collective-permute-start(bf16[3,8,68,2]{3,2,1,0:T(8,128)(2,1)S(1)} %get-tuple-element.26), channel_id=1, source_target_pairs={{0,1},{2,3},{4,5},{6,7},{8,9},{10,11},{12,13},{14,15},{16,17},{18,... | collective-permute-start | bytes 19592 | tf_op jit(solution)/shard_map/ppermute | solution.py:22
  88.4 15.0 %copy-start.3 = (pred[4]{0:T(512)(128)(4,1)S(1)}, pred[4]{0:T(512)(128)(4,1)}, u32[]{:S(2)}) copy-start(pred[4]{0:T(512)(128)(4,1)} %constant.244.clone.1) | copy-start | bytes 16
  88.4 15.2 %copy-start.4 = (pred[16]{0:T(512)(128)(4,1)S(1)}, pred[16]{0:T(512)(128)(4,1)}, u32[]{:S(2)}) copy-start(pred[16]{0:T(512)(128)(4,1)} %constant.245.clone.1) | copy-start | bytes 52
  91.0 5.9 %collective-permute-start.13 = (f32[3,1,2,20]{3,2,1,0:T(2,128)S(1)}, f32[3,1,2,20]{3,2,1,0:T(2,128)S(1)}, u32[]{:S(2)}, u32[]{:S(2)}) collective-permute-start(f32[3,1,2,20]{3,2,1,0:T(2,128)S(1)} %get-tuple-element.43), channel_id=1, source_target_pairs={{4,0},{8,4},{12,8},{5,1},{9,5},{13,9},{6,2},{10,6},{14,10},{7,3},{... | collective-permute-start | bytes 1448 | tf_op jit(solution)/shard_map/ppermute | solution.py:23
  92.3 5.9 %collective-permute-start.12 = (f32[3,1,2,20]{3,2,1,0:T(2,128)S(1)}, f32[3,1,2,20]{3,2,1,0:T(2,128)S(1)}, u32[]{:S(2)}, u32[]{:S(2)}) collective-permute-start(f32[3,1,2,20]{3,2,1,0:T(2,128)S(1)} %get-tuple-element.42), channel_id=1, source_target_pairs={{0,4},{4,8},{8,12},{1,5},{5,9},{9,13},{2,6},{6,10},{10,14},{3,7},{... | collective-permute-start | bytes 1448 | tf_op jit(solution)/shard_map/ppermute | solution.py:22
  98.3 4.3 %collective-permute-start.15 = (f32[3,1,12,2]{3,2,1,0:T(8,128)S(1)}, f32[3,1,12,2]{3,2,1,0:T(8,128)S(1)}, u32[]{:S(2)}, u32[]{:S(2)}) collective-permute-start(f32[3,1,12,2]{3,2,1,0:T(8,128)S(1)} %get-tuple-element.41), channel_id=1, source_target_pairs={{1,0},{3,2},{5,4},{7,6},{9,8},{11,10},{13,12},{15,14},{17,16},{19,... | collective-permute-start | bytes 872 | tf_op jit(solution)/shard_map/ppermute | solution.py:23
  99.6 3.9 %collective-permute-start.14 = (f32[3,1,12,2]{3,2,1,0:T(8,128)S(1)}, f32[3,1,12,2]{3,2,1,0:T(8,128)S(1)}, u32[]{:S(2)}, u32[]{:S(2)}) collective-permute-start(f32[3,1,12,2]{3,2,1,0:T(8,128)S(1)} %get-tuple-element.40), channel_id=1, source_target_pairs={{0,1},{2,3},{4,5},{6,7},{8,9},{10,11},{12,13},{14,15},{16,17},{18,... | collective-permute-start | bytes 872 | tf_op jit(solution)/shard_map/ppermute | solution.py:22
where the time goes:
time: 111 us; the launch traced here: 110 us
  starting transfers between devices  42.9 us (39%)
  blocking collectives  23.4 us (21%)
  waiting for transfers between devices  13.4 us (12%)
  local copies, waits for them, and re-layouts  13.3 us (12%)
  other arithmetic  8.79 us (8%)
  between operations  5.84 us (5%)
  matrix products  2.18 us (2%)
    ppermute x8, starting transfers between devices, with_halo(): before = lax.ppermute(last, axis, up)  32.6 us
    all_gather x1, blocking collectives, body(): piece = lax.all_gather(moving_image, 'tile', axis=1, tiled=True)  17.4 us
    ppermute x8, starting transfers between devices, with_halo(): after = lax.ppermute(first, axis, down)  10.3 us
    ppermute x8, waiting for transfers between devices, with_halo(): before = lax.ppermute(last, axis, up)  9.28 us
    psum x1, blocking collectives, body(): return lax.psum(owned_grad, 'gz')  6.01 us
    gather x8, local copies, waits for them, and re-layouts, body(): taken = jnp.take(columns_part, jnp.clip(wanted, 0, length - 1), axis=1)  4.71 us
    ppermute x8, waiting for transfers between devices, with_halo(): after = lax.ppermute(first, axis, down)  4.08 us
    gather x2, local copies, waits for them, and re-layouts, roll_block(): return jnp.roll(jnp.roll(block, amounts[0], axis=1), amounts[1], axis=2)  2.45 us
  transfers between devices with their start and end apart: 16, of which 10 were waited for; matrix products, arithmetic and copies ran while one was open for 0% of the time, Pallas kernels for 0%

commit v1 on v0

--- a/solution.py
+++ b/solution.py
@@ -1,16 +1,20 @@
+import functools
+
 import jax
 import jax.numpy as jnp
 from jax import lax
+from jax.experimental import pallas as pl
+from jax.experimental.pallas import tpu as pltpu
 from jax.sharding import PartitionSpec as P
 
 BLK_Y = 16
 BLK_X = 128
 RAD = 2
 SPACING = 16
+MAX_NAMED = 4
 
 
 den_floor = 1e-05
-
 
 def with_halo(array, sides, width):
     for axis, dim in sides:
@@ -176,9 +180,308 @@
     return lax.psum(owned_grad, "gz")
 
 
+EDGE = 2 * RAD
+SEND_ROWS = 48
+
+
+def pack_kernel(tiles, source_ref, place_ref, moving_ref, fixed_ref, *out_refs):
+    me, half = place_ref[0], place_ref[1]
+    packs, fixed_out = out_refs[:-1], out_refs[-1]
+    height, width = moving_ref.shape[1:]
+    xblocks = width // BLK_X
+    blocks = (height // BLK_Y) * xblocks
+    for step in range(1, tiles):
+        pack = packs[step - 1]
+        pack[...] = jnp.zeros_like(pack)
+        other = lax.bitwise_xor(me, step)
+        count = jnp.int32(0)
+        for block in range(blocks):
+            row, col = (block // xblocks) * BLK_Y, (block % xblocks) * BLK_X
+            named = source_ref[other, block] == me
+
+            @pl.when(named)
+            def _(pack=pack, count=count, row=row, col=col):
+                slot = jnp.minimum(count, pack.shape[0] - 1)
+                pack[slot] = moving_ref[:, row : row + BLK_Y, col : col + BLK_X]
+
+            count = count + named.astype(jnp.int32)
+    start = pl.multiple_of((1 - half) * BLK_Y, BLK_Y)
+    fixed_out[...] = fixed_ref[:, pl.ds(start, SEND_ROWS), :]
+
+
+def unpack_kernel(tiles, source_ref, shift_ref, place_ref, moving_ref, fixed_ref, *refs):
+    recvs = refs[: tiles - 1]
+    own_ref, send_ref, straight_ref, slant_ref, rims = refs[tiles - 1 :]
+    me, half = place_ref[0], place_ref[1]
+    depth, height, width = moving_ref.shape
+    xblocks = width // BLK_X
+    blocks = (height // BLK_Y) * xblocks
+    cap = recvs[0].shape[0]
+    for block in range(blocks):
+        row, col = (block // xblocks) * BLK_Y, (block % xblocks) * BLK_X
+        source = source_ref[me, block]
+        slot = jnp.int32(0)
+        for earlier in range(block):
+            slot = slot + (source_ref[me, earlier] == source).astype(jnp.int32)
+        slot = jnp.minimum(slot, cap - 1)
+        step = lax.bitwise_xor(source, me)
+        value = moving_ref[:, row : row + BLK_Y, col : col + BLK_X].astype(jnp.float32)
+        for other in range(1, tiles):
+            value = jnp.where(step == other, recvs[other - 1][slot].astype(jnp.float32), value)
+        down = lax.rem(shift_ref[block, 0], BLK_Y)
+        right = lax.rem(shift_ref[block, 1], BLK_X)
+        value = pltpu.roll(value, right, 2)
+        for bit in (1, 2, 4, 8):
+            value = jnp.where(lax.bitwise_and(down, bit) != 0, pltpu.roll(value, bit, 1), value)
+        own_ref[:, row : row + BLK_Y, col : col + BLK_X] = value.astype(own_ref.dtype)
+        if row == 0:
+            for plane in range(depth):
+                rims[1, 0, plane * EDGE : (plane + 1) * EDGE, col : col + BLK_X] = value[plane, :EDGE]
+        if row == height - BLK_Y:
+            for plane in range(depth):
+                rims[1, 1, plane * EDGE : (plane + 1) * EDGE, col : col + BLK_X] = value[plane, -EDGE:]
+    for plane in range(depth):
+        top = fixed_ref[plane, :BLK_Y, :].astype(jnp.float32)
+        bottom = fixed_ref[plane, height - BLK_Y :, :].astype(jnp.float32)
+        rims[0, 0, plane * EDGE : (plane + 1) * EDGE, :] = top[:EDGE]
+        rims[0, 1, plane * EDGE : (plane + 1) * EDGE, :] = bottom[-EDGE:]
+    for image in range(2):
+        straight_ref[image] = rims[image, 1 - half].astype(straight_ref.dtype)
+        slant_ref[image] = rims[image, half].astype(slant_ref.dtype)
+    start = pl.multiple_of((1 - half) * BLK_Y, BLK_Y)
+    send_ref[...] = own_ref[:, pl.ds(start, SEND_ROWS), :]
+
+
+def five(array, axis):
+    size = array.shape[axis]
+    pair = array + pltpu.roll(array, 1, axis)
+    return pltpu.roll(pair, size - 2, axis) + pair + pltpu.roll(array, 2, axis)
+
+
+def main_kernel(
+    place_ref, fixed_own, fixed_got, warp_own, warp_got, straight, slant,
+    fixed_own_n, fixed_got_n, warp_own_n, warp_got_n, straight_n, slant_n,
+    table_y, table_x, out_ref, images, terms, sums,
+):
+    half, side, first, last = place_ref[1], place_ref[2], place_ref[3], place_ref[4]
+    depth, rows, _ = fixed_own.shape
+    planes = 2 * depth
+    window, span = images.shape[2:]
+    width = 2 * BLK_X
+    own_col = pl.multiple_of(side * BLK_X, BLK_X)
+    new_col = pl.multiple_of((1 - side) * width, BLK_X)
+    take = pl.multiple_of(side * BLK_X, BLK_X)
+    start = pl.multiple_of(half * BLK_Y, BLK_Y)
+    lanes = lax.broadcasted_iota(jnp.int32, (window, span), 1)
+    levels = lax.broadcasted_iota(jnp.int32, (window, span), 0)
+    low_lane = jnp.where(side == 0, 0, BLK_X - 48)
+    high_lane = jnp.where(side == 0, width + 32, span)
+    inside = (lanes >= low_lane) & (lanes < high_lane)
+    low_row = jnp.where(first != 0, EDGE, RAD)
+    high_row = jnp.where(last != 0, window - EDGE, window - RAD)
+    inside = inside & (levels >= low_row) & (levels < high_row)
+    near = lax.broadcasted_iota(jnp.int32, (window, BLK_X), 1)
+    near = (near >= low_lane) & (near < jnp.where(side == 0, 32, BLK_X))
+    zero_plane = jnp.zeros((window, span), jnp.float32)
+    for pad in (0, 1, planes + 2, planes + 3):
+        for which in range(2):
+            images[which, pad] = zero_plane
+        for which in range(3):
+            terms[which, pad] = zero_plane
+
+    def place(which, plane, value, value_n):
+        images[which, plane, :, pl.ds(own_col, width)] = value
+        images[which, plane, :, pl.ds(new_col, BLK_X)] = jnp.where(near, value_n, 0.0)
+
+    def shift_in(piece):
+        return pltpu.roll(piece, jnp.where(half == 0, EDGE, SEND_ROWS - BLK_Y + EDGE), 0)[:window]
+
+    for which, (own, got, own_n, got_n) in enumerate(
+        ((fixed_own, fixed_got, fixed_own_n, fixed_got_n), (warp_own, warp_got, warp_own_n, warp_got_n))
+    ):
+        for i in range(depth):
+            mine, theirs = 2 + half * depth + i, 2 + (1 - half) * depth + i
+            place(
+                which, mine,
+                shift_in(own[i, pl.ds(start, SEND_ROWS), :].astype(jnp.float32)),
+                shift_in(own_n[i, pl.ds(start, SEND_ROWS), pl.ds(take, BLK_X)].astype(jnp.float32)),
+            )
+            place(
+                which, theirs,
+                shift_in(got[i].astype(jnp.float32)),
+                shift_in(got_n[i, :, pl.ds(take, BLK_X)].astype(jnp.float32)),
+            )
+        outer = (first + last) != 0
+        for rim, rim_n, base in ((straight, straight_n, half), (slant, slant_n, 1 - half)):
+            value = jnp.where(outer, 0.0, rim[which].astype(jnp.float32))
+            value_n = jnp.where(outer, 0.0, rim_n[which, :, pl.ds(take, BLK_X)].astype(jnp.float32))
+            value_n = jnp.where(near[: value_n.shape[0]], value_n, 0.0)
+            for i in range(depth):
+                plane = 2 + base * depth + i
+                for at_half, row in ((0, 0), (1, window - EDGE)):
+
+                    @pl.when(half == at_half)
+                    def _(plane=plane, row=row, i=i, value=value, value_n=value_n, which=which):
+                        images[which, plane, row : row + EDGE, pl.ds(own_col, width)] = value[i * EDGE : (i + 1) * EDGE]
+                        images[which, plane, row : row + EDGE, pl.ds(new_col, BLK_X)] = value_n[i * EDGE : (i + 1) * EDGE]
+
+    volume = float((2 * RAD + 1) ** 3)
+
+    def box(total):
+        return five(five(total, 0), 1)
+
+    def first_pass(z, carry):
+        f = [images[0, z + k] for k in range(5)]
+        w = [images[1, z + k] for k in range(5)]
+        sum_f = box(f[0] + f[1] + f[2] + f[3] + f[4])
+        sum_w = box(w[0] + w[1] + w[2] + w[3] + w[4])
+        sum_ff = box(sum(a * a for a in f[1:]) + f[0] * f[0])
+        sum_ww = box(sum(a * a for a in w[1:]) + w[0] * w[0])
+        sum_fw = box(sum(a * b for a, b in zip(f[1:], w[1:])) + f[0] * w[0])
+        cross = sum_fw - sum_f * sum_w / volume
+        var_f = sum_ff - sum_f * sum_f / volume
+        var_w = sum_ww - sum_w * sum_w / volume
+        inverse = 1.0 / (var_f * var_w + den_floor)
+        ratio = cross * inverse
+        term_a = 2.0 * ratio
+        term_b = -(ratio * ratio) * var_f
+        term_c = -(term_a * sum_f + 2.0 * term_b * sum_w) / volume
+        terms[0, z + 2] = jnp.where(inside, term_a, 0.0)
+        terms[1, z + 2] = jnp.where(inside, term_b, 0.0)
+        terms[2, z + 2] = jnp.where(inside, term_c, 0.0)
+        return carry
+
+    lax.fori_loop(0, planes, first_pass, 0)
+    for d in range(3):
+        sums[d] = zero_plane
+    owned = (levels >= EDGE) & (levels < window - EDGE)
+
+    def second_pass(z, carry):
+        boxes = []
+        for which in range(3):
+            t = [terms[which, z + k] for k in range(5)]
+            boxes.append(box(t[0] + t[1] + t[2] + t[3] + t[4]))
+        f, w = images[0, z + 2], images[1, z + 2]
+        gain = -(f * boxes[0] + 2.0 * w * boxes[1] + boxes[2])
+        u = z.astype(jnp.float32) * (1.0 / SPACING)
+        weight = (3.0 * u * u * u - 6.0 * u * u + 4.0) * (0.5 / 6.0)
+        gain = jnp.where(owned, gain, 0.0) * weight
+        sums[0] += gain * (images[1, z + 3] - images[1, z + 1])
+        sums[1] += gain * (pltpu.roll(w, window - 1, 0) - pltpu.roll(w, 1, 0))
+        sums[2] += gain * (pltpu.roll(w, span - 1, 1) - pltpu.roll(w, 1, 1))
+        return carry
+
+    lax.fori_loop(0, planes, second_pass, 0)
+    for d in range(3):
+        along_x = lax.dot_general(
+            sums[d], table_x[...], (((1,), (1,)), ((), ())),
+            precision=lax.Precision.HIGHEST, preferred_element_type=jnp.float32,
+        )
+        out_ref[d] = lax.dot_general(
+            table_y[...], along_x, (((1,), (0,)), ((), ())),
+            precision=lax.Precision.HIGHEST, preferred_element_type=jnp.float32,
+        )
+
+
+def fast_body(tiles, fixed_image, moving_image, source_tile, block_shifts):
+    depth, height, width = fixed_image.shape
+    me, half, side = lax.axis_index("tile"), lax.axis_index("gz"), lax.axis_index("rep")
+    sources = source_tile[:, 0, :, 0]
+    shifts = block_shifts[0, 0]
+    first, last = (me == 0) & (half == 0), (me == tiles - 1) & (half == 1)
+    place = jnp.stack([me, half, side, first.astype(jnp.int32), last.astype(jnp.int32)])
+    blocks = sources.shape[1]
+    cap = MAX_NAMED if tiles == 4 else blocks
+    smem = pl.BlockSpec(memory_space=pltpu.SMEM)
+    vmem = pl.BlockSpec(memory_space=pltpu.VMEM)
+    pack_shape = jax.ShapeDtypeStruct((cap, depth, BLK_Y, BLK_X), jnp.bfloat16)
+    send_shape = jax.ShapeDtypeStruct((depth, SEND_ROWS, width), jnp.bfloat16)
+    rim_shape = jax.ShapeDtypeStruct((2, depth * EDGE, width), jnp.bfloat16)
+    *packs, fixed_send = pl.pallas_call(
+        functools.partial(pack_kernel, tiles),
+        out_shape=[pack_shape] * (tiles - 1) + [send_shape],
+        in_specs=[smem, smem, vmem, vmem],
+        out_specs=[vmem] * tiles,
+    )(sources, place, moving_image, fixed_image)
+
+    trio = ("tile", "gz", "rep")
+
+    def number(t, g, r):
+        return (t * 2 + g) * 2 + r
+
+    swap = [(0, 1), (1, 0)]
+    straight, slant = [], []
+    for r in range(2):
+        for t in range(tiles):
+            for g in range(2):
+                to = t + 1 if g == 0 else t - 1
+                straight.append((number(t, g, r), number(to, g, r) if 0 <= to < tiles else number(t, 1 - g, r)))
+                to = t - 1 if g == 0 else t + 1
+                slant.append((number(t, g, r), number(to, 1 - g, r) if 0 <= to < tiles else number(t, g, 1 - r)))
+
+    got = [
+        lax.ppermute(pack, "tile", [(t, t ^ step) for t in range(tiles)])
+        for step, pack in zip(range(1, tiles), packs)
+    ]
+    fixed_got = lax.ppermute(fixed_send, "gz", swap)
+    fixed_own_n = lax.ppermute(fixed_image, "rep", swap)
+    own, send, rim_straight, rim_slant = pl.pallas_call(
+        functools.partial(unpack_kernel, tiles),
+        out_shape=[jax.ShapeDtypeStruct(moving_image.shape, jnp.bfloat16), send_shape, rim_shape, rim_shape],
+        in_specs=[smem, smem, smem] + [vmem] * (tiles + 1),
+        out_specs=[vmem] * 4,
+        scratch_shapes=[pltpu.VMEM((2, 2, depth * EDGE, width), jnp.float32)],
+    )(sources, shifts, place, moving_image, fixed_image, *got)
+
+    warp_got = lax.ppermute(send, "gz", swap)
+    straight_got = lax.ppermute(rim_straight, trio, straight)
+    slant_got = lax.ppermute(rim_slant, trio, slant)
+    fixed_got_n = lax.ppermute(fixed_got, "rep", swap)
+    warp_own_n = lax.ppermute(own, "rep", swap)
+    warp_got_n = lax.ppermute(warp_got, "rep", swap)
+    straight_n = lax.ppermute(straight_got, "rep", swap)
+    slant_n = lax.ppermute(slant_got, "rep", swap)
+
+    window = height // 2 + 2 * EDGE
+    span = width + BLK_X
+    row_knots, col_knots = height // SPACING, width // SPACING
+    row_at = jnp.arange(window, dtype=jnp.int32)
+    table_y = spline_table(half * (height // 2) - EDGE, window, -2, row_knots + 4)
+    table_y = jnp.where(((row_at >= EDGE) & (row_at < window - EDGE))[:, None], table_y, 0.0).T
+    table_x = spline_table(side * BLK_X, span, side * col_knots, col_knots).T
+    planes = 2 * depth + 4
+    part = pl.pallas_call(
+        main_kernel,
+        out_shape=jax.ShapeDtypeStruct((3, row_knots + 4, col_knots), jnp.float32),
+        in_specs=[smem] + [vmem] * 14,
+        out_specs=vmem,
+        scratch_shapes=[
+            pltpu.VMEM((2, planes, window, span), jnp.float32),
+            pltpu.VMEM((3, planes, window, span), jnp.float32),
+            pltpu.VMEM((3, window, span), jnp.float32),
+        ],
+    )(
+        place, fixed_image, fixed_got, own, warp_got, straight_got, slant_got,
+        fixed_own_n, fixed_got_n, warp_own_n, warp_got_n, straight_n, slant_n, table_y, table_x,
+    )
+    back = [(b, a) for a, b in straight]
+    across = lax.ppermute(part, "gz", swap)
+    part_straight = lax.ppermute(part, trio, back)
+    part_slant = lax.ppermute(part, trio, slant)
+    below = jnp.where(half == 0, part_straight, part_slant)
+    above = jnp.where(half == 0, part_slant, part_straight)
+    below = jnp.where(me == tiles - 1, 0.0, below[:, :2])
+    above = jnp.where(me == 0, 0.0, above[:, row_knots + 2 :])
+    middle = part[:, 2 : row_knots + 2] + across[:, 2 : row_knots + 2]
+    return (middle + jnp.concatenate([above, below], axis=1))[:, None]
+
+
 def solution(mesh):
+    sizes = mesh.shape
+    tiles = sizes["tile"]
+    fast = sizes["gz"] == 2 and sizes["rep"] == 2 and tiles & (tiles - 1) == 0 and tiles > 1
     return jax.shard_map(
-        body,
+        functools.partial(fast_body, tiles) if fast else body,
         mesh=mesh,
         in_specs=(
             P(("slab", "gz"), "tile", "rep"),

time: 111 us -> 43.8 us (0.39)
  starting transfers between devices: 42.9 us -> 16.1 us
  blocking collectives: 23.4 us -> 0 us
  Pallas kernels: 0 us -> 14.5 us
  local copies, waits for them, and re-layouts: 13.3 us -> 3.38 us
  other arithmetic: 8.79 us -> 2.1 us
  waiting for transfers between devices: 13.4 us -> 7.34 us
  between operations: 5.84 us -> 0.19 us
  matrix products: 2.18 us -> 0 us
    ppermute x16, starting transfers between devices: 42.9 us -> 16.1 us  [the longest x3 5.18 us: fast_body(): lax.ppermute(pack, 'tile', [(t, t ^ step) for t in range(tiles)])]
    all_gather x1 -> x0, blocking collectives: 17.4 us -> none  [body(): piece = lax.all_gather(moving_image, 'tile', axis=1, tiled=True)]
    pallas_call x0 -> x3, Pallas kernels: none -> 14.5 us  [the longest x1 10.6 us: fast_body(): pl.pallas_call(main_kernel, out_shape=jax.ShapeDtypeStruct((3, row_knots...]
    gather x10 -> x0, local copies, waits for them, and re-layouts: 7.16 us -> none  [the longest x8 4.71 us: body(): taken = jnp.take(columns_part, jnp.clip(wanted, 0, length - 1), axis=1)]
    ppermute x16, waiting for transfers between devices: 13.4 us -> 7.34 us  [the longest x3 2.42 us: fast_body(): lax.ppermute(pack, 'tile', [(t, t ^ step) for t in range(tiles)])]
    psum x1 -> x0, blocking collectives: 6.01 us -> none  [body(): return lax.psum(owned_grad, 'gz')]
    another operation x6 -> x0, other arithmetic: 3.08 us -> none  [the longest x3 1.6 us: body(): jnp.stack((term_a, term_b, term_c)).astype(jnp.bfloat16)]
    dot_general x3 -> x0, matrix products: 2.18 us -> none  [the longest x1 1.05 us: contract(): along_x = jnp.einsum('czyx,xk->czyk', pieces, table_x, precision=highest)]
  transfers between devices with their start and end apart: 16 -> 16, of which waited for: 10 -> 7; matrix products, arithmetic and copies ran while one was open for 0% -> 6% of each run, Pallas kernels for 0% -> 9%
where the time goes in v1:
time: 43.8 us; the launch traced here: 43.6 us
  starting transfers between devices  16.1 us (37%)
  Pallas kernels  14.5 us (33%)
  waiting for transfers between devices  7.34 us (17%)
  local copies, waits for them, and re-layouts  3.38 us (8%)
  other arithmetic  2.1 us (5%)
    pallas_call x1, Pallas kernels, fast_body(): pl.pallas_call(main_kernel, out_shape=jax.ShapeDtypeStruct((3, row_knots...  10.6 us
    ppermute x3, starting transfers between devices, fast_body(): lax.ppermute(pack, 'tile', [(t, t ^ step) for t in range(tiles)])  5.18 us
    ppermute x1, starting transfers between devices, fast_body(): warp_got = lax.ppermute(send, 'gz', swap)  2.99 us
    ppermute x3, waiting for transfers between devices, fast_body(): lax.ppermute(pack, 'tile', [(t, t ^ step) for t in range(tiles)])  2.42 us
    ppermute x1, waiting for transfers between devices, fast_body(): across = lax.ppermute(part, 'gz', swap)  2.23 us
    unnamed x30, local copies, waits for them, and re-layouts  2.04 us
    ppermute x1, starting transfers between devices, fast_body(): part_straight = lax.ppermute(part, trio, back)  2.01 us
    pallas_call x1, Pallas kernels, fast_body(): pl.pallas_call(functools.partial(unpack_kernel, tiles), out_shape=[jax.Sh...  1.95 us
  transfers between devices with their start and end apart: 16, of which 7 were waited for; matrix products, arithmetic and copies ran while one was open for 6% of the time, Pallas kernels for 9%

profile of v1, /device:TPU:0, one launch (start us, length us, event | category | flops | bytes accessed | tf_op | source)
XLA Modules:
  0.0 43.6 jit_solution(3810422774109621645)
XLA Ops:
  0.0 0.5 %collective-permute-start.7 = (bf16[4,64,256]{2,1,0:T(8,128)(2,1)}, bf16[4,64,256]{2,1,0:T(8,128)(2,1)S(1)}, u32[]{:S(2)}, u32[]{:S(2)}) collective-permute-start(bf16[4,64,256]{2,1,0:T(8,128)(2,1)} %fixed_own.1), channel_id=1, source_target_pairs={{0,1},{1,0},{2,3},{3,2},{4,5},{5,4},{6,7},{7,6},{8,9},{9,8},{10,11... | collective-permute-start | bytes 393224 | tf_op jit(solution)/shard_map/ppermute | solution.py:427
  0.5 0.7 %stack.31.place_ref = s32[5]{0:T(128)} concatenate(s32[1]{0:T(128)} %bitcast, s32[1]{0:T(128)} %bitcast.1, s32[1]{0:T(128)} %bitcast.2, s32[1]{0:T(128)} %bitcast.3, s32[1]{0:T(128)} %bitcast.4), dimensions={0} | concatenate | bytes 40 | tf_op jit(solution)/shard_map/stack | solution.py:392
  1.1 1.9 %shard_map.46 = (bf16[4,4,16,128]{3,2,1,0:T(8,128)(2,1)}, bf16[4,4,16,128]{3,2,1,0:T(8,128)(2,1)}, bf16[4,4,16,128]{3,2,1,0:T(8,128)(2,1)}, bf16[4,48,256]{2,1,0:T(8,128)(2,1)}) custom-call(s32[4,8]{1,0:T(4,128)} %bitcast.11, s32[5]{0:T(128)} %stack.31.place_ref, bf16[4,64,256]{2,1,0:T(8,128)(2,1)} %moving_ref.3, bf16[4,64,256]{2,1,0:T(8,128)(2,1)} %fixed_own.1), custom_call_target="tpu_custom_call" | custom-call | tf_op jit(solution)/shard_map/pallas_call | solution.py:400
  3.1 2.6 %collective-permute-start.1 = (bf16[4,4,16,128]{3,2,1,0:T(8,128)(2,1)}, bf16[4,4,16,128]{3,2,1,0:T(8,128)(2,1)S(1)}, u32[]{:S(2)}, u32[]{:S(2)}) collective-permute-start(bf16[4,4,16,128]{3,2,1,0:T(8,128)(2,1)} %get-tuple-element.14), channel_id=1, source_target_pairs={{0,4},{4,0},{8,12},{12,8},{1,5},{5,1},{9,13},{13,9},{2,6},{6,2},{1... | collective-permute-start | bytes 196616 | tf_op jit(solution)/shard_map/ppermute | solution.py:423
  5.6 2.6 %collective-permute-start.2 = (bf16[4,4,16,128]{3,2,1,0:T(8,128)(2,1)}, bf16[4,4,16,128]{3,2,1,0:T(8,128)(2,1)S(1)}, u32[]{:S(2)}, u32[]{:S(2)}) collective-permute-start(bf16[4,4,16,128]{3,2,1,0:T(8,128)(2,1)} %get-tuple-element.15), channel_id=1, source_target_pairs={{0,8},{4,12},{8,0},{12,4},{1,9},{5,13},{9,1},{13,5},{2,10},{6,14},... | collective-permute-start | bytes 196616 | tf_op jit(solution)/shard_map/ppermute | solution.py:423
  8.2 0.0 collective-permute-start.3
  8.2 1.7 %collective-permute-start = (bf16[4,48,256]{2,1,0:T(8,128)(2,1)}, bf16[4,48,256]{2,1,0:T(8,128)(2,1)S(1)}, u32[]{:S(2)}, u32[]{:S(2)}) collective-permute-start(bf16[4,48,256]{2,1,0:T(8,128)(2,1)} %get-tuple-element.13), channel_id=1, source_target_pairs={{0,2},{2,0},{1,3},{3,1},{4,6},{6,4},{5,7},{7,5},{8,10},{10,8},{9,1... | collective-permute-start | bytes 294920 | tf_op jit(solution)/shard_map/ppermute | solution.py:426
  10.1 0.0 copy-start.14
  10.1 0.7 %copy-done.14 = s32[1,1,8,2]{2,3,1,0:T(2,128)S(1)} copy-done((s32[1,1,8,2]{2,3,1,0:T(2,128)S(1)}, s32[1,1,8,2]{2,3,1,0:T(2,128)}, u32[]{:S(2)}) %copy-start.14) | copy-done | bytes 88
  10.8 0.7 %copy.5.shift_ref = s32[8,2]{1,0:T(8,128)} copy(s32[8,2]{0,1:T(2,128)S(1)} %bitcast.13) | data formatting | bytes 128 | tf_op jit(solution)/shard_map/squeeze | solution.py:390
  11.4 0.7 %select_add_fusion.table_x = f32[16,384]{1,0:T(8,128)} fusion(f32[384]{0:T(512)S(1)} %get-tuple-element.36, s32[384]{0:T(512)S(1)} %get-tuple-element.32, f32[384]{0:T(512)S(1)} %get-tuple-element.34, s32[384]{0:T(512)S(1)} %get-tuple-element.38, f32[384]{0:T(512)S(1)} %get-tuple-element.33, s32[384]{0:T(512)S(1)} %get-tuple-element.31, ...), kind=kLoop, calls=%fused_computation | loop fusion | flops 67584 | bytes 36928 | tf_op jit(solution)/shard_map/add | solution.py:96
  12.1 0.0 collective-permute-done.1.refs_0_
  12.1 0.0 copy-start.6
  12.2 0.6 %collective-permute-done.2.refs_1_ = bf16[4,4,16,128]{3,2,1,0:T(8,128)(2,1)S(1)} collective-permute-done((bf16[4,4,16,128]{3,2,1,0:T(8,128)(2,1)}, bf16[4,4,16,128]{3,2,1,0:T(8,128)(2,1)S(1)}, u32[]{:S(2)}, u32[]{:S(2)}) %collective-permute-start.2) | collective-permute-done | bytes 65568 | tf_op jit(solution)/shard_map/ppermute | solution.py:423
  12.8 0.0 copy-start.7
  12.8 1.8 %collective-permute-done.3.refs_2_ = bf16[4,4,16,128]{3,2,1,0:T(8,128)(2,1)S(1)} collective-permute-done((bf16[4,4,16,128]{3,2,1,0:T(8,128)(2,1)}, bf16[4,4,16,128]{3,2,1,0:T(8,128)(2,1)S(1)}, u32[]{:S(2)}, u32[]{:S(2)}) %collective-permute-start.3) | collective-permute-done | bytes 65568 | tf_op jit(solution)/shard_map/ppermute | solution.py:423
  14.6 0.0 copy-done.6
  14.6 0.0 copy-done.7
  14.6 0.0 copy-start.8
  14.6 0.6 %copy-done.8 = bf16[4,4,16,128]{3,2,1,0:T(8,128)(2,1)} copy-done((bf16[4,4,16,128]{3,2,1,0:T(8,128)(2,1)}, bf16[4,4,16,128]{3,2,1,0:T(8,128)(2,1)S(1)}, u32[]{:S(2)}) %copy-start.8) | copy-done | bytes 65560
  15.2 1.9 %shard_map.47 = (bf16[4,64,256]{2,1,0:T(8,128)(2,1)}, bf16[4,48,256]{2,1,0:T(8,128)(2,1)}, bf16[2,16,256]{2,1,0:T(8,128)(2,1)}, bf16[2,16,256]{2,1,0:T(8,128)(2,1)}) custom-call(s32[4,8]{1,0:T(4,128)} %bitcast.12, s32[8,2]{1,0:T(8,128)} %copy.5.shift_ref, s32[5]{0:T(128)} %stack.31.place_ref, bf16[4,64,256]{2,1,0:T(8,128)(2,1)} %moving_ref.3, ...), custom_call_target="tpu_custom_call" | custom-call | tf_op jit(solution)/shard_map/pallas_call | solution.py:428
  17.1 1.2 %collective-permute-start.5 = (bf16[2,16,256]{2,1,0:T(8,128)(2,1)}, bf16[2,16,256]{2,1,0:T(8,128)(2,1)S(1)}, u32[]{:S(2)}, u32[]{:S(2)}) collective-permute-start(bf16[2,16,256]{2,1,0:T(8,128)(2,1)} %get-tuple-element.19), channel_id=1, source_target_pairs={{0,4},{2,0},{4,8},{6,2},{8,12},{10,6},{12,14},{14,10},{1,5},{3,1},... | collective-permute-start | bytes 49160 | tf_op jit(solution)/shard_map/ppermute | solution.py:437
  18.4 0.0 collective-permute-start.6
  18.4 3.0 %collective-permute-start.4 = (bf16[4,48,256]{2,1,0:T(8,128)(2,1)}, bf16[4,48,256]{2,1,0:T(8,128)(2,1)S(1)}, u32[]{:S(2)}, u32[]{:S(2)}) collective-permute-start(bf16[4,48,256]{2,1,0:T(8,128)(2,1)} %get-tuple-element.18), channel_id=1, source_target_pairs={{0,2},{2,0},{1,3},{3,1},{4,6},{6,4},{5,7},{7,5},{8,10},{10,8},{9,1... | collective-permute-start | bytes 294920 | tf_op jit(solution)/shard_map/ppermute | solution.py:436
  21.4 0.0 collective-permute-done.5.straight
  21.4 0.0 copy-start.10
  21.4 0.0 collective-permute-start.11
  21.4 0.0 collective-permute-done.6.slant
  21.4 0.0 copy-start.11
  21.4 0.6 %collective-permute-start.9 = (bf16[4,64,256]{2,1,0:T(8,128)(2,1)}, bf16[4,64,256]{2,1,0:T(8,128)(2,1)S(1)}, u32[]{:S(2)}, u32[]{:S(2)}) collective-permute-start(bf16[4,64,256]{2,1,0:T(8,128)(2,1)} %get-tuple-element.17.warp_own), channel_id=1, source_target_pairs={{0,1},{1,0},{2,3},{3,2},{4,5},{5,4},{6,7},{7,6},{8,9},{9,8},{10,11... | collective-permute-start | bytes 393224 | tf_op jit(solution)/shard_map/ppermute | solution.py:440
  22.0 0.6 %collective-permute-done.11.straight_n = bf16[2,16,256]{2,1,0:T(8,128)(2,1)S(1)} collective-permute-done((bf16[2,16,256]{2,1,0:T(8,128)(2,1)S(1)}, bf16[2,16,256]{2,1,0:T(8,128)(2,1)S(1)}, u32[]{:S(2)}, u32[]{:S(2)}) %collective-permute-start.11) | collective-permute-done | bytes 16416 | tf_op jit(solution)/shard_map/ppermute | solution.py:442
  22.6 0.2 collective-permute-start.12
  22.7 0.0 collective-permute-done.fixed_got
  22.7 0.3 collective-permute-start.8
  23.1 1.1 %collective-permute-done.4.warp_got = bf16[4,48,256]{2,1,0:T(8,128)(2,1)S(1)} collective-permute-done((bf16[4,48,256]{2,1,0:T(8,128)(2,1)}, bf16[4,48,256]{2,1,0:T(8,128)(2,1)S(1)}, u32[]{:S(2)}, u32[]{:S(2)}) %collective-permute-start.4) | collective-permute-done | bytes 98336 | tf_op jit(solution)/shard_map/ppermute | solution.py:436
  24.2 0.0 collective-permute-start.10
  24.2 0.7 %add_select_fusion.table_y = f32[8,40]{1,0:T(8,128)} fusion(f32[40]{0:T(128)S(1)} %get-tuple-element.28, s32[40]{0:T(128)S(1)} %get-tuple-element.24, f32[40]{0:T(128)S(1)} %get-tuple-element.26, s32[40]{0:T(128)S(1)} %get-tuple-element.30, f32[40]{0:T(128)S(1)} %get-tuple-element.27, s32[40]{0:T(128)S(1)} %get-tuple-element.23, f32[40]{0:T(128)S(1)} %get-tuple-element.25, ...), kind=kLoop, calls=%fused_computation.4 | loop fusion | flops 3840 | bytes 2632 | tf_op jit(solution)/shard_map/jit(_where)/select_n | solution.py:450
  24.8 0.0 collective-permute-done.12.slant_n
  24.9 0.0 collective-permute-done.7.fixed_own_n
  24.9 0.0 copy-start
  24.9 0.0 collective-permute-done.9.warp_own_n
  24.9 0.0 copy-start.1
  24.9 0.0 collective-permute-done.8.fixed_got_n
  24.9 0.0 copy-start.4
  24.9 0.6 %collective-permute-done.10.warp_got_n = bf16[4,48,256]{2,1,0:T(8,128)(2,1)S(1)} collective-permute-done((bf16[4,48,256]{2,1,0:T(8,128)(2,1)S(1)}, bf16[4,48,256]{2,1,0:T(8,128)(2,1)S(1)}, u32[]{:S(2)}, u32[]{:S(2)}) %collective-permute-start.10) | collective-permute-done | bytes 98336 | tf_op jit(solution)/shard_map/ppermute | solution.py:441
  25.5 0.0 copy-done.10
  25.5 0.0 copy-done.11
  25.5 0.0 copy-done.12
  25.5 0.0 copy-done.2
  25.5 0.0 copy-done.3
  25.5 0.0 copy-done.13
  25.5 0.0 copy-done
  25.5 0.0 copy-done.1
  25.6 0.0 copy-done.4
  25.6 0.6 %copy-done.5 = bf16[4,48,256]{2,1,0:T(8,128)(2,1)} copy-done((bf16[4,48,256]{2,1,0:T(8,128)(2,1)}, bf16[4,48,256]{2,1,0:T(8,128)(2,1)S(1)}, u32[]{:S(2)}) %copy-start.5) | copy-done | bytes 98328
  26.2 10.6 %shard_map.48 = f32[3,8,16]{2,1,0:T(8,128)} custom-call(s32[5]{0:T(128)} %stack.31.place_ref, bf16[4,64,256]{2,1,0:T(8,128)(2,1)} %fixed_own.1, bf16[4,48,256]{2,1,0:T(8,128)(2,1)} %copy-done.2, bf16[4,64,256]{2,1,0:T(8,128)(2,1)} %get-tuple-element.17.warp_own, bf16[4,48,256]{2,1,0:T(8,128)(2,1)} %copy-done.3, bf16[2,16,256]{2,1,0:T(8,128)(2,1)} %copy-done.10, ...), custom_call_target="tpu_custom_call" | custom-call | tf_op jit(solution)/shard_map/pallas_call | solution.py:453
  36.9 2.0 %collective-permute-start.15 = (f32[3,8,16]{2,1,0:T(8,128)}, f32[3,8,16]{2,1,0:T(8,128)S(1)}, u32[]{:S(2)}, u32[]{:S(2)}) collective-permute-start(f32[3,8,16]{2,1,0:T(8,128)} %shard_map.48), channel_id=1, source_target_pairs={{4,0},{0,2},{8,4},{2,6},{12,8},{6,10},{14,12},{10,14},{5,1},{1,3},... | collective-permute-start | bytes 4616 | tf_op jit(solution)/shard_map/ppermute | solution.py:469
  38.9 0.2 collective-permute-start.14
  39.1 1.2 %collective-permute-start.13 = (f32[3,8,16]{2,1,0:T(8,128)}, f32[3,8,16]{2,1,0:T(8,128)S(1)}, u32[]{:S(2)}, u32[]{:S(2)}) collective-permute-start(f32[3,8,16]{2,1,0:T(8,128)} %shard_map.48), channel_id=1, source_target_pairs={{0,2},{2,0},{1,3},{3,1},{4,6},{6,4},{5,7},{7,5},{8,10},{10,8},{9,1... | collective-permute-start | bytes 4616 | tf_op jit(solution)/shard_map/ppermute | solution.py:468
  40.3 0.4 collective-permute-done.15
  40.8 0.0 collective-permute-done.14
  40.8 2.2 %collective-permute-done.13 = f32[3,8,16]{2,1,0:T(8,128)S(1)} collective-permute-done((f32[3,8,16]{2,1,0:T(8,128)}, f32[3,8,16]{2,1,0:T(8,128)S(1)}, u32[]{:S(2)}, u32[]{:S(2)}) %collective-permute-start.13) | collective-permute-done | bytes 1568 | tf_op jit(solution)/shard_map/ppermute | solution.py:468
  43.0 0.0 copy-done.9
  43.0 0.6 %fusion.1 = f32[3,1,4,16]{3,2,1,0:T(4,128)} fusion(f32[3,8,16]{2,1,0:T(8,128)S(1)} %collective-permute-done.13, f32[3,8,16]{2,1,0:T(8,128)S(1)} %copy-done.9, f32[3,2,16]{2,1,0:T(2,128)S(1)} %get-tuple-element.22, f32[3,2,16]{2,1,0:T(2,128)S(1)} %get-tuple-element.21), kind=kLoop, calls=%fused_computation.3 | loop fusion | flops 576 | bytes 3072 | tf_op jit(solution)/shard_map/broadcast_in_dim | solution.py:476
  (18 shorter events, 0.2 us)
Async XLA Ops:
  0.0 24.9 %collective-permute-start.7 = (bf16[4,64,256]{2,1,0:T(8,128)(2,1)}, bf16[4,64,256]{2,1,0:T(8,128)(2,1)S(1)}, u32[]{:S(2)}, u32[]{:S(2)}) collective-permute-start(bf16[4,64,256]{2,1,0:T(8,128)(2,1)} %fixed_own.1), channel_id=1, source_target_pairs={{0,1},{1,0},{2,3},{3,2},{4,5},{5,4},{6,7},{7,6},{8,9},{9,8},{10,11... | collective-permute-start | bytes 393224 | tf_op jit(solution)/shard_map/ppermute | solution.py:427
  3.1 9.1 %collective-permute-start.1 = (bf16[4,4,16,128]{3,2,1,0:T(8,128)(2,1)}, bf16[4,4,16,128]{3,2,1,0:T(8,128)(2,1)S(1)}, u32[]{:S(2)}, u32[]{:S(2)}) collective-permute-start(bf16[4,4,16,128]{3,2,1,0:T(8,128)(2,1)} %get-tuple-element.14), channel_id=1, source_target_pairs={{0,4},{4,0},{8,12},{12,8},{1,5},{5,1},{9,13},{13,9},{2,6},{6,2},{1... | collective-permute-start | bytes 196616 | tf_op jit(solution)/shard_map/ppermute | solution.py:423
  5.6 7.2 %collective-permute-start.2 = (bf16[4,4,16,128]{3,2,1,0:T(8,128)(2,1)}, bf16[4,4,16,128]{3,2,1,0:T(8,128)(2,1)S(1)}, u32[]{:S(2)}, u32[]{:S(2)}) collective-permute-start(bf16[4,4,16,128]{3,2,1,0:T(8,128)(2,1)} %get-tuple-element.15), channel_id=1, source_target_pairs={{0,8},{4,12},{8,0},{12,4},{1,9},{5,13},{9,1},{13,5},{2,10},{6,14},... | collective-permute-start | bytes 196616 | tf_op jit(solution)/shard_map/ppermute | solution.py:423
  8.2 6.3 %collective-permute-start.3 = (bf16[4,4,16,128]{3,2,1,0:T(8,128)(2,1)}, bf16[4,4,16,128]{3,2,1,0:T(8,128)(2,1)S(1)}, u32[]{:S(2)}, u32[]{:S(2)}) collective-permute-start(bf16[4,4,16,128]{3,2,1,0:T(8,128)(2,1)} %get-tuple-element.16), channel_id=1, source_target_pairs={{0,12},{4,8},{8,4},{12,0},{1,13},{5,9},{9,5},{13,1},{2,14},{6,10},... | collective-permute-start | bytes 196616 | tf_op jit(solution)/shard_map/ppermute | solution.py:423
  8.2 14.5 %collective-permute-start = (bf16[4,48,256]{2,1,0:T(8,128)(2,1)}, bf16[4,48,256]{2,1,0:T(8,128)(2,1)S(1)}, u32[]{:S(2)}, u32[]{:S(2)}) collective-permute-start(bf16[4,48,256]{2,1,0:T(8,128)(2,1)} %get-tuple-element.13), channel_id=1, source_target_pairs={{0,2},{2,0},{1,3},{3,1},{4,6},{6,4},{5,7},{7,5},{8,10},{10,8},{9,1... | collective-permute-start | bytes 294920 | tf_op jit(solution)/shard_map/ppermute | solution.py:426
  10.1 0.7 %copy-start.14 = (s32[1,1,8,2]{2,3,1,0:T(2,128)S(1)}, s32[1,1,8,2]{2,3,1,0:T(2,128)}, u32[]{:S(2)}) copy-start(s32[1,1,8,2]{2,3,1,0:T(2,128)} %param.7) | copy-start | bytes 196
  12.1 2.4 %copy-start.6 = (bf16[4,4,16,128]{3,2,1,0:T(8,128)(2,1)}, bf16[4,4,16,128]{3,2,1,0:T(8,128)(2,1)S(1)}, u32[]{:S(2)}) copy-start(bf16[4,4,16,128]{3,2,1,0:T(8,128)(2,1)S(1)} %collective-permute-done.1.refs_0_) | copy-start | bytes 196612
  12.8 1.8 %copy-start.7 = (bf16[4,4,16,128]{3,2,1,0:T(8,128)(2,1)}, bf16[4,4,16,128]{3,2,1,0:T(8,128)(2,1)S(1)}, u32[]{:S(2)}) copy-start(bf16[4,4,16,128]{3,2,1,0:T(8,128)(2,1)S(1)} %collective-permute-done.2.refs_1_) | copy-start | bytes 196612
  14.6 0.6 %copy-start.8 = (bf16[4,4,16,128]{3,2,1,0:T(8,128)(2,1)}, bf16[4,4,16,128]{3,2,1,0:T(8,128)(2,1)S(1)}, u32[]{:S(2)}) copy-start(bf16[4,4,16,128]{3,2,1,0:T(8,128)(2,1)S(1)} %collective-permute-done.3.refs_2_) | copy-start | bytes 196612
  17.1 4.2 %collective-permute-start.5 = (bf16[2,16,256]{2,1,0:T(8,128)(2,1)}, bf16[2,16,256]{2,1,0:T(8,128)(2,1)S(1)}, u32[]{:S(2)}, u32[]{:S(2)}) collective-permute-start(bf16[2,16,256]{2,1,0:T(8,128)(2,1)} %get-tuple-element.19), channel_id=1, source_target_pairs={{0,4},{2,0},{4,8},{6,2},{8,12},{10,6},{12,14},{14,10},{1,5},{3,1},... | collective-permute-start | bytes 49160 | tf_op jit(solution)/shard_map/ppermute | solution.py:437
  18.4 3.0 %collective-permute-start.6 = (bf16[2,16,256]{2,1,0:T(8,128)(2,1)}, bf16[2,16,256]{2,1,0:T(8,128)(2,1)S(1)}, u32[]{:S(2)}, u32[]{:S(2)}) collective-permute-start(bf16[2,16,256]{2,1,0:T(8,128)(2,1)} %get-tuple-element.20), channel_id=1, source_target_pairs={{0,1},{2,4},{4,2},{6,8},{8,6},{10,12},{12,10},{14,15},{1,0},{3,5},... | collective-permute-start | bytes 49160 | tf_op jit(solution)/shard_map/ppermute | solution.py:438
  18.4 5.8 %collective-permute-start.4 = (bf16[4,48,256]{2,1,0:T(8,128)(2,1)}, bf16[4,48,256]{2,1,0:T(8,128)(2,1)S(1)}, u32[]{:S(2)}, u32[]{:S(2)}) collective-permute-start(bf16[4,48,256]{2,1,0:T(8,128)(2,1)} %get-tuple-element.18), channel_id=1, source_target_pairs={{0,2},{2,0},{1,3},{3,1},{4,6},{6,4},{5,7},{7,5},{8,10},{10,8},{9,1... | collective-permute-start | bytes 294920 | tf_op jit(solution)/shard_map/ppermute | solution.py:436
  21.4 4.1 %copy-start.10 = (bf16[2,16,256]{2,1,0:T(8,128)(2,1)}, bf16[2,16,256]{2,1,0:T(8,128)(2,1)S(1)}, u32[]{:S(2)}) copy-start(bf16[2,16,256]{2,1,0:T(8,128)(2,1)S(1)} %collective-permute-done.5.straight) | copy-start | bytes 49156
  21.4 1.2 %collective-permute-start.11 = (bf16[2,16,256]{2,1,0:T(8,128)(2,1)S(1)}, bf16[2,16,256]{2,1,0:T(8,128)(2,1)S(1)}, u32[]{:S(2)}, u32[]{:S(2)}) collective-permute-start(bf16[2,16,256]{2,1,0:T(8,128)(2,1)S(1)} %collective-permute-done.5.straight), channel_id=1, source_target_pairs={{0,1},{1,0},{2,3},{3,2},{4,5},{5,4},{6,7},{7,6},{8,9},{9,8},{10,11... | collective-permute-start | bytes 49160 | tf_op jit(solution)/shard_map/ppermute | solution.py:442
  21.4 4.1 %copy-start.11 = (bf16[2,16,256]{2,1,0:T(8,128)(2,1)}, bf16[2,16,256]{2,1,0:T(8,128)(2,1)S(1)}, u32[]{:S(2)}) copy-start(bf16[2,16,256]{2,1,0:T(8,128)(2,1)S(1)} %collective-permute-done.6.slant) | copy-start | bytes 49156
  21.4 3.5 %collective-permute-start.9 = (bf16[4,64,256]{2,1,0:T(8,128)(2,1)}, bf16[4,64,256]{2,1,0:T(8,128)(2,1)S(1)}, u32[]{:S(2)}, u32[]{:S(2)}) collective-permute-start(bf16[4,64,256]{2,1,0:T(8,128)(2,1)} %get-tuple-element.17.warp_own), channel_id=1, source_target_pairs={{0,1},{1,0},{2,3},{3,2},{4,5},{5,4},{6,7},{7,6},{8,9},{9,8},{10,11... | collective-permute-start | bytes 393224 | tf_op jit(solution)/shard_map/ppermute | solution.py:440
  22.6 2.9 %copy-start.12 = (bf16[2,16,256]{2,1,0:T(8,128)(2,1)}, bf16[2,16,256]{2,1,0:T(8,128)(2,1)S(1)}, u32[]{:S(2)}) copy-start(bf16[2,16,256]{2,1,0:T(8,128)(2,1)S(1)} %collective-permute-done.11.straight_n) | copy-start | bytes 49156
  22.6 2.3 %collective-permute-start.12 = (bf16[2,16,256]{2,1,0:T(8,128)(2,1)S(1)}, bf16[2,16,256]{2,1,0:T(8,128)(2,1)S(1)}, u32[]{:S(2)}, u32[]{:S(2)}) collective-permute-start(bf16[2,16,256]{2,1,0:T(8,128)(2,1)S(1)} %collective-permute-done.6.slant), channel_id=1, source_target_pairs={{0,1},{1,0},{2,3},{3,2},{4,5},{5,4},{6,7},{7,6},{8,9},{9,8},{10,11... | collective-permute-start | bytes 49160 | tf_op jit(solution)/shard_map/ppermute | solution.py:443
  22.7 2.8 %copy-start.2 = (bf16[4,48,256]{2,1,0:T(8,128)(2,1)}, bf16[4,48,256]{2,1,0:T(8,128)(2,1)S(1)}, u32[]{:S(2)}) copy-start(bf16[4,48,256]{2,1,0:T(8,128)(2,1)S(1)} %collective-permute-done.fixed_got) | copy-start | bytes 294916
  22.7 2.2 %collective-permute-start.8 = (bf16[4,48,256]{2,1,0:T(8,128)(2,1)S(1)}, bf16[4,48,256]{2,1,0:T(8,128)(2,1)S(1)}, u32[]{:S(2)}, u32[]{:S(2)}) collective-permute-start(bf16[4,48,256]{2,1,0:T(8,128)(2,1)S(1)} %collective-permute-done.fixed_got), channel_id=1, source_target_pairs={{0,1},{1,0},{2,3},{3,2},{4,5},{5,4},{6,7},{7,6},{8,9},{9,8},{10,11... | collective-permute-start | bytes 294920 | tf_op jit(solution)/shard_map/ppermute | solution.py:439
  24.2 1.3 %copy-start.3 = (bf16[4,48,256]{2,1,0:T(8,128)(2,1)}, bf16[4,48,256]{2,1,0:T(8,128)(2,1)S(1)}, u32[]{:S(2)}) copy-start(bf16[4,48,256]{2,1,0:T(8,128)(2,1)S(1)} %collective-permute-done.4.warp_got) | copy-start | bytes 294916
  24.2 1.3 %collective-permute-start.10 = (bf16[4,48,256]{2,1,0:T(8,128)(2,1)S(1)}, bf16[4,48,256]{2,1,0:T(8,128)(2,1)S(1)}, u32[]{:S(2)}, u32[]{:S(2)}) collective-permute-start(bf16[4,48,256]{2,1,0:T(8,128)(2,1)S(1)} %collective-permute-done.4.warp_got), channel_id=1, source_target_pairs={{0,1},{1,0},{2,3},{3,2},{4,5},{5,4},{6,7},{7,6},{8,9},{9,8},{10,11... | collective-permute-start | bytes 294920 | tf_op jit(solution)/shard_map/ppermute | solution.py:441
  24.8 0.7 %copy-start.13 = (bf16[2,16,256]{2,1,0:T(8,128)(2,1)}, bf16[2,16,256]{2,1,0:T(8,128)(2,1)S(1)}, u32[]{:S(2)}) copy-start(bf16[2,16,256]{2,1,0:T(8,128)(2,1)S(1)} %collective-permute-done.12.slant_n) | copy-start | bytes 49156
  24.9 0.7 %copy-start = (bf16[4,64,256]{2,1,0:T(8,128)(2,1)}, bf16[4,64,256]{2,1,0:T(8,128)(2,1)S(1)}, u32[]{:S(2)}) copy-start(bf16[4,64,256]{2,1,0:T(8,128)(2,1)S(1)} %collective-permute-done.7.fixed_own_n) | copy-start | bytes 393220
  24.9 0.7 %copy-start.1 = (bf16[4,64,256]{2,1,0:T(8,128)(2,1)}, bf16[4,64,256]{2,1,0:T(8,128)(2,1)S(1)}, u32[]{:S(2)}) copy-start(bf16[4,64,256]{2,1,0:T(8,128)(2,1)S(1)} %collective-permute-done.9.warp_own_n) | copy-start | bytes 393220
  24.9 0.7 %copy-start.4 = (bf16[4,48,256]{2,1,0:T(8,128)(2,1)}, bf16[4,48,256]{2,1,0:T(8,128)(2,1)S(1)}, u32[]{:S(2)}) copy-start(bf16[4,48,256]{2,1,0:T(8,128)(2,1)S(1)} %collective-permute-done.8.fixed_got_n) | copy-start | bytes 294916
  25.6 0.6 %copy-start.5 = (bf16[4,48,256]{2,1,0:T(8,128)(2,1)}, bf16[4,48,256]{2,1,0:T(8,128)(2,1)S(1)}, u32[]{:S(2)}) copy-start(bf16[4,48,256]{2,1,0:T(8,128)(2,1)S(1)} %collective-permute-done.10.warp_got_n) | copy-start | bytes 294916
  36.9 6.2 %copy-start.9 = (f32[3,8,16]{2,1,0:T(8,128)S(1)}, f32[3,8,16]{2,1,0:T(8,128)}, u32[]{:S(2)}) copy-start(f32[3,8,16]{2,1,0:T(8,128)} %shard_map.48) | copy-start | bytes 4612
  36.9 3.9 %collective-permute-start.15 = (f32[3,8,16]{2,1,0:T(8,128)}, f32[3,8,16]{2,1,0:T(8,128)S(1)}, u32[]{:S(2)}, u32[]{:S(2)}) collective-permute-start(f32[3,8,16]{2,1,0:T(8,128)} %shard_map.48), channel_id=1, source_target_pairs={{4,0},{0,2},{8,4},{2,6},{12,8},{6,10},{14,12},{10,14},{5,1},{1,3},... | collective-permute-start | bytes 4616 | tf_op jit(solution)/shard_map/ppermute | solution.py:469
  38.9 1.9 %collective-permute-start.14 = (f32[3,8,16]{2,1,0:T(8,128)}, f32[3,8,16]{2,1,0:T(8,128)S(1)}, u32[]{:S(2)}, u32[]{:S(2)}) collective-permute-start(f32[3,8,16]{2,1,0:T(8,128)} %shard_map.48), channel_id=1, source_target_pairs={{0,1},{2,4},{4,2},{6,8},{8,6},{10,12},{12,10},{14,15},{1,0},{3,5},... | collective-permute-start | bytes 4616 | tf_op jit(solution)/shard_map/ppermute | solution.py:470
  39.1 3.9 %collective-permute-start.13 = (f32[3,8,16]{2,1,0:T(8,128)}, f32[3,8,16]{2,1,0:T(8,128)S(1)}, u32[]{:S(2)}, u32[]{:S(2)}) collective-permute-start(f32[3,8,16]{2,1,0:T(8,128)} %shard_map.48), channel_id=1, source_target_pairs={{0,2},{2,0},{1,3},{3,1},{4,6},{6,4},{5,7},{7,5},{8,10},{10,8},{9,1... | collective-permute-start | bytes 4616 | tf_op jit(solution)/shard_map/ppermute | solution.py:468

commit v2 on v1

--- a/solution.py
+++ b/solution.py
@@ -184,8 +184,8 @@
 SEND_ROWS = 48
 
 
-def pack_kernel(tiles, source_ref, place_ref, moving_ref, fixed_ref, *out_refs):
-    me, half = place_ref[0], place_ref[1]
+def pack_kernel(tiles, source_ref, moving_ref, fixed_ref, *out_refs):
+    me, half = lax.axis_index("tile"), lax.axis_index("gz")
     packs, fixed_out = out_refs[:-1], out_refs[-1]
     height, width = moving_ref.shape[1:]
     xblocks = width // BLK_X
@@ -209,10 +209,10 @@
     fixed_out[...] = fixed_ref[:, pl.ds(start, SEND_ROWS), :]
 
 
-def unpack_kernel(tiles, source_ref, shift_ref, place_ref, moving_ref, fixed_ref, *refs):
+def unpack_kernel(tiles, source_ref, shift_ref, moving_ref, fixed_ref, *refs):
     recvs = refs[: tiles - 1]
     own_ref, send_ref, straight_ref, slant_ref, rims = refs[tiles - 1 :]
-    me, half = place_ref[0], place_ref[1]
+    me, half = lax.axis_index("tile"), lax.axis_index("gz")
     depth, height, width = moving_ref.shape
     xblocks = width // BLK_X
     blocks = (height // BLK_Y) * xblocks
@@ -259,12 +259,15 @@
 
 
 def main_kernel(
-    place_ref, fixed_own, fixed_got, warp_own, warp_got, straight, slant,
+    tiles, fixed_own, fixed_got, warp_own, warp_got, straight, slant,
     fixed_own_n, fixed_got_n, warp_own_n, warp_got_n, straight_n, slant_n,
-    table_y, table_x, out_ref, images, terms, sums,
+    table_y, table_x, out_ref, images, rows_sum, terms, sums, band,
 ):
-    half, side, first, last = place_ref[1], place_ref[2], place_ref[3], place_ref[4]
-    depth, rows, _ = fixed_own.shape
+    half, side = lax.axis_index("gz"), lax.axis_index("rep")
+    me = lax.axis_index("tile")
+    first = jnp.where(half == 0, (me == 0).astype(jnp.int32), 0)
+    last = jnp.where(half == 1, (me == tiles - 1).astype(jnp.int32), 0)
+    depth = fixed_own.shape[0]
     planes = 2 * depth
     window, span = images.shape[2:]
     width = 2 * BLK_X
@@ -276,18 +279,21 @@
     levels = lax.broadcasted_iota(jnp.int32, (window, span), 0)
     low_lane = jnp.where(side == 0, 0, BLK_X - 48)
     high_lane = jnp.where(side == 0, width + 32, span)
-    inside = (lanes >= low_lane) & (lanes < high_lane)
     low_row = jnp.where(first != 0, EDGE, RAD)
     high_row = jnp.where(last != 0, window - EDGE, window - RAD)
-    inside = inside & (levels >= low_row) & (levels < high_row)
+    inside = (lanes >= low_lane) & (lanes < high_lane) & (levels >= low_row) & (levels < high_row)
     near = lax.broadcasted_iota(jnp.int32, (window, BLK_X), 1)
     near = (near >= low_lane) & (near < jnp.where(side == 0, 32, BLK_X))
     zero_plane = jnp.zeros((window, span), jnp.float32)
+    across = lax.broadcasted_iota(jnp.int32, (span, span), 0) - lax.broadcasted_iota(jnp.int32, (span, span), 1)
+    band[...] = jnp.where(jnp.abs(across) <= RAD, 1.0, 0.0).astype(band.dtype)
     for pad in (0, 1, planes + 2, planes + 3):
-        for which in range(2):
-            images[which, pad] = zero_plane
+        for which in range(5):
+            rows_sum[which, pad] = zero_plane
         for which in range(3):
             terms[which, pad] = zero_plane
+    for pad in (0, planes + 1):
+        images[1, pad] = zero_plane
 
     def place(which, plane, value, value_n):
         images[which, plane, :, pl.ds(own_col, width)] = value
@@ -300,7 +306,7 @@
         ((fixed_own, fixed_got, fixed_own_n, fixed_got_n), (warp_own, warp_got, warp_own_n, warp_got_n))
     ):
         for i in range(depth):
-            mine, theirs = 2 + half * depth + i, 2 + (1 - half) * depth + i
+            mine, theirs = 1 + half * depth + i, 1 + (1 - half) * depth + i
             place(
                 which, mine,
                 shift_in(own[i, pl.ds(start, SEND_ROWS), :].astype(jnp.float32)),
@@ -317,7 +323,7 @@
             value_n = jnp.where(outer, 0.0, rim_n[which, :, pl.ds(take, BLK_X)].astype(jnp.float32))
             value_n = jnp.where(near[: value_n.shape[0]], value_n, 0.0)
             for i in range(depth):
-                plane = 2 + base * depth + i
+                plane = 1 + base * depth + i
                 for at_half, row in ((0, 0), (1, window - EDGE)):
 
                     @pl.when(half == at_half)
@@ -327,51 +333,65 @@
 
     volume = float((2 * RAD + 1) ** 3)
 
-    def box(total):
-        return five(five(total, 0), 1)
-
-    def first_pass(z, carry):
-        f = [images[0, z + k] for k in range(5)]
-        w = [images[1, z + k] for k in range(5)]
-        sum_f = box(f[0] + f[1] + f[2] + f[3] + f[4])
-        sum_w = box(w[0] + w[1] + w[2] + w[3] + w[4])
-        sum_ff = box(sum(a * a for a in f[1:]) + f[0] * f[0])
-        sum_ww = box(sum(a * a for a in w[1:]) + w[0] * w[0])
-        sum_fw = box(sum(a * b for a, b in zip(f[1:], w[1:])) + f[0] * w[0])
-        cross = sum_fw - sum_f * sum_w / volume
-        var_f = sum_ff - sum_f * sum_f / volume
-        var_w = sum_ww - sum_w * sum_w / volume
+    def row_pass(z, carry):
+        f, w = images[0, z + 1], images[1, z + 1]
+        products = [f * f, w * w, f * w]
+        low = [value - value.astype(jnp.bfloat16).astype(jnp.float32) for value in products]
+        boxed = jnp.dot(
+            jnp.concatenate([f, w] + products + low, axis=0).astype(jnp.bfloat16), band[...], preferred_element_type=jnp.float32
+        )
+        pieces = [boxed[k * window : (k + 1) * window] for k in range(8)]
+        for which in range(5):
+            value = pieces[which] if which < 2 else pieces[which] + pieces[which + 3]
+            rows_sum[which, z + 2] = five(value, 0)
+        return carry
+
+    lax.fori_loop(0, planes, row_pass, 0, unroll=8)
+
+    def term_pass(z, carry):
+        sum_f, sum_w, sum_ff, sum_ww, sum_fw = (
+            rows_sum[which, z] + rows_sum[which, z + 1] + rows_sum[which, z + 2]
+            + rows_sum[which, z + 3] + rows_sum[which, z + 4]
+            for which in range(5)
+        )
+        cross = sum_fw - sum_f * sum_w * (1.0 / volume)
+        var_f = sum_ff - sum_f * sum_f * (1.0 / volume)
+        var_w = sum_ww - sum_w * sum_w * (1.0 / volume)
         inverse = 1.0 / (var_f * var_w + den_floor)
         ratio = cross * inverse
         term_a = 2.0 * ratio
         term_b = -(ratio * ratio) * var_f
-        term_c = -(term_a * sum_f + 2.0 * term_b * sum_w) / volume
-        terms[0, z + 2] = jnp.where(inside, term_a, 0.0)
-        terms[1, z + 2] = jnp.where(inside, term_b, 0.0)
-        terms[2, z + 2] = jnp.where(inside, term_c, 0.0)
+        term_c = -(term_a * sum_f + 2.0 * term_b * sum_w) * (1.0 / volume)
+        values = [five(jnp.where(inside, value, 0.0), 0) for value in (term_a, term_b, term_c)]
+        low = [value - value.astype(jnp.bfloat16).astype(jnp.float32) for value in values]
+        boxed = jnp.dot(
+            jnp.concatenate(values + low, axis=0).astype(jnp.bfloat16), band[...], preferred_element_type=jnp.float32
+        )
+        for which in range(3):
+            terms[which, z + 2] = boxed[which * window : (which + 1) * window] + boxed[(which + 3) * window : (which + 4) * window]
         return carry
 
-    lax.fori_loop(0, planes, first_pass, 0)
+    lax.fori_loop(0, planes, term_pass, 0, unroll=8)
     for d in range(3):
         sums[d] = zero_plane
     owned = (levels >= EDGE) & (levels < window - EDGE)
 
-    def second_pass(z, carry):
-        boxes = []
-        for which in range(3):
-            t = [terms[which, z + k] for k in range(5)]
-            boxes.append(box(t[0] + t[1] + t[2] + t[3] + t[4]))
-        f, w = images[0, z + 2], images[1, z + 2]
-        gain = -(f * boxes[0] + 2.0 * w * boxes[1] + boxes[2])
+    def gain_pass(z, carry):
+        box_a, box_b, box_c = (
+            terms[which, z] + terms[which, z + 1] + terms[which, z + 2] + terms[which, z + 3] + terms[which, z + 4]
+            for which in range(3)
+        )
+        f, w = images[0, z + 1], images[1, z + 1]
+        gain = -(f * box_a + 2.0 * w * box_b + box_c)
         u = z.astype(jnp.float32) * (1.0 / SPACING)
         weight = (3.0 * u * u * u - 6.0 * u * u + 4.0) * (0.5 / 6.0)
         gain = jnp.where(owned, gain, 0.0) * weight
-        sums[0] += gain * (images[1, z + 3] - images[1, z + 1])
+        sums[0] += gain * (images[1, z + 2] - images[1, z])
         sums[1] += gain * (pltpu.roll(w, window - 1, 0) - pltpu.roll(w, 1, 0))
         sums[2] += gain * (pltpu.roll(w, span - 1, 1) - pltpu.roll(w, 1, 1))
         return carry
 
-    lax.fori_loop(0, planes, second_pass, 0)
+    lax.fori_loop(0, planes, gain_pass, 0, unroll=8)
     for d in range(3):
         along_x = lax.dot_general(
             sums[d], table_x[...], (((1,), (1,)), ((), ())),
@@ -381,6 +401,21 @@
             table_y[...], along_x, (((1,), (0,)), ((), ())),
             precision=lax.Precision.HIGHEST, preferred_element_type=jnp.float32,
         )
+
+
+def held(array, space=pltpu.VMEM):
+    return pltpu.with_memory_space_constraint(array, space)
+
+
+def local_kernel(kernel, shapes, dtype, scalars, arrays, scratch=()):
+    smem, vmem = (pl.BlockSpec(memory_space=space) for space in (pltpu.SMEM, pltpu.VMEM))
+    return pl.pallas_call(
+        kernel,
+        out_shape=[pltpu.VMEM(shape, dtype) for shape in shapes],
+        in_specs=[smem] * len(scalars) + [vmem] * len(arrays),
+        out_specs=[vmem] * len(shapes),
+        scratch_shapes=list(scratch),
+    )(*scalars, *(held(array) for array in arrays))
 
 
 def fast_body(tiles, fixed_image, moving_image, source_tile, block_shifts):
@@ -388,21 +423,20 @@
     me, half, side = lax.axis_index("tile"), lax.axis_index("gz"), lax.axis_index("rep")
     sources = source_tile[:, 0, :, 0]
     shifts = block_shifts[0, 0]
-    first, last = (me == 0) & (half == 0), (me == tiles - 1) & (half == 1)
-    place = jnp.stack([me, half, side, first.astype(jnp.int32), last.astype(jnp.int32)])
     blocks = sources.shape[1]
     cap = MAX_NAMED if tiles == 4 else blocks
-    smem = pl.BlockSpec(memory_space=pltpu.SMEM)
-    vmem = pl.BlockSpec(memory_space=pltpu.VMEM)
-    pack_shape = jax.ShapeDtypeStruct((cap, depth, BLK_Y, BLK_X), jnp.bfloat16)
-    send_shape = jax.ShapeDtypeStruct((depth, SEND_ROWS, width), jnp.bfloat16)
-    rim_shape = jax.ShapeDtypeStruct((2, depth * EDGE, width), jnp.bfloat16)
-    *packs, fixed_send = pl.pallas_call(
+    pack_shape = (cap, depth, BLK_Y, BLK_X)
+    send_shape = (depth, SEND_ROWS, width)
+    rim_shape = (2, depth * EDGE, width)
+    sources, shifts = held(sources, pltpu.SMEM), held(shifts, pltpu.SMEM)
+    moving_image, fixed_image = held(moving_image), held(fixed_image)
+    *packs, fixed_send = local_kernel(
         functools.partial(pack_kernel, tiles),
-        out_shape=[pack_shape] * (tiles - 1) + [send_shape],
-        in_specs=[smem, smem, vmem, vmem],
-        out_specs=[vmem] * tiles,
-    )(sources, place, moving_image, fixed_image)
+        [pack_shape] * (tiles - 1) + [send_shape],
+        jnp.bfloat16,
+        [sources],
+        [moving_image, fixed_image],
+    )
 
     trio = ("tile", "gz", "rep")
 
@@ -425,13 +459,14 @@
     ]
     fixed_got = lax.ppermute(fixed_send, "gz", swap)
     fixed_own_n = lax.ppermute(fixed_image, "rep", swap)
-    own, send, rim_straight, rim_slant = pl.pallas_call(
+    own, send, rim_straight, rim_slant = local_kernel(
         functools.partial(unpack_kernel, tiles),
-        out_shape=[jax.ShapeDtypeStruct(moving_image.shape, jnp.bfloat16), send_shape, rim_shape, rim_shape],
-        in_specs=[smem, smem, smem] + [vmem] * (tiles + 1),
-        out_specs=[vmem] * 4,
-        scratch_shapes=[pltpu.VMEM((2, 2, depth * EDGE, width), jnp.float32)],
-    )(sources, shifts, place, moving_image, fixed_image, *got)
+        [moving_image.shape, send_shape, rim_shape, rim_shape],
+        jnp.bfloat16,
+        [sources, shifts],
+        [moving_image, fixed_image, *got],
+        [pltpu.VMEM((2, 2, depth * EDGE, width), jnp.float32)],
+    )
 
     warp_got = lax.ppermute(send, "gz", swap)
     straight_got = lax.ppermute(rim_straight, trio, straight)
@@ -449,20 +484,23 @@
     table_y = spline_table(half * (height // 2) - EDGE, window, -2, row_knots + 4)
     table_y = jnp.where(((row_at >= EDGE) & (row_at < window - EDGE))[:, None], table_y, 0.0).T
     table_x = spline_table(side * BLK_X, span, side * col_knots, col_knots).T
-    planes = 2 * depth + 4
-    part = pl.pallas_call(
-        main_kernel,
-        out_shape=jax.ShapeDtypeStruct((3, row_knots + 4, col_knots), jnp.float32),
-        in_specs=[smem] + [vmem] * 14,
-        out_specs=vmem,
-        scratch_shapes=[
-            pltpu.VMEM((2, planes, window, span), jnp.float32),
-            pltpu.VMEM((3, planes, window, span), jnp.float32),
+    planes = 2 * depth
+    part, = local_kernel(
+        functools.partial(main_kernel, tiles),
+        [(3, row_knots + 4, col_knots)],
+        jnp.float32,
+        [],
+        [
+            fixed_image, fixed_got, own, warp_got, straight_got, slant_got,
+            fixed_own_n, fixed_got_n, warp_own_n, warp_got_n, straight_n, slant_n, table_y, table_x,
+        ],
+        [
+            pltpu.VMEM((2, planes + 2, window, span), jnp.float32),
+            pltpu.VMEM((5, planes + 4, window, span), jnp.float32),
+            pltpu.VMEM((3, planes + 4, window, span), jnp.float32),
             pltpu.VMEM((3, window, span), jnp.float32),
+            pltpu.VMEM((span, span), jnp.bfloat16),
         ],
-    )(
-        place, fixed_image, fixed_got, own, warp_got, straight_got, slant_got,
-        fixed_own_n, fixed_got_n, warp_own_n, warp_got_n, straight_n, slant_n, table_y, table_x,
     )
     back = [(b, a) for a, b in straight]
     across = lax.ppermute(part, "gz", swap)

time: 43.8 us -> 37 us (0.84)
  Pallas kernels: 14.5 us -> 7.22 us
  waiting for transfers between devices: 7.34 us -> 9.25 us
  other arithmetic: 2.1 us -> 0.91 us
    pallas_call x3, Pallas kernels: 14.5 us -> 7.22 us  [local_kernel(): pl.pallas_call(kernel, out_shape=[pltpu.VMEM(shape, dtype) for shape in s...]
    ppermute x1, starting transfers between devices: 2.01 us -> 4.31 us  [fast_body(): part_straight = lax.ppermute(part, trio, back)]
    ppermute x1, starting transfers between devices: 2.99 us -> 0.8 us  [fast_body(): warp_got = lax.ppermute(send, 'gz', swap)]
    ppermute x1, waiting for transfers between devices: 0.01 us -> 1.87 us  [fast_body(): straight_got = lax.ppermute(rim_straight, trio, straight)]
    ppermute x1, waiting for transfers between devices: 1.09 us -> 0.24 us  [fast_body(): warp_got = lax.ppermute(send, 'gz', swap)]
    another operation x1 -> x0, local copies, waits for them, and re-layouts: 0.67 us -> none  [fast_body(): jnp.stack([me, half, side, first.astype(jnp.int32), last.astype(jnp.int32)])]
    add x1, other arithmetic: 0.67 us -> 0.08 us  [spline_table(): table + jnp.where(targets[None, :] == (knots + offset - 1)[:, None], weig...]
    select_n x1, other arithmetic: 0.67 us -> 0.07 us  [fast_body(): jnp.where(((row_at >= EDGE) & (row_at < window - EDGE))[:, None], table_y...]
  transfers between devices with their start and end apart: 16 -> 16, of which waited for: 7 -> 10; matrix products, arithmetic and copies ran while one was open for 6% -> 3% of each run, Pallas kernels for 9% -> 5%
where the time goes in v2:
time: 37 us; the launch traced here: 36.8 us
  starting transfers between devices  16.2 us (44%)
  waiting for transfers between devices  9.25 us (25%)
  Pallas kernels  7.22 us (20%)
  local copies, waits for them, and re-layouts  3.16 us (9%)
  other arithmetic  0.91 us (2%)
    pallas_call x3, Pallas kernels, local_kernel(): pl.pallas_call(kernel, out_shape=[pltpu.VMEM(shape, dtype) for shape in s...  7.22 us
    ppermute x3, starting transfers between devices, fast_body(): lax.ppermute(pack, 'tile', [(t, t ^ step) for t in range(tiles)])  5.24 us
    ppermute x1, starting transfers between devices, fast_body(): part_straight = lax.ppermute(part, trio, back)  4.31 us
    ppermute x3, waiting for transfers between devices, fast_body(): lax.ppermute(pack, 'tile', [(t, t ^ step) for t in range(tiles)])  2.78 us
    unnamed x8, local copies, waits for them, and re-layouts  2.49 us
    ppermute x1, waiting for transfers between devices, fast_body(): across = lax.ppermute(part, 'gz', swap)  2.16 us
    ppermute x1, waiting for transfers between devices, fast_body(): straight_got = lax.ppermute(rim_straight, trio, straight)  1.87 us
    ppermute x1, starting transfers between devices, fast_body(): fixed_got = lax.ppermute(fixed_send, 'gz', swap)  1.7 us
  transfers between devices with their start and end apart: 16, of which 10 were waited for; matrix products, arithmetic and copies ran while one was open for 3% of the time, Pallas kernels for 5%

profile of v2, /device:TPU:0, one launch (start us, length us, event | category | flops | bytes accessed | tf_op | source)
XLA Modules:
  0.0 36.8 jit_solution(10538804455022050877)
XLA Ops:
  0.0 0.5 %collective-permute-start.7 = (bf16[4,64,256]{2,1,0:T(8,128)(2,1)}, bf16[4,64,256]{2,1,0:T(8,128)(2,1)S(1)}, u32[]{:S(2)}, u32[]{:S(2)}) collective-permute-start(bf16[4,64,256]{2,1,0:T(8,128)(2,1)} %fixed_own.1), channel_id=1, source_target_pairs={{0,1},{1,0},{2,3},{3,2},{4,5},{5,4},{6,7},{7,6},{8,9},{9,8},{10,11... | collective-permute-start | bytes 393224 | tf_op jit(solution)/shard_map/ppermute | solution.py:461
  0.5 0.0 copy-start
  0.5 0.9 %copy-done = bf16[4,64,256]{2,1,0:T(8,128)(2,1)S(1)} copy-done((bf16[4,64,256]{2,1,0:T(8,128)(2,1)S(1)}, bf16[4,64,256]{2,1,0:T(8,128)(2,1)}, u32[]{:S(2)}) %copy-start) | copy-done | bytes 131096
  1.4 0.0 copy-start.2
  1.4 0.9 %copy-done.2 = bf16[4,64,256]{2,1,0:T(8,128)(2,1)S(1)} copy-done((bf16[4,64,256]{2,1,0:T(8,128)(2,1)S(1)}, bf16[4,64,256]{2,1,0:T(8,128)(2,1)}, u32[]{:S(2)}) %copy-start.2) | copy-done | bytes 131096
  2.3 0.9 %shard_map.46 = (bf16[4,4,16,128]{3,2,1,0:T(8,128)(2,1)S(1)}, bf16[4,4,16,128]{3,2,1,0:T(8,128)(2,1)S(1)}, bf16[4,4,16,128]{3,2,1,0:T(8,128)(2,1)S(1)}, bf16[4,48,256]{2,1,0:T(8,128)(2,1)S(1)}) custom-call(s32[4,8]{1,0:T(4,128)} %bitcast.6, bf16[4,64,256]{2,1,0:T(8,128)(2,1)S(1)} %copy-done.2, bf16[4,64,256]{2,1,0:T(8,128)(2,1)S(1)} %copy-done), custom_call_target="tpu_custom_call" | custom-call | tf_op jit(solution)/shard_map/pallas_call | solution.py:412
  3.2 2.6 %collective-permute-start.1 = (bf16[4,4,16,128]{3,2,1,0:T(8,128)(2,1)S(1)}, bf16[4,4,16,128]{3,2,1,0:T(8,128)(2,1)S(1)}, u32[]{:S(2)}, u32[]{:S(2)}) collective-permute-start(bf16[4,4,16,128]{3,2,1,0:T(8,128)(2,1)S(1)} %get-tuple-element.14), channel_id=1, source_target_pairs={{0,4},{4,0},{8,12},{12,8},{1,5},{5,1},{9,13},{13,9},{2,6},{6,2},{1... | collective-permute-start | bytes 196616 | tf_op jit(solution)/shard_map/ppermute | solution.py:457
  5.8 2.6 %collective-permute-start.2 = (bf16[4,4,16,128]{3,2,1,0:T(8,128)(2,1)S(1)}, bf16[4,4,16,128]{3,2,1,0:T(8,128)(2,1)S(1)}, u32[]{:S(2)}, u32[]{:S(2)}) collective-permute-start(bf16[4,4,16,128]{3,2,1,0:T(8,128)(2,1)S(1)} %get-tuple-element.15), channel_id=1, source_target_pairs={{0,8},{4,12},{8,0},{12,4},{1,9},{5,13},{9,1},{13,5},{2,10},{6,14},... | collective-permute-start | bytes 196616 | tf_op jit(solution)/shard_map/ppermute | solution.py:457
  8.4 0.0 collective-permute-start.3
  8.5 1.7 %collective-permute-start = (bf16[4,48,256]{2,1,0:T(8,128)(2,1)S(1)}, bf16[4,48,256]{2,1,0:T(8,128)(2,1)S(1)}, u32[]{:S(2)}, u32[]{:S(2)}) collective-permute-start(bf16[4,48,256]{2,1,0:T(8,128)(2,1)S(1)} %get-tuple-element.13), channel_id=1, source_target_pairs={{0,2},{2,0},{1,3},{3,1},{4,6},{6,4},{5,7},{7,5},{8,10},{10,8},{9,1... | collective-permute-start | bytes 294920 | tf_op jit(solution)/shard_map/ppermute | solution.py:460
  10.3 0.0 copy-start.3
  10.3 0.7 %copy-done.3 = s32[1,1,8,2]{2,3,1,0:T(2,128)S(1)} copy-done((s32[1,1,8,2]{2,3,1,0:T(2,128)S(1)}, s32[1,1,8,2]{2,3,1,0:T(2,128)}, u32[]{:S(2)}) %copy-start.3) | copy-done | bytes 88
  11.0 0.7 %copy.5.shift_ref = s32[8,2]{1,0:T(8,128)} copy(s32[8,2]{0,1:T(2,128)S(1)} %bitcast.8) | data formatting | bytes 128 | tf_op jit(solution)/shard_map/squeeze | solution.py:425
  11.7 0.1 select_add_fusion.table_x
  11.8 0.0 copy-start.1
  11.8 0.0 collective-permute-done.1.refs_0_
  11.8 1.0 %collective-permute-done.2.refs_1_ = bf16[4,4,16,128]{3,2,1,0:T(8,128)(2,1)S(1)} collective-permute-done((bf16[4,4,16,128]{3,2,1,0:T(8,128)(2,1)S(1)}, bf16[4,4,16,128]{3,2,1,0:T(8,128)(2,1)S(1)}, u32[]{:S(2)}, u32[]{:S(2)}) %collective-permute-start.2) | collective-permute-done | bytes 65568 | tf_op jit(solution)/shard_map/ppermute | solution.py:457
  12.8 1.8 %collective-permute-done.3.refs_2_ = bf16[4,4,16,128]{3,2,1,0:T(8,128)(2,1)S(1)} collective-permute-done((bf16[4,4,16,128]{3,2,1,0:T(8,128)(2,1)S(1)}, bf16[4,4,16,128]{3,2,1,0:T(8,128)(2,1)S(1)}, u32[]{:S(2)}, u32[]{:S(2)}) %collective-permute-start.3) | collective-permute-done | bytes 65568 | tf_op jit(solution)/shard_map/ppermute | solution.py:457
  14.6 1.0 %shard_map.47 = (bf16[4,64,256]{2,1,0:T(8,128)(2,1)S(1)}, bf16[4,48,256]{2,1,0:T(8,128)(2,1)S(1)}, bf16[2,16,256]{2,1,0:T(8,128)(2,1)S(1)}, bf16[2,16,256]{2,1,0:T(8,128)(2,1)S(1)}) custom-call(s32[4,8]{1,0:T(4,128)} %bitcast.7, s32[8,2]{1,0:T(8,128)} %copy.5.shift_ref, bf16[4,64,256]{2,1,0:T(8,128)(2,1)S(1)} %copy-done.2, bf16[4,64,256]{2,1,0:T(8,128)(2,1)S(1)} %copy-done, ...), custom_call_target="tpu_custom_call" | custom-call | tf_op jit(solution)/shard_map/pallas_call | solution.py:412
  15.6 1.3 %collective-permute-start.5 = (bf16[2,16,256]{2,1,0:T(8,128)(2,1)S(1)}, bf16[2,16,256]{2,1,0:T(8,128)(2,1)S(1)}, u32[]{:S(2)}, u32[]{:S(2)}) collective-permute-start(bf16[2,16,256]{2,1,0:T(8,128)(2,1)S(1)} %get-tuple-element.19), channel_id=1, source_target_pairs={{0,4},{2,0},{4,8},{6,2},{8,12},{10,6},{12,14},{14,10},{1,5},{3,1},... | collective-permute-start | bytes 49160 | tf_op jit(solution)/shard_map/ppermute | solution.py:472
  16.8 0.8 %collective-permute-start.4 = (bf16[4,48,256]{2,1,0:T(8,128)(2,1)S(1)}, bf16[4,48,256]{2,1,0:T(8,128)(2,1)S(1)}, u32[]{:S(2)}, u32[]{:S(2)}) collective-permute-start(bf16[4,48,256]{2,1,0:T(8,128)(2,1)S(1)} %get-tuple-element.18), channel_id=1, source_target_pairs={{0,2},{2,0},{1,3},{3,1},{4,6},{6,4},{5,7},{7,5},{8,10},{10,8},{9,1... | collective-permute-start | bytes 294920 | tf_op jit(solution)/shard_map/ppermute | solution.py:471
  17.6 0.0 collective-permute-start.6
  17.6 1.9 %collective-permute-done.5.straight = bf16[2,16,256]{2,1,0:T(8,128)(2,1)S(1)} collective-permute-done((bf16[2,16,256]{2,1,0:T(8,128)(2,1)S(1)}, bf16[2,16,256]{2,1,0:T(8,128)(2,1)S(1)}, u32[]{:S(2)}, u32[]{:S(2)}) %collective-permute-start.5) | collective-permute-done | bytes 16416 | tf_op jit(solution)/shard_map/ppermute | solution.py:472
  19.5 0.0 collective-permute-start.11
  19.5 0.0 collective-permute-done.6.slant
  19.5 0.5 %collective-permute-start.9 = (bf16[4,64,256]{2,1,0:T(8,128)(2,1)S(1)}, bf16[4,64,256]{2,1,0:T(8,128)(2,1)S(1)}, u32[]{:S(2)}, u32[]{:S(2)}) collective-permute-start(bf16[4,64,256]{2,1,0:T(8,128)(2,1)S(1)} %get-tuple-element.17.warp_own), channel_id=1, source_target_pairs={{0,1},{1,0},{2,3},{3,2},{4,5},{5,4},{6,7},{7,6},{8,9},{9,8},{10,11... | collective-permute-start | bytes 393224 | tf_op jit(solution)/shard_map/ppermute | solution.py:475
  20.0 0.7 %collective-permute-done.11.straight_n = bf16[2,16,256]{2,1,0:T(8,128)(2,1)S(1)} collective-permute-done((bf16[2,16,256]{2,1,0:T(8,128)(2,1)S(1)}, bf16[2,16,256]{2,1,0:T(8,128)(2,1)S(1)}, u32[]{:S(2)}, u32[]{:S(2)}) %collective-permute-start.11) | collective-permute-done | bytes 16416 | tf_op jit(solution)/shard_map/ppermute | solution.py:477
  20.7 0.2 collective-permute-start.12
  20.9 0.0 collective-permute-done.fixed_got
  20.9 0.3 collective-permute-start.8
  21.2 0.2 collective-permute-done.4.warp_got
  21.5 0.0 collective-permute-start.10
  21.5 0.1 add_select_fusion.table_y
  21.5 0.4 collective-permute-done.12.slant_n
  21.9 0.0 collective-permute-done.7.fixed_own_n
  21.9 0.0 collective-permute-done.9.warp_own_n
  21.9 0.3 collective-permute-done.8.fixed_got_n
  22.2 0.6 %collective-permute-done.10.warp_got_n = bf16[4,48,256]{2,1,0:T(8,128)(2,1)S(1)} collective-permute-done((bf16[4,48,256]{2,1,0:T(8,128)(2,1)S(1)}, bf16[4,48,256]{2,1,0:T(8,128)(2,1)S(1)}, u32[]{:S(2)}, u32[]{:S(2)}) %collective-permute-start.10) | collective-permute-done | bytes 98336 | tf_op jit(solution)/shard_map/ppermute | solution.py:476
  22.8 0.0 copy-done.1
  22.8 5.3 %shard_map.48 = f32[3,8,16]{2,1,0:T(8,128)S(1)} custom-call(bf16[4,64,256]{2,1,0:T(8,128)(2,1)S(1)} %copy-done.1, bf16[4,48,256]{2,1,0:T(8,128)(2,1)S(1)} %collective-permute-done.fixed_got, bf16[4,64,256]{2,1,0:T(8,128)(2,1)S(1)} %get-tuple-element.17.warp_own, bf16[4,48,256]{2,1,0:T(8,128)(2,1)S(1)} %collective-permute-done.4.warp_got, ...), custom_call_target="tpu_custom_call" | custom-call | tf_op jit(solution)/shard_map/pallas_call | solution.py:412
  28.0 0.2 collective-permute-start.14
  28.2 4.3 %collective-permute-start.15 = (f32[3,8,16]{2,1,0:T(8,128)S(1)}, f32[3,8,16]{2,1,0:T(8,128)S(1)}, u32[]{:S(2)}, u32[]{:S(2)}) collective-permute-start(f32[3,8,16]{2,1,0:T(8,128)S(1)} %shard_map.48), channel_id=1, source_target_pairs={{4,0},{0,2},{8,4},{2,6},{12,8},{6,10},{14,12},{10,14},{5,1},{1,3},... | collective-permute-start | bytes 4616 | tf_op jit(solution)/shard_map/ppermute | solution.py:507
  32.5 1.2 %collective-permute-start.13 = (f32[3,8,16]{2,1,0:T(8,128)S(1)}, f32[3,8,16]{2,1,0:T(8,128)S(1)}, u32[]{:S(2)}, u32[]{:S(2)}) collective-permute-start(f32[3,8,16]{2,1,0:T(8,128)S(1)} %shard_map.48), channel_id=1, source_target_pairs={{0,2},{2,0},{1,3},{3,1},{4,6},{6,4},{5,7},{7,5},{8,10},{10,8},{9,1... | collective-permute-start | bytes 4616 | tf_op jit(solution)/shard_map/ppermute | solution.py:506
  33.8 0.0 collective-permute-done.14
  33.8 0.3 collective-permute-done.15
  34.1 2.2 %collective-permute-done.13 = f32[3,8,16]{2,1,0:T(8,128)S(1)} collective-permute-done((f32[3,8,16]{2,1,0:T(8,128)S(1)}, f32[3,8,16]{2,1,0:T(8,128)S(1)}, u32[]{:S(2)}, u32[]{:S(2)}) %collective-permute-start.13) | collective-permute-done | bytes 1568 | tf_op jit(solution)/shard_map/ppermute | solution.py:506
  36.2 0.6 %fusion.1 = f32[3,1,4,16]{3,2,1,0:T(4,128)} fusion(f32[3,8,16]{2,1,0:T(8,128)S(1)} %collective-permute-done.13, f32[3,8,16]{2,1,0:T(8,128)S(1)} %shard_map.48, f32[3,2,16]{2,1,0:T(2,128)S(1)} %get-tuple-element.22, f32[3,2,16]{2,1,0:T(2,128)S(1)} %get-tuple-element.21), kind=kLoop, calls=%fused_computation.3 | loop fusion | flops 576 | bytes 3072 | tf_op jit(solution)/shard_map/broadcast_in_dim | solution.py:514
  (12 shorter events, 0.2 us)
Async XLA Ops:
  0.0 21.9 %collective-permute-start.7 = (bf16[4,64,256]{2,1,0:T(8,128)(2,1)}, bf16[4,64,256]{2,1,0:T(8,128)(2,1)S(1)}, u32[]{:S(2)}, u32[]{:S(2)}) collective-permute-start(bf16[4,64,256]{2,1,0:T(8,128)(2,1)} %fixed_own.1), channel_id=1, source_target_pairs={{0,1},{1,0},{2,3},{3,2},{4,5},{5,4},{6,7},{7,6},{8,9},{9,8},{10,11... | collective-permute-start | bytes 393224 | tf_op jit(solution)/shard_map/ppermute | solution.py:461
  0.5 0.9 %copy-start = (bf16[4,64,256]{2,1,0:T(8,128)(2,1)S(1)}, bf16[4,64,256]{2,1,0:T(8,128)(2,1)}, u32[]{:S(2)}) copy-start(bf16[4,64,256]{2,1,0:T(8,128)(2,1)} %fixed_own.1) | copy-start | bytes 393220
  1.4 0.9 %copy-start.2 = (bf16[4,64,256]{2,1,0:T(8,128)(2,1)S(1)}, bf16[4,64,256]{2,1,0:T(8,128)(2,1)}, u32[]{:S(2)}) copy-start(bf16[4,64,256]{2,1,0:T(8,128)(2,1)} %moving_ref.3) | copy-start | bytes 393220
  3.2 8.6 %collective-permute-start.1 = (bf16[4,4,16,128]{3,2,1,0:T(8,128)(2,1)S(1)}, bf16[4,4,16,128]{3,2,1,0:T(8,128)(2,1)S(1)}, u32[]{:S(2)}, u32[]{:S(2)}) collective-permute-start(bf16[4,4,16,128]{3,2,1,0:T(8,128)(2,1)S(1)} %get-tuple-element.14), channel_id=1, source_target_pairs={{0,4},{4,0},{8,12},{12,8},{1,5},{5,1},{9,13},{13,9},{2,6},{6,2},{1... | collective-permute-start | bytes 196616 | tf_op jit(solution)/shard_map/ppermute | solution.py:457
  5.8 6.9 %collective-permute-start.2 = (bf16[4,4,16,128]{3,2,1,0:T(8,128)(2,1)S(1)}, bf16[4,4,16,128]{3,2,1,0:T(8,128)(2,1)S(1)}, u32[]{:S(2)}, u32[]{:S(2)}) collective-permute-start(bf16[4,4,16,128]{3,2,1,0:T(8,128)(2,1)S(1)} %get-tuple-element.15), channel_id=1, source_target_pairs={{0,8},{4,12},{8,0},{12,4},{1,9},{5,13},{9,1},{13,5},{2,10},{6,14},... | collective-permute-start | bytes 196616 | tf_op jit(solution)/shard_map/ppermute | solution.py:457
  8.4 6.1 %collective-permute-start.3 = (bf16[4,4,16,128]{3,2,1,0:T(8,128)(2,1)S(1)}, bf16[4,4,16,128]{3,2,1,0:T(8,128)(2,1)S(1)}, u32[]{:S(2)}, u32[]{:S(2)}) collective-permute-start(bf16[4,4,16,128]{3,2,1,0:T(8,128)(2,1)S(1)} %get-tuple-element.16), channel_id=1, source_target_pairs={{0,12},{4,8},{8,4},{12,0},{1,13},{5,9},{9,5},{13,1},{2,14},{6,10},... | collective-permute-start | bytes 196616 | tf_op jit(solution)/shard_map/ppermute | solution.py:457
  8.5 12.4 %collective-permute-start = (bf16[4,48,256]{2,1,0:T(8,128)(2,1)S(1)}, bf16[4,48,256]{2,1,0:T(8,128)(2,1)S(1)}, u32[]{:S(2)}, u32[]{:S(2)}) collective-permute-start(bf16[4,48,256]{2,1,0:T(8,128)(2,1)S(1)} %get-tuple-element.13), channel_id=1, source_target_pairs={{0,2},{2,0},{1,3},{3,1},{4,6},{6,4},{5,7},{7,5},{8,10},{10,8},{9,1... | collective-permute-start | bytes 294920 | tf_op jit(solution)/shard_map/ppermute | solution.py:460
  10.3 0.7 %copy-start.3 = (s32[1,1,8,2]{2,3,1,0:T(2,128)S(1)}, s32[1,1,8,2]{2,3,1,0:T(2,128)}, u32[]{:S(2)}) copy-start(s32[1,1,8,2]{2,3,1,0:T(2,128)} %param.7) | copy-start | bytes 196
  11.8 11.0 %copy-start.1 = (bf16[4,64,256]{2,1,0:T(8,128)(2,1)S(1)}, bf16[4,64,256]{2,1,0:T(8,128)(2,1)}, u32[]{:S(2)}) copy-start(bf16[4,64,256]{2,1,0:T(8,128)(2,1)} %fixed_own.1) | copy-start | bytes 393220
  15.6 4.0 %collective-permute-start.5 = (bf16[2,16,256]{2,1,0:T(8,128)(2,1)S(1)}, bf16[2,16,256]{2,1,0:T(8,128)(2,1)S(1)}, u32[]{:S(2)}, u32[]{:S(2)}) collective-permute-start(bf16[2,16,256]{2,1,0:T(8,128)(2,1)S(1)} %get-tuple-element.19), channel_id=1, source_target_pairs={{0,4},{2,0},{4,8},{6,2},{8,12},{10,6},{12,14},{14,10},{1,5},{3,1},... | collective-permute-start | bytes 49160 | tf_op jit(solution)/shard_map/ppermute | solution.py:472
  16.8 4.6 %collective-permute-start.4 = (bf16[4,48,256]{2,1,0:T(8,128)(2,1)S(1)}, bf16[4,48,256]{2,1,0:T(8,128)(2,1)S(1)}, u32[]{:S(2)}, u32[]{:S(2)}) collective-permute-start(bf16[4,48,256]{2,1,0:T(8,128)(2,1)S(1)} %get-tuple-element.18), channel_id=1, source_target_pairs={{0,2},{2,0},{1,3},{3,1},{4,6},{6,4},{5,7},{7,5},{8,10},{10,8},{9,1... | collective-permute-start | bytes 294920 | tf_op jit(solution)/shard_map/ppermute | solution.py:471
  17.6 1.9 %collective-permute-start.6 = (bf16[2,16,256]{2,1,0:T(8,128)(2,1)S(1)}, bf16[2,16,256]{2,1,0:T(8,128)(2,1)S(1)}, u32[]{:S(2)}, u32[]{:S(2)}) collective-permute-start(bf16[2,16,256]{2,1,0:T(8,128)(2,1)S(1)} %get-tuple-element.20), channel_id=1, source_target_pairs={{0,1},{2,4},{4,2},{6,8},{8,6},{10,12},{12,10},{14,15},{1,0},{3,5},... | collective-permute-start | bytes 49160 | tf_op jit(solution)/shard_map/ppermute | solution.py:473
  19.5 1.2 %collective-permute-start.11 = (bf16[2,16,256]{2,1,0:T(8,128)(2,1)S(1)}, bf16[2,16,256]{2,1,0:T(8,128)(2,1)S(1)}, u32[]{:S(2)}, u32[]{:S(2)}) collective-permute-start(bf16[2,16,256]{2,1,0:T(8,128)(2,1)S(1)} %collective-permute-done.5.straight), channel_id=1, source_target_pairs={{0,1},{1,0},{2,3},{3,2},{4,5},{5,4},{6,7},{7,6},{8,9},{9,8},{10,11... | collective-permute-start | bytes 49160 | tf_op jit(solution)/shard_map/ppermute | solution.py:477
  19.5 2.4 %collective-permute-start.9 = (bf16[4,64,256]{2,1,0:T(8,128)(2,1)S(1)}, bf16[4,64,256]{2,1,0:T(8,128)(2,1)S(1)}, u32[]{:S(2)}, u32[]{:S(2)}) collective-permute-start(bf16[4,64,256]{2,1,0:T(8,128)(2,1)S(1)} %get-tuple-element.17.warp_own), channel_id=1, source_target_pairs={{0,1},{1,0},{2,3},{3,2},{4,5},{5,4},{6,7},{7,6},{8,9},{9,8},{10,11... | collective-permute-start | bytes 393224 | tf_op jit(solution)/shard_map/ppermute | solution.py:475
  20.7 1.2 %collective-permute-start.12 = (bf16[2,16,256]{2,1,0:T(8,128)(2,1)S(1)}, bf16[2,16,256]{2,1,0:T(8,128)(2,1)S(1)}, u32[]{:S(2)}, u32[]{:S(2)}) collective-permute-start(bf16[2,16,256]{2,1,0:T(8,128)(2,1)S(1)} %collective-permute-done.6.slant), channel_id=1, source_target_pairs={{0,1},{1,0},{2,3},{3,2},{4,5},{5,4},{6,7},{7,6},{8,9},{9,8},{10,11... | collective-permute-start | bytes 49160 | tf_op jit(solution)/shard_map/ppermute | solution.py:478
  20.9 1.3 %collective-permute-start.8 = (bf16[4,48,256]{2,1,0:T(8,128)(2,1)S(1)}, bf16[4,48,256]{2,1,0:T(8,128)(2,1)S(1)}, u32[]{:S(2)}, u32[]{:S(2)}) collective-permute-start(bf16[4,48,256]{2,1,0:T(8,128)(2,1)S(1)} %collective-permute-done.fixed_got), channel_id=1, source_target_pairs={{0,1},{1,0},{2,3},{3,2},{4,5},{5,4},{6,7},{7,6},{8,9},{9,8},{10,11... | collective-permute-start | bytes 294920 | tf_op jit(solution)/shard_map/ppermute | solution.py:474
  21.5 1.3 %collective-permute-start.10 = (bf16[4,48,256]{2,1,0:T(8,128)(2,1)S(1)}, bf16[4,48,256]{2,1,0:T(8,128)(2,1)S(1)}, u32[]{:S(2)}, u32[]{:S(2)}) collective-permute-start(bf16[4,48,256]{2,1,0:T(8,128)(2,1)S(1)} %collective-permute-done.4.warp_got), channel_id=1, source_target_pairs={{0,1},{1,0},{2,3},{3,2},{4,5},{5,4},{6,7},{7,6},{8,9},{9,8},{10,11... | collective-permute-start | bytes 294920 | tf_op jit(solution)/shard_map/ppermute | solution.py:476
  28.0 5.7 %collective-permute-start.14 = (f32[3,8,16]{2,1,0:T(8,128)S(1)}, f32[3,8,16]{2,1,0:T(8,128)S(1)}, u32[]{:S(2)}, u32[]{:S(2)}) collective-permute-start(f32[3,8,16]{2,1,0:T(8,128)S(1)} %shard_map.48), channel_id=1, source_target_pairs={{0,1},{2,4},{4,2},{6,8},{8,6},{10,12},{12,10},{14,15},{1,0},{3,5},... | collective-permute-start | bytes 4616 | tf_op jit(solution)/shard_map/ppermute | solution.py:508
  28.2 5.8 %collective-permute-start.15 = (f32[3,8,16]{2,1,0:T(8,128)S(1)}, f32[3,8,16]{2,1,0:T(8,128)S(1)}, u32[]{:S(2)}, u32[]{:S(2)}) collective-permute-start(f32[3,8,16]{2,1,0:T(8,128)S(1)} %shard_map.48), channel_id=1, source_target_pairs={{4,0},{0,2},{8,4},{2,6},{12,8},{6,10},{14,12},{10,14},{5,1},{1,3},... | collective-permute-start | bytes 4616 | tf_op jit(solution)/shard_map/ppermute | solution.py:507
  32.5 3.7 %collective-permute-start.13 = (f32[3,8,16]{2,1,0:T(8,128)S(1)}, f32[3,8,16]{2,1,0:T(8,128)S(1)}, u32[]{:S(2)}, u32[]{:S(2)}) collective-permute-start(f32[3,8,16]{2,1,0:T(8,128)S(1)} %shard_map.48), channel_id=1, source_target_pairs={{0,2},{2,0},{1,3},{3,1},{4,6},{6,4},{5,7},{7,5},{8,10},{10,8},{9,1... | collective-permute-start | bytes 4616 | tf_op jit(solution)/shard_map/ppermute | solution.py:506

commit v3 on v2

--- a/solution.py
+++ b/solution.py
@@ -185,28 +185,26 @@
 
 
 def pack_kernel(tiles, source_ref, moving_ref, fixed_ref, *out_refs):
-    me, half = lax.axis_index("tile"), lax.axis_index("gz")
-    packs, fixed_out = out_refs[:-1], out_refs[-1]
+    packs, moving_out, fixed_out = out_refs[:-2], out_refs[-2], out_refs[-1]
+    moving_out[...] = moving_ref[...]
+    fixed_out[...] = fixed_ref[...]
+    me = lax.axis_index("tile")
     height, width = moving_ref.shape[1:]
     xblocks = width // BLK_X
     blocks = (height // BLK_Y) * xblocks
+    cap = packs[0].shape[0]
     for step in range(1, tiles):
-        pack = packs[step - 1]
-        pack[...] = jnp.zeros_like(pack)
         other = lax.bitwise_xor(me, step)
         count = jnp.int32(0)
+        chosen = [jnp.int32(0)] * cap
         for block in range(blocks):
-            row, col = (block // xblocks) * BLK_Y, (block % xblocks) * BLK_X
             named = source_ref[other, block] == me
-
-            @pl.when(named)
-            def _(pack=pack, count=count, row=row, col=col):
-                slot = jnp.minimum(count, pack.shape[0] - 1)
-                pack[slot] = moving_ref[:, row : row + BLK_Y, col : col + BLK_X]
-
+            chosen = [jnp.where(named & (count == slot), block, old) for slot, old in enumerate(chosen)]
             count = count + named.astype(jnp.int32)
-    start = pl.multiple_of((1 - half) * BLK_Y, BLK_Y)
-    fixed_out[...] = fixed_ref[:, pl.ds(start, SEND_ROWS), :]
+        for slot, block in enumerate(chosen):
+            row = pl.multiple_of(block // xblocks * BLK_Y, BLK_Y)
+            col = pl.multiple_of(lax.rem(block, xblocks) * BLK_X, BLK_X)
+            packs[step - 1][slot] = moving_ref[:, pl.ds(row, BLK_Y), pl.ds(col, BLK_X)]
 
 
 def unpack_kernel(tiles, source_ref, shift_ref, moving_ref, fixed_ref, *refs):
@@ -314,8 +312,8 @@
             )
             place(
                 which, theirs,
-                shift_in(got[i].astype(jnp.float32)),
-                shift_in(got_n[i, :, pl.ds(take, BLK_X)].astype(jnp.float32)),
+                shift_in(got[i, pl.ds(start if which == 0 else 0, SEND_ROWS), :].astype(jnp.float32)),
+                shift_in(got_n[i, pl.ds(start if which == 0 else 0, SEND_ROWS), pl.ds(take, BLK_X)].astype(jnp.float32)),
             )
         outer = (first + last) != 0
         for rim, rim_n, base in ((straight, straight_n, half), (slant, slant_n, 1 - half)):
@@ -403,19 +401,15 @@
         )
 
 
-def held(array, space=pltpu.VMEM):
-    return pltpu.with_memory_space_constraint(array, space)
-
-
-def local_kernel(kernel, shapes, dtype, scalars, arrays, scratch=()):
-    smem, vmem = (pl.BlockSpec(memory_space=space) for space in (pltpu.SMEM, pltpu.VMEM))
+def local_kernel(kernel, shapes, dtype, arrays, scratch=()):
+    vmem = pl.BlockSpec(memory_space=pltpu.VMEM)
     return pl.pallas_call(
         kernel,
         out_shape=[pltpu.VMEM(shape, dtype) for shape in shapes],
-        in_specs=[smem] * len(scalars) + [vmem] * len(arrays),
+        in_specs=[vmem] * len(arrays),
         out_specs=[vmem] * len(shapes),
         scratch_shapes=list(scratch),
-    )(*scalars, *(held(array) for array in arrays))
+    )(*(pltpu.with_memory_space_constraint(array, pltpu.VMEM) for array in arrays))
 
 
 def fast_body(tiles, fixed_image, moving_image, source_tile, block_shifts):
@@ -428,15 +422,14 @@
     pack_shape = (cap, depth, BLK_Y, BLK_X)
     send_shape = (depth, SEND_ROWS, width)
     rim_shape = (2, depth * EDGE, width)
-    sources, shifts = held(sources, pltpu.SMEM), held(shifts, pltpu.SMEM)
-    moving_image, fixed_image = held(moving_image), held(fixed_image)
-    *packs, fixed_send = local_kernel(
+    smem, vmem = (pl.BlockSpec(memory_space=space) for space in (pltpu.SMEM, pltpu.VMEM))
+    *packs, moving_image, fixed_image = pl.pallas_call(
         functools.partial(pack_kernel, tiles),
-        [pack_shape] * (tiles - 1) + [send_shape],
-        jnp.bfloat16,
-        [sources],
-        [moving_image, fixed_image],
-    )
+        out_shape=[pltpu.VMEM(pack_shape, jnp.bfloat16)] * (tiles - 1)
+        + [pltpu.VMEM(moving_image.shape, jnp.bfloat16)] * 2,
+        in_specs=[smem, vmem, vmem],
+        out_specs=[vmem] * (tiles + 1),
+    )(sources, moving_image, fixed_image)
 
     trio = ("tile", "gz", "rep")
 
@@ -457,14 +450,13 @@
         lax.ppermute(pack, "tile", [(t, t ^ step) for t in range(tiles)])
         for step, pack in zip(range(1, tiles), packs)
     ]
-    fixed_got = lax.ppermute(fixed_send, "gz", swap)
+    fixed_got = lax.ppermute(fixed_image, "gz", swap)
     fixed_own_n = lax.ppermute(fixed_image, "rep", swap)
     own, send, rim_straight, rim_slant = local_kernel(
         functools.partial(unpack_kernel, tiles),
         [moving_image.shape, send_shape, rim_shape, rim_shape],
         jnp.bfloat16,
-        [sources, shifts],
-        [moving_image, fixed_image, *got],
+        [sources, shifts, moving_image, fixed_image, *got],
         [pltpu.VMEM((2, 2, depth * EDGE, width), jnp.float32)],
     )
 
@@ -489,7 +481,6 @@
         functools.partial(main_kernel, tiles),
         [(3, row_knots + 4, col_knots)],
         jnp.float32,
-        [],
         [
             fixed_image, fixed_got, own, warp_got, straight_got, slant_got,
             fixed_own_n, fixed_got_n, warp_own_n, warp_got_n, straight_n, slant_n, table_y, table_x,

time: 37 us -> 35.7 us (0.965)
  waiting for transfers between devices: 9.25 us -> 11.7 us
  local copies, waits for them, and re-layouts: 3.16 us -> 0.76 us
  starting transfers between devices: 16.2 us -> 15.3 us
  Pallas kernels: 7.22 us -> 6.82 us
    ppermute x3, waiting for transfers between devices: 2.78 us -> 4.86 us  [fast_body(): lax.ppermute(pack, 'tile', [(t, t ^ step) for t in range(tiles)])]
    unnamed x8 -> x4, local copies, waits for them, and re-layouts: 2.49 us -> 0.68 us
    pallas_call x3 -> x2, Pallas kernels: 7.22 us -> 5.64 us  [local_kernel(): pl.pallas_call(kernel, out_shape=[pltpu.VMEM(shape, dtype) for shape in s...]
    ppermute x1, starting transfers between devices: 1.7 us -> 3 us  [fast_body(): fixed_got = lax.ppermute(fixed_image, 'gz', swap)]
    pallas_call x0 -> x1, Pallas kernels: none -> 1.18 us  [fast_body(): pl.pallas_call(functools.partial(pack_kernel, tiles), out_shape=[pltpu.VM...]
    ppermute x1, waiting for transfers between devices: 0.3 us -> 1.25 us  [fast_body(): part_straight = lax.ppermute(part, trio, back)]
    ppermute x3, starting transfers between devices: 5.24 us -> 4.39 us  [fast_body(): lax.ppermute(pack, 'tile', [(t, t ^ step) for t in range(tiles)])]
    ppermute x1, waiting for transfers between devices: 2.16 us -> 1.56 us  [fast_body(): across = lax.ppermute(part, 'gz', swap)]
  transfers between devices with their start and end apart: 16 -> 16, of which waited for: 10 -> 9; matrix products, arithmetic and copies ran while one was open for 3% -> 1% of each run, Pallas kernels for 5% -> 1%
where the time goes in v3:
time: 35.7 us; the launch traced here: 35.5 us
  starting transfers between devices  15.3 us (43%)
  waiting for transfers between devices  11.7 us (33%)
  Pallas kernels  6.82 us (19%)
  other arithmetic  0.91 us (3%)
  local copies, waits for them, and re-layouts  0.76 us (2%)
    pallas_call x2, Pallas kernels, local_kernel(): pl.pallas_call(kernel, out_shape=[pltpu.VMEM(shape, dtype) for shape in s...  5.64 us
    ppermute x3, waiting for transfers between devices, fast_body(): lax.ppermute(pack, 'tile', [(t, t ^ step) for t in range(tiles)])  4.86 us
    ppermute x3, starting transfers between devices, fast_body(): lax.ppermute(pack, 'tile', [(t, t ^ step) for t in range(tiles)])  4.39 us
    ppermute x1, starting transfers between devices, fast_body(): part_straight = lax.ppermute(part, trio, back)  3.73 us
    ppermute x1, starting transfers between devices, fast_body(): fixed_got = lax.ppermute(fixed_image, 'gz', swap)  3 us
    ppermute x1, waiting for transfers between devices, fast_body(): straight_got = lax.ppermute(rim_straight, trio, straight)  1.87 us
    ppermute x1, waiting for transfers between devices, fast_body(): across = lax.ppermute(part, 'gz', swap)  1.56 us
    ppermute x1, starting transfers between devices, fast_body(): straight_got = lax.ppermute(rim_straight, trio, straight)  1.29 us
  transfers between devices with their start and end apart: 16, of which 9 were waited for; matrix products, arithmetic and copies ran while one was open for 1% of the time, Pallas kernels for 1%

profile of v3, /device:TPU:0, one launch (start us, length us, event | category | flops | bytes accessed | tf_op | source)
XLA Modules:
  0.0 35.5 jit_solution(5186685647253689986)
XLA Ops:
  0.0 1.2 %shard_map.46 = (bf16[4,4,16,128]{3,2,1,0:T(8,128)(2,1)S(1)}, bf16[4,4,16,128]{3,2,1,0:T(8,128)(2,1)S(1)}, bf16[4,4,16,128]{3,2,1,0:T(8,128)(2,1)S(1)}, bf16[4,6...) custom-call(s32[4,8]{1,0:T(4,128)} %bitcast.6, bf16[4,64,256]{2,1,0:T(8,128)(2,1)} %moving_ref.1, bf16[4,64,256]{2,1,0:T(8,128)(2,1)} %fixed_ref.1), custom_call_target="tpu_custom_call" | custom-call | tf_op jit(solution)/shard_map/pallas_call | solution.py:426
  1.2 3.0 %collective-permute-start = (bf16[4,64,256]{2,1,0:T(8,128)(2,1)S(1)}, bf16[4,64,256]{2,1,0:T(8,128)(2,1)S(1)}, u32[]{:S(2)}, u32[]{:S(2)}) collective-permute-start(bf16[4,64,256]{2,1,0:T(8,128)(2,1)S(1)} %get-tuple-element.14.fixed_ref.fixed_own), channel_id=1, source_target_pairs={{0,2},{2,0},{1,3},{3,1},{4,6},{6,4},{5,7},{7,5},{8,10},{10,8},{9,1... | collective-permute-start | bytes 393224 | tf_op jit(solution)/shard_map/ppermute | solution.py:453
  4.2 0.0 collective-permute-start.7
  4.2 1.6 %collective-permute-start.1 = (bf16[4,4,16,128]{3,2,1,0:T(8,128)(2,1)S(1)}, bf16[4,4,16,128]{3,2,1,0:T(8,128)(2,1)S(1)}, u32[]{:S(2)}, u32[]{:S(2)}) collective-permute-start(bf16[4,4,16,128]{3,2,1,0:T(8,128)(2,1)S(1)} %get-tuple-element.16), channel_id=1, source_target_pairs={{0,4},{4,0},{8,12},{12,8},{1,5},{5,1},{9,13},{13,9},{2,6},{6,2},{1... | collective-permute-start | bytes 196616 | tf_op jit(solution)/shard_map/ppermute | solution.py:450
  5.8 2.6 %collective-permute-start.2 = (bf16[4,4,16,128]{3,2,1,0:T(8,128)(2,1)S(1)}, bf16[4,4,16,128]{3,2,1,0:T(8,128)(2,1)S(1)}, u32[]{:S(2)}, u32[]{:S(2)}) collective-permute-start(bf16[4,4,16,128]{3,2,1,0:T(8,128)(2,1)S(1)} %get-tuple-element.17), channel_id=1, source_target_pairs={{0,8},{4,12},{8,0},{12,4},{1,9},{5,13},{9,1},{13,5},{2,10},{6,14},... | collective-permute-start | bytes 196616 | tf_op jit(solution)/shard_map/ppermute | solution.py:450
  8.4 0.2 collective-permute-start.3
  8.7 0.0 copy-start.1
  8.8 0.7 %copy-done.1 = s32[1,1,8,2]{2,3,1,0:T(2,128)S(1)} copy-done((s32[1,1,8,2]{2,3,1,0:T(2,128)S(1)}, s32[1,1,8,2]{2,3,1,0:T(2,128)}, u32[]{:S(2)}) %copy-start.1) | copy-done | bytes 88
  9.4 0.1 copy.5.shift_ref
  9.5 0.1 select_add_fusion.table_x
  9.6 0.0 copy-start
  9.6 0.0 collective-permute-done.1.refs_0_
  9.6 3.1 %collective-permute-done.2.refs_1_ = bf16[4,4,16,128]{3,2,1,0:T(8,128)(2,1)S(1)} collective-permute-done((bf16[4,4,16,128]{3,2,1,0:T(8,128)(2,1)S(1)}, bf16[4,4,16,128]{3,2,1,0:T(8,128)(2,1)S(1)}, u32[]{:S(2)}, u32[]{:S(2)}) %collective-permute-start.2) | collective-permute-done | bytes 65568 | tf_op jit(solution)/shard_map/ppermute | solution.py:450
  12.7 1.8 %collective-permute-done.3.refs_2_ = bf16[4,4,16,128]{3,2,1,0:T(8,128)(2,1)S(1)} collective-permute-done((bf16[4,4,16,128]{3,2,1,0:T(8,128)(2,1)S(1)}, bf16[4,4,16,128]{3,2,1,0:T(8,128)(2,1)S(1)}, u32[]{:S(2)}, u32[]{:S(2)}) %collective-permute-start.3) | collective-permute-done | bytes 65568 | tf_op jit(solution)/shard_map/ppermute | solution.py:450
  14.5 0.0 copy-done
  14.5 0.3 shard_map.47
  14.8 1.3 %collective-permute-start.5 = (bf16[2,16,256]{2,1,0:T(8,128)(2,1)S(1)}, bf16[2,16,256]{2,1,0:T(8,128)(2,1)S(1)}, u32[]{:S(2)}, u32[]{:S(2)}) collective-permute-start(bf16[2,16,256]{2,1,0:T(8,128)(2,1)S(1)} %get-tuple-element.21), channel_id=1, source_target_pairs={{0,4},{2,0},{4,8},{6,2},{8,12},{10,6},{12,14},{14,10},{1,5},{3,1},... | collective-permute-start | bytes 49160 | tf_op jit(solution)/shard_map/ppermute | solution.py:464
  16.1 0.8 %collective-permute-start.4 = (bf16[4,48,256]{2,1,0:T(8,128)(2,1)S(1)}, bf16[4,48,256]{2,1,0:T(8,128)(2,1)S(1)}, u32[]{:S(2)}, u32[]{:S(2)}) collective-permute-start(bf16[4,48,256]{2,1,0:T(8,128)(2,1)S(1)} %get-tuple-element.20), channel_id=1, source_target_pairs={{0,2},{2,0},{1,3},{3,1},{4,6},{6,4},{5,7},{7,5},{8,10},{10,8},{9,1... | collective-permute-start | bytes 294920 | tf_op jit(solution)/shard_map/ppermute | solution.py:463
  16.9 0.0 collective-permute-start.6
  16.9 1.9 %collective-permute-done.5.straight = bf16[2,16,256]{2,1,0:T(8,128)(2,1)S(1)} collective-permute-done((bf16[2,16,256]{2,1,0:T(8,128)(2,1)S(1)}, bf16[2,16,256]{2,1,0:T(8,128)(2,1)S(1)}, u32[]{:S(2)}, u32[]{:S(2)}) %collective-permute-start.5) | collective-permute-done | bytes 16416 | tf_op jit(solution)/shard_map/ppermute | solution.py:464
  18.8 0.0 collective-permute-start.11
  18.8 0.0 collective-permute-done.6.slant
  18.8 0.5 %collective-permute-start.9 = (bf16[4,64,256]{2,1,0:T(8,128)(2,1)S(1)}, bf16[4,64,256]{2,1,0:T(8,128)(2,1)S(1)}, u32[]{:S(2)}, u32[]{:S(2)}) collective-permute-start(bf16[4,64,256]{2,1,0:T(8,128)(2,1)S(1)} %get-tuple-element.19.warp_own), channel_id=1, source_target_pairs={{0,1},{1,0},{2,3},{3,2},{4,5},{5,4},{6,7},{7,6},{8,9},{9,8},{10,11... | collective-permute-start | bytes 393224 | tf_op jit(solution)/shard_map/ppermute | solution.py:467
  19.3 0.7 %collective-permute-done.11.straight_n = bf16[2,16,256]{2,1,0:T(8,128)(2,1)S(1)} collective-permute-done((bf16[2,16,256]{2,1,0:T(8,128)(2,1)S(1)}, bf16[2,16,256]{2,1,0:T(8,128)(2,1)S(1)}, u32[]{:S(2)}, u32[]{:S(2)}) %collective-permute-start.11) | collective-permute-done | bytes 16416 | tf_op jit(solution)/shard_map/ppermute | solution.py:469
  20.0 0.2 collective-permute-start.12
  20.2 0.0 collective-permute-done.fixed_got
  20.2 0.3 collective-permute-start.8
  20.5 0.2 collective-permute-done.4.warp_got
  20.8 0.0 collective-permute-start.10
  20.8 0.1 add_select_fusion.table_y
  20.8 0.3 collective-permute-done.12.slant_n
  21.2 0.0 collective-permute-done.7.fixed_own_n
  21.2 0.0 collective-permute-done.9.warp_own_n
  21.2 0.9 %collective-permute-done.10.warp_got_n = bf16[4,48,256]{2,1,0:T(8,128)(2,1)S(1)} collective-permute-done((bf16[4,48,256]{2,1,0:T(8,128)(2,1)S(1)}, bf16[4,48,256]{2,1,0:T(8,128)(2,1)S(1)}, u32[]{:S(2)}, u32[]{:S(2)}) %collective-permute-start.10) | collective-permute-done | bytes 98336 | tf_op jit(solution)/shard_map/ppermute | solution.py:468
  22.1 0.0 collective-permute-done.8.fixed_got_n
  22.1 5.3 %shard_map.48 = f32[3,8,16]{2,1,0:T(8,128)S(1)} custom-call(bf16[4,64,256]{2,1,0:T(8,128)(2,1)S(1)} %get-tuple-element.14.fixed_ref.fixed_own, bf16[4,64,256]{2,1,0:T(8,128)(2,1)S(1)} %collective-permute-done.fixed_got, bf16[4,64,256]{2,1,0:T(8,128)(2,1)S(1)} %get-tuple-element.19.warp_own, bf16[4,48,256]{2,1,0:T(8,128)(2,1)S(1)} %collective-permute-done.4.warp_got, ...), custom_call_target="tpu_custom_call" | custom-call | tf_op jit(solution)/shard_map/pallas_call | solution.py:406
  27.3 0.2 collective-permute-start.14
  27.5 3.7 %collective-permute-start.15 = (f32[3,8,16]{2,1,0:T(8,128)S(1)}, f32[3,8,16]{2,1,0:T(8,128)S(1)}, u32[]{:S(2)}, u32[]{:S(2)}) collective-permute-start(f32[3,8,16]{2,1,0:T(8,128)S(1)} %shard_map.48), channel_id=1, source_target_pairs={{4,0},{0,2},{8,4},{2,6},{12,8},{6,10},{14,12},{10,14},{5,1},{1,3},... | collective-permute-start | bytes 4616 | tf_op jit(solution)/shard_map/ppermute | solution.py:498
  31.2 0.9 %collective-permute-start.13 = (f32[3,8,16]{2,1,0:T(8,128)S(1)}, f32[3,8,16]{2,1,0:T(8,128)S(1)}, u32[]{:S(2)}, u32[]{:S(2)}) collective-permute-start(f32[3,8,16]{2,1,0:T(8,128)S(1)} %shard_map.48), channel_id=1, source_target_pairs={{0,2},{2,0},{1,3},{3,1},{4,6},{6,4},{5,7},{7,5},{8,10},{10,8},{9,1... | collective-permute-start | bytes 4616 | tf_op jit(solution)/shard_map/ppermute | solution.py:497
  32.1 0.0 collective-permute-done.14
  32.1 1.2 %collective-permute-done.15 = f32[3,8,16]{2,1,0:T(8,128)S(1)} collective-permute-done((f32[3,8,16]{2,1,0:T(8,128)S(1)}, f32[3,8,16]{2,1,0:T(8,128)S(1)}, u32[]{:S(2)}, u32[]{:S(2)}) %collective-permute-start.15) | collective-permute-done | bytes 1568 | tf_op jit(solution)/shard_map/ppermute | solution.py:498
  33.4 1.6 %collective-permute-done.13 = f32[3,8,16]{2,1,0:T(8,128)S(1)} collective-permute-done((f32[3,8,16]{2,1,0:T(8,128)S(1)}, f32[3,8,16]{2,1,0:T(8,128)S(1)}, u32[]{:S(2)}, u32[]{:S(2)}) %collective-permute-start.13) | collective-permute-done | bytes 1568 | tf_op jit(solution)/shard_map/ppermute | solution.py:497
  34.9 0.6 %fusion.1 = f32[3,1,4,16]{3,2,1,0:T(4,128)} fusion(f32[3,8,16]{2,1,0:T(8,128)S(1)} %collective-permute-done.13, f32[3,8,16]{2,1,0:T(8,128)S(1)} %shard_map.48, f32[3,2,16]{2,1,0:T(2,128)S(1)} %get-tuple-element.24, f32[3,2,16]{2,1,0:T(2,128)S(1)} %get-tuple-element.23), kind=kLoop, calls=%fused_computation.3 | loop fusion | flops 576 | bytes 3072 | tf_op jit(solution)/shard_map/broadcast_in_dim | solution.py:505
  (12 shorter events, 0.2 us)
Async XLA Ops:
  1.2 19.0 %collective-permute-start = (bf16[4,64,256]{2,1,0:T(8,128)(2,1)S(1)}, bf16[4,64,256]{2,1,0:T(8,128)(2,1)S(1)}, u32[]{:S(2)}, u32[]{:S(2)}) collective-permute-start(bf16[4,64,256]{2,1,0:T(8,128)(2,1)S(1)} %get-tuple-element.14.fixed_ref.fixed_own), channel_id=1, source_target_pairs={{0,2},{2,0},{1,3},{3,1},{4,6},{6,4},{5,7},{7,5},{8,10},{10,8},{9,1... | collective-permute-start | bytes 393224 | tf_op jit(solution)/shard_map/ppermute | solution.py:453
  4.2 17.0 %collective-permute-start.7 = (bf16[4,64,256]{2,1,0:T(8,128)(2,1)S(1)}, bf16[4,64,256]{2,1,0:T(8,128)(2,1)S(1)}, u32[]{:S(2)}, u32[]{:S(2)}) collective-permute-start(bf16[4,64,256]{2,1,0:T(8,128)(2,1)S(1)} %get-tuple-element.14.fixed_ref.fixed_own), channel_id=1, source_target_pairs={{0,1},{1,0},{2,3},{3,2},{4,5},{5,4},{6,7},{7,6},{8,9},{9,8},{10,11... | collective-permute-start | bytes 393224 | tf_op jit(solution)/shard_map/ppermute | solution.py:454
  4.2 5.4 %collective-permute-start.1 = (bf16[4,4,16,128]{3,2,1,0:T(8,128)(2,1)S(1)}, bf16[4,4,16,128]{3,2,1,0:T(8,128)(2,1)S(1)}, u32[]{:S(2)}, u32[]{:S(2)}) collective-permute-start(bf16[4,4,16,128]{3,2,1,0:T(8,128)(2,1)S(1)} %get-tuple-element.16), channel_id=1, source_target_pairs={{0,4},{4,0},{8,12},{12,8},{1,5},{5,1},{9,13},{13,9},{2,6},{6,2},{1... | collective-permute-start | bytes 196616 | tf_op jit(solution)/shard_map/ppermute | solution.py:450
  5.8 7.0 %collective-permute-start.2 = (bf16[4,4,16,128]{3,2,1,0:T(8,128)(2,1)S(1)}, bf16[4,4,16,128]{3,2,1,0:T(8,128)(2,1)S(1)}, u32[]{:S(2)}, u32[]{:S(2)}) collective-permute-start(bf16[4,4,16,128]{3,2,1,0:T(8,128)(2,1)S(1)} %get-tuple-element.17), channel_id=1, source_target_pairs={{0,8},{4,12},{8,0},{12,4},{1,9},{5,13},{9,1},{13,5},{2,10},{6,14},... | collective-permute-start | bytes 196616 | tf_op jit(solution)/shard_map/ppermute | solution.py:450
  8.4 6.1 %collective-permute-start.3 = (bf16[4,4,16,128]{3,2,1,0:T(8,128)(2,1)S(1)}, bf16[4,4,16,128]{3,2,1,0:T(8,128)(2,1)S(1)}, u32[]{:S(2)}, u32[]{:S(2)}) collective-permute-start(bf16[4,4,16,128]{3,2,1,0:T(8,128)(2,1)S(1)} %get-tuple-element.18), channel_id=1, source_target_pairs={{0,12},{4,8},{8,4},{12,0},{1,13},{5,9},{9,5},{13,1},{2,14},{6,10},... | collective-permute-start | bytes 196616 | tf_op jit(solution)/shard_map/ppermute | solution.py:450
  8.7 0.7 %copy-start.1 = (s32[1,1,8,2]{2,3,1,0:T(2,128)S(1)}, s32[1,1,8,2]{2,3,1,0:T(2,128)}, u32[]{:S(2)}) copy-start(s32[1,1,8,2]{2,3,1,0:T(2,128)} %param.7) | copy-start | bytes 196
  9.6 4.9 %copy-start = (s32[4,1,8,1]{2,3,1,0:T(1,128)S(1)}, s32[4,1,8,1]{2,3,1,0:T(1,128)}, u32[]{:S(2)}) copy-start(s32[4,1,8,1]{2,3,1,0:T(1,128)} %param.6) | copy-start | bytes 388
  14.8 4.0 %collective-permute-start.5 = (bf16[2,16,256]{2,1,0:T(8,128)(2,1)S(1)}, bf16[2,16,256]{2,1,0:T(8,128)(2,1)S(1)}, u32[]{:S(2)}, u32[]{:S(2)}) collective-permute-start(bf16[2,16,256]{2,1,0:T(8,128)(2,1)S(1)} %get-tuple-element.21), channel_id=1, source_target_pairs={{0,4},{2,0},{4,8},{6,2},{8,12},{10,6},{12,14},{14,10},{1,5},{3,1},... | collective-permute-start | bytes 49160 | tf_op jit(solution)/shard_map/ppermute | solution.py:464
  16.1 4.6 %collective-permute-start.4 = (bf16[4,48,256]{2,1,0:T(8,128)(2,1)S(1)}, bf16[4,48,256]{2,1,0:T(8,128)(2,1)S(1)}, u32[]{:S(2)}, u32[]{:S(2)}) collective-permute-start(bf16[4,48,256]{2,1,0:T(8,128)(2,1)S(1)} %get-tuple-element.20), channel_id=1, source_target_pairs={{0,2},{2,0},{1,3},{3,1},{4,6},{6,4},{5,7},{7,5},{8,10},{10,8},{9,1... | collective-permute-start | bytes 294920 | tf_op jit(solution)/shard_map/ppermute | solution.py:463
  16.9 1.9 %collective-permute-start.6 = (bf16[2,16,256]{2,1,0:T(8,128)(2,1)S(1)}, bf16[2,16,256]{2,1,0:T(8,128)(2,1)S(1)}, u32[]{:S(2)}, u32[]{:S(2)}) collective-permute-start(bf16[2,16,256]{2,1,0:T(8,128)(2,1)S(1)} %get-tuple-element.22), channel_id=1, source_target_pairs={{0,1},{2,4},{4,2},{6,8},{8,6},{10,12},{12,10},{14,15},{1,0},{3,5},... | collective-permute-start | bytes 49160 | tf_op jit(solution)/shard_map/ppermute | solution.py:465
  18.8 1.2 %collective-permute-start.11 = (bf16[2,16,256]{2,1,0:T(8,128)(2,1)S(1)}, bf16[2,16,256]{2,1,0:T(8,128)(2,1)S(1)}, u32[]{:S(2)}, u32[]{:S(2)}) collective-permute-start(bf16[2,16,256]{2,1,0:T(8,128)(2,1)S(1)} %collective-permute-done.5.straight), channel_id=1, source_target_pairs={{0,1},{1,0},{2,3},{3,2},{4,5},{5,4},{6,7},{7,6},{8,9},{9,8},{10,11... | collective-permute-start | bytes 49160 | tf_op jit(solution)/shard_map/ppermute | solution.py:469
  18.8 2.4 %collective-permute-start.9 = (bf16[4,64,256]{2,1,0:T(8,128)(2,1)S(1)}, bf16[4,64,256]{2,1,0:T(8,128)(2,1)S(1)}, u32[]{:S(2)}, u32[]{:S(2)}) collective-permute-start(bf16[4,64,256]{2,1,0:T(8,128)(2,1)S(1)} %get-tuple-element.19.warp_own), channel_id=1, source_target_pairs={{0,1},{1,0},{2,3},{3,2},{4,5},{5,4},{6,7},{7,6},{8,9},{9,8},{10,11... | collective-permute-start | bytes 393224 | tf_op jit(solution)/shard_map/ppermute | solution.py:467
  20.0 1.2 %collective-permute-start.12 = (bf16[2,16,256]{2,1,0:T(8,128)(2,1)S(1)}, bf16[2,16,256]{2,1,0:T(8,128)(2,1)S(1)}, u32[]{:S(2)}, u32[]{:S(2)}) collective-permute-start(bf16[2,16,256]{2,1,0:T(8,128)(2,1)S(1)} %collective-permute-done.6.slant), channel_id=1, source_target_pairs={{0,1},{1,0},{2,3},{3,2},{4,5},{5,4},{6,7},{7,6},{8,9},{9,8},{10,11... | collective-permute-start | bytes 49160 | tf_op jit(solution)/shard_map/ppermute | solution.py:470
  20.2 1.9 %collective-permute-start.8 = (bf16[4,64,256]{2,1,0:T(8,128)(2,1)S(1)}, bf16[4,64,256]{2,1,0:T(8,128)(2,1)S(1)}, u32[]{:S(2)}, u32[]{:S(2)}) collective-permute-start(bf16[4,64,256]{2,1,0:T(8,128)(2,1)S(1)} %collective-permute-done.fixed_got), channel_id=1, source_target_pairs={{0,1},{1,0},{2,3},{3,2},{4,5},{5,4},{6,7},{7,6},{8,9},{9,8},{10,11... | collective-permute-start | bytes 393224 | tf_op jit(solution)/shard_map/ppermute | solution.py:466
  20.8 1.3 %collective-permute-start.10 = (bf16[4,48,256]{2,1,0:T(8,128)(2,1)S(1)}, bf16[4,48,256]{2,1,0:T(8,128)(2,1)S(1)}, u32[]{:S(2)}, u32[]{:S(2)}) collective-permute-start(bf16[4,48,256]{2,1,0:T(8,128)(2,1)S(1)} %collective-permute-done.4.warp_got), channel_id=1, source_target_pairs={{0,1},{1,0},{2,3},{3,2},{4,5},{5,4},{6,7},{7,6},{8,9},{9,8},{10,11... | collective-permute-start | bytes 294920 | tf_op jit(solution)/shard_map/ppermute | solution.py:468
  27.3 4.8 %collective-permute-start.14 = (f32[3,8,16]{2,1,0:T(8,128)S(1)}, f32[3,8,16]{2,1,0:T(8,128)S(1)}, u32[]{:S(2)}, u32[]{:S(2)}) collective-permute-start(f32[3,8,16]{2,1,0:T(8,128)S(1)} %shard_map.48), channel_id=1, source_target_pairs={{0,1},{2,4},{4,2},{6,8},{8,6},{10,12},{12,10},{14,15},{1,0},{3,5},... | collective-permute-start | bytes 4616 | tf_op jit(solution)/shard_map/ppermute | solution.py:499
  27.5 5.8 %collective-permute-start.15 = (f32[3,8,16]{2,1,0:T(8,128)S(1)}, f32[3,8,16]{2,1,0:T(8,128)S(1)}, u32[]{:S(2)}, u32[]{:S(2)}) collective-permute-start(f32[3,8,16]{2,1,0:T(8,128)S(1)} %shard_map.48), channel_id=1, source_target_pairs={{4,0},{0,2},{8,4},{2,6},{12,8},{6,10},{14,12},{10,14},{5,1},{1,3},... | collective-permute-start | bytes 4616 | tf_op jit(solution)/shard_map/ppermute | solution.py:498
  31.2 3.7 %collective-permute-start.13 = (f32[3,8,16]{2,1,0:T(8,128)S(1)}, f32[3,8,16]{2,1,0:T(8,128)S(1)}, u32[]{:S(2)}, u32[]{:S(2)}) collective-permute-start(f32[3,8,16]{2,1,0:T(8,128)S(1)} %shard_map.48), channel_id=1, source_target_pairs={{0,2},{2,0},{1,3},{3,1},{4,6},{6,4},{5,7},{7,5},{8,10},{10,8},{9,1... | collective-permute-start | bytes 4616 | tf_op jit(solution)/shard_map/ppermute | solution.py:497

commit v4 on v0

--- a/solution.py
+++ b/solution.py
@@ -1,16 +1,20 @@
+import functools
+
 import jax
 import jax.numpy as jnp
 from jax import lax
+from jax.experimental import pallas as pl
+from jax.experimental.pallas import tpu as pltpu
 from jax.sharding import PartitionSpec as P
 
 BLK_Y = 16
 BLK_X = 128
 RAD = 2
 SPACING = 16
+MAX_NAMED = 4
 
 
 den_floor = 1e-05
-
 
 def with_halo(array, sides, width):
     for axis, dim in sides:
@@ -176,9 +180,394 @@
     return lax.psum(owned_grad, "gz")
 
 
+EDGE = 2 * RAD
+SEND_ROWS = 48
+KERNEL_BYTES = 24 << 20
+
+
+def pack_kernel(tiles, source_ref, source_in, moving_ref, fixed_ref, *out_refs):
+    *packs, source_out, moving_out, fixed_out, send_out = out_refs
+    source_out[...] = source_in[...]
+    moving_out[...] = moving_ref[...]
+    fixed_out[...] = fixed_ref[...]
+    me = lax.axis_index("tile")
+    half = lax.rem(me + lax.axis_index("gz"), 2)
+    start = pl.multiple_of((1 - half) * BLK_Y, BLK_Y)
+    send_out[...] = fixed_ref[:, pl.ds(start, SEND_ROWS), :]
+    height, width = moving_ref.shape[1:]
+    xblocks = width // BLK_X
+    blocks = (height // BLK_Y) * xblocks
+    cap = packs[0].shape[0]
+    for step in range(1, tiles):
+        other = lax.bitwise_xor(me, step)
+        count = jnp.int32(0)
+        chosen = [jnp.int32(0)] * cap
+        for block in range(blocks):
+            named = source_ref[other, block] == me
+            chosen = [jnp.where(named & (count == slot), block, old) for slot, old in enumerate(chosen)]
+            count = count + named.astype(jnp.int32)
+        for slot, block in enumerate(chosen):
+            row = pl.multiple_of(block // xblocks * BLK_Y, BLK_Y)
+            col = pl.multiple_of(lax.rem(block, xblocks) * BLK_X, BLK_X)
+            packs[step - 1][slot] = moving_ref[:, pl.ds(row, BLK_Y), pl.ds(col, BLK_X)]
+
+
+def unpack_kernel(tiles, source_ref, shift_ref, moving_ref, *refs):
+    recvs = refs[: tiles - 1]
+    own_ref, send_ref = refs[tiles - 1 :]
+    me = lax.axis_index("tile")
+    half = lax.rem(me + lax.axis_index("gz"), 2)
+    height, width = moving_ref.shape[1:]
+    xblocks = width // BLK_X
+    blocks = (height // BLK_Y) * xblocks
+    cap = recvs[0].shape[0]
+    for block in range(blocks):
+        row, col = (block // xblocks) * BLK_Y, (block % xblocks) * BLK_X
+        source = source_ref[me, block]
+        slot = jnp.int32(0)
+        for earlier in range(block):
+            slot = slot + (source_ref[me, earlier] == source).astype(jnp.int32)
+        slot = jnp.minimum(slot, cap - 1)
+        step = lax.bitwise_xor(source, me)
+        value = moving_ref[:, row : row + BLK_Y, col : col + BLK_X].astype(jnp.float32)
+        for other in range(1, tiles):
+            value = jnp.where(step == other, recvs[other - 1][slot].astype(jnp.float32), value)
+        down = lax.rem(shift_ref[block, 0], BLK_Y)
+        right = lax.rem(shift_ref[block, 1], BLK_X)
+        value = pltpu.roll(value, right, 2)
+        for bit in (1, 2, 4, 8):
+            value = jnp.where(lax.bitwise_and(down, bit) != 0, pltpu.roll(value, bit, 1), value)
+        own_ref[:, row : row + BLK_Y, col : col + BLK_X] = value.astype(own_ref.dtype)
+    start = pl.multiple_of((1 - half) * BLK_Y, BLK_Y)
+    send_ref[...] = own_ref[:, pl.ds(start, SEND_ROWS), :]
+
+
+def side_kernel(own_ref, got_ref, *refs):
+    out_ref = refs[-1]
+    group = lax.axis_index("gz")
+    half = lax.rem(lax.axis_index("tile") + group, 2)
+    depth = own_ref.shape[0]
+    col = pl.multiple_of((1 - lax.axis_index("rep")) * BLK_X, BLK_X)
+    start = pl.multiple_of(half * BLK_Y, BLK_Y)
+    for i in range(depth):
+        out_ref[group * depth + i] = own_ref[i, pl.ds(start, SEND_ROWS), pl.ds(col, BLK_X)]
+        out_ref[(1 - group) * depth + i] = got_ref[i, :, pl.ds(col, BLK_X)]
+
+
+def five(array, axis):
+    size = array.shape[axis]
+    pair = array + pltpu.roll(array, 1, axis)
+    return pltpu.roll(pair, size - 2, axis) + pair + pltpu.roll(array, 2, axis)
+
+
+def lane_limits(side, width, span):
+    return jnp.where(side == 0, 0, BLK_X - 48), jnp.where(side == 0, width + 32, span)
+
+
+def assemble(own, got, near_in, image):
+    group, side = lax.axis_index("gz"), lax.axis_index("rep")
+    half = lax.rem(lax.axis_index("tile") + group, 2)
+    depth, _, width = own.shape
+    window, span = image.shape[1:]
+    own_col = pl.multiple_of(side * BLK_X, BLK_X)
+    new_col = pl.multiple_of((1 - side) * width, BLK_X)
+    start = pl.multiple_of(half * BLK_Y, BLK_Y)
+    low, high = lane_limits(side, width, span)
+    lanes = lax.broadcasted_iota(jnp.int32, (window, BLK_X), 1) + new_col
+    levels = lax.broadcasted_iota(jnp.int32, (window, BLK_X), 0)
+    inner = (levels >= jnp.where(half == 0, EDGE, 0)) & (levels < jnp.where(half == 0, window, window - EDGE))
+    near = inner & (lanes >= low) & (lanes < high)
+    turn = jnp.where(half == 0, EDGE, SEND_ROWS - BLK_Y + EDGE)
+
+    def shift_in(piece):
+        return pltpu.roll(piece.astype(jnp.float32), turn, 0)[:window]
+
+    for i in range(depth):
+        mine, theirs = group * depth + i, (1 - group) * depth + i
+        for plane, piece in ((mine, own[i, pl.ds(start, SEND_ROWS), :]), (theirs, got[i])):
+            piece = shift_in(piece)
+            for part in range(width // BLK_X):
+                col = pl.multiple_of(own_col + part * BLK_X, BLK_X)
+                value = piece[:, part * BLK_X : (part + 1) * BLK_X]
+                image[plane, :, pl.ds(col, BLK_X)] = jnp.where(inner, value, 0.0)
+        for plane in (mine, theirs):
+            image[plane, :, pl.ds(new_col, BLK_X)] = jnp.where(near, shift_in(near_in[plane]), 0.0)
+
+
+def fill_band(band):
+    span = band.shape[0]
+    across = lax.broadcasted_iota(jnp.int32, (span, span), 0) - lax.broadcasted_iota(jnp.int32, (span, span), 1)
+    band[...] = jnp.where(jnp.abs(across) <= RAD, 1.0, 0.0).astype(band.dtype)
+
+
+def lane_sums(exact, products, band):
+    rows = (exact + products)[0].shape[0]
+    low = [value - value.astype(jnp.bfloat16).astype(jnp.float32) for value in products]
+    boxed = jnp.dot(
+        jnp.concatenate(exact + products + low, axis=0).astype(jnp.bfloat16), band[...],
+        preferred_element_type=jnp.float32,
+    )
+    pieces = [boxed[k * rows : (k + 1) * rows] for k in range(len(exact) + 2 * len(products))]
+    first = len(exact)
+    return pieces[:first] + [
+        pieces[first + k] + pieces[first + len(products) + k] for k in range(len(products))
+    ]
+
+
+def near_planes(z, planes):
+    return range(max(0, z - RAD), min(planes, z + RAD + 1))
+
+
+def total(values):
+    values = list(values)
+    result = values[0]
+    for value in values[1:]:
+        result = result + value
+    return result
+
+
+def sum_planes(rows, boxes):
+    for which in range(boxes.shape[0]):
+        for z in range(boxes.shape[1]):
+            boxes[which, z] = total(rows[which, k] for k in near_planes(z, boxes.shape[1]))
+
+
+def fixed_kernel(own, got, near_in, image, boxes, band, rows):
+    assemble(own, got, near_in, image)
+    fill_band(band)
+    for z in range(image.shape[0]):
+        f = image[z]
+        for which, value in enumerate(lane_sums([f], [f * f], band)):
+            rows[which, z] = five(value, 0)
+    sum_planes(rows, boxes)
+
+
+def warped_kernel(own, got, near_in, fixed, image, rims):
+    assemble(own, got, near_in, image)
+    half = lax.rem(lax.axis_index("tile") + lax.axis_index("gz"), 2)
+    planes, window, span = image.shape
+    upper = lax.broadcasted_iota(jnp.int32, (2 * EDGE, span), 0) < EDGE
+    for which, source in enumerate((fixed, image)):
+        tiles = []
+        for z in range(0, planes, 2):
+            low, high = source.at[z], source.at[z + 1]
+            top = jnp.where(upper, pltpu.roll(low[: 2 * EDGE], EDGE, 0), high[: 2 * EDGE])
+            end = jnp.where(upper, low[window - 2 * EDGE :], pltpu.roll(high[window - 2 * EDGE :], EDGE, 0))
+            tiles.append(jnp.where(half == 0, top, end))
+        rims[which] = jnp.concatenate(tiles, axis=0).astype(rims.dtype)
+
+
+def cross_kernel(fixed, warped, band, boxes, rows):
+    for z in range(fixed.shape[0]):
+        f, w = fixed[z], warped[z]
+        for which, value in enumerate(lane_sums([w], [w * w, f * w], band)):
+            rows[which, z] = five(value, 0)
+    sum_planes(rows, boxes)
+
+
+def main_kernel(
+    tiles, fixed, warped, fixed_boxes, warped_boxes, rims, band, table_y, table_x,
+    out_ref, images, edges, terms, sums,
+):
+    side, me = lax.axis_index("rep"), lax.axis_index("tile")
+    half = lax.rem(me + lax.axis_index("gz"), 2)
+    first = jnp.where(half == 0, (me == 0).astype(jnp.int32), 0)
+    last = jnp.where(half == 1, (me == tiles - 1).astype(jnp.int32), 0)
+    planes, window, span = fixed.shape
+    tile = 2 * EDGE
+    lanes = lax.broadcasted_iota(jnp.int32, (window, span), 1)
+    levels = lax.broadcasted_iota(jnp.int32, (window, span), 0)
+    low_lane, high_lane = lane_limits(side, span - BLK_X, span)
+    low_row = jnp.where(first != 0, EDGE, RAD)
+    high_row = jnp.where(last != 0, window - EDGE, window - RAD)
+    inside = (lanes >= low_lane) & (lanes < high_lane) & (levels >= low_row) & (levels < high_row)
+
+    outer = (first + last) != 0
+    rim_f = jnp.where(outer, 0.0, rims[0].astype(jnp.float32))
+    rim_w = jnp.where(outer, 0.0, rims[1].astype(jnp.float32))
+    rim_sums = lane_sums([rim_f, rim_w], [rim_f * rim_f, rim_w * rim_w, rim_f * rim_w], band)
+    at = lax.broadcasted_iota(jnp.int32, (tile, span), 0)
+    upper = at < EDGE
+    on_top, on_end = jnp.where(half == 0, 1.0, 0.0), jnp.where(half == 0, 0.0, 1.0)
+    held = (at >= jnp.where(half == 0, 0, EDGE)) & (at < jnp.where(half == 0, EDGE, tile))
+    reach = (at >= jnp.where(half == 0, 0, RAD)) & (at < jnp.where(half == 0, tile - RAD, tile))
+
+    def rim_tile(rim, z):
+        pair = rim[z // 2 * tile : (z // 2 + 1) * tile]
+        other = pltpu.roll(pair, EDGE, 0)
+        both = jnp.where(upper, pair, other) if z % 2 == 0 else jnp.where(upper, other, pair)
+        return jnp.where(held, both, 0.0)
+
+    def with_tile(value, extra):
+        return jnp.concatenate(
+            [value[:tile] + extra * on_top, value[tile : window - tile], value[window - tile :] + extra * on_end],
+            axis=0,
+        )
+
+    for which in range(5):
+        for z in range(planes):
+            edges[which, z] = jnp.where(reach, five(rim_tile(rim_sums[which], z), 0), 0.0)
+    for z in range(planes):
+        images[z] = with_tile(warped[z], rim_tile(rim_w, z))
+
+    volume = float((2 * RAD + 1) ** 3)
+    sources = (fixed_boxes, 0), (warped_boxes, 0), (fixed_boxes, 1), (warped_boxes, 1), (warped_boxes, 2)
+    for z in range(planes):
+        sum_f, sum_w, sum_ff, sum_ww, sum_fw = (
+            with_tile(source[index, z], total(edges[which, k] for k in near_planes(z, planes)))
+            for which, (source, index) in enumerate(sources)
+        )
+        cross = sum_fw - sum_f * sum_w * (1.0 / volume)
+        var_f = sum_ff - sum_f * sum_f * (1.0 / volume)
+        var_w = sum_ww - sum_w * sum_w * (1.0 / volume)
+        inverse = 1.0 / (var_f * var_w + den_floor)
+        ratio = cross * inverse
+        term_a = 2.0 * ratio
+        term_b = -(ratio * ratio) * var_f
+        term_c = -(term_a * sum_f + 2.0 * term_b * sum_w) * (1.0 / volume)
+        values = [five(jnp.where(inside, value, 0.0), 0) for value in (term_a, term_b, term_c)]
+        for which, value in enumerate(lane_sums([], values, band)):
+            terms[which, z] = value
+
+    for d in range(3):
+        sums[d] = jnp.zeros((window, span), jnp.float32)
+    owned = (levels >= EDGE) & (levels < window - EDGE)
+    for z in range(planes):
+        box_a, box_b, box_c = (total(terms[which, k] for k in near_planes(z, planes)) for which in range(3))
+        f, w = fixed[z], images[z]
+        gain = -(f * box_a + 2.0 * w * box_b + box_c)
+        u = z / SPACING
+        weight = (3.0 * u * u * u - 6.0 * u * u + 4.0) * (0.5 / 6.0)
+        gain = jnp.where(owned, gain, 0.0) * weight
+        ahead = images[z + 1] if z + 1 < planes else 0.0
+        behind = images[z - 1] if z > 0 else 0.0
+        sums[0] += gain * (ahead - behind)
+        sums[1] += gain * (pltpu.roll(w, window - 1, 0) - pltpu.roll(w, 1, 0))
+        sums[2] += gain * (pltpu.roll(w, span - 1, 1) - pltpu.roll(w, 1, 1))
+
+    for d in range(3):
+        along_x = lax.dot_general(
+            sums[d], table_x[...], (((1,), (1,)), ((), ())),
+            precision=lax.Precision.HIGHEST, preferred_element_type=jnp.float32,
+        )
+        out_ref[d] = lax.dot_general(
+            table_y[...], along_x, (((1,), (0,)), ((), ())),
+            precision=lax.Precision.HIGHEST, preferred_element_type=jnp.float32,
+        )
+
+
+def local_kernel(kernel, outs, arrays, scratch=()):
+    vmem = pl.BlockSpec(memory_space=pltpu.VMEM)
+    return pl.pallas_call(
+        kernel,
+        out_shape=[pltpu.VMEM(shape, dtype) for shape, dtype in outs],
+        in_specs=[vmem] * len(arrays),
+        out_specs=[vmem] * len(outs),
+        scratch_shapes=list(scratch),
+        compiler_params=pltpu.CompilerParams(vmem_limit_bytes=KERNEL_BYTES),
+    )(*(pltpu.with_memory_space_constraint(array, pltpu.VMEM) for array in arrays))
+
+
+def fast_body(tiles, fixed_image, moving_image, source_tile, block_shifts):
+    depth, height, width = fixed_image.shape
+    me, group, side = lax.axis_index("tile"), lax.axis_index("gz"), lax.axis_index("rep")
+    half = lax.rem(me + group, 2)
+    sources = source_tile[:, 0, :, 0]
+    shifts = block_shifts[0, 0]
+    cap = MAX_NAMED if tiles == 4 else sources.shape[1]
+    planes = 2 * depth
+    window, span = height // 2 + 2 * EDGE, width + BLK_X
+    short, full = jnp.bfloat16, jnp.float32
+    whole, send_shape = (fixed_image.shape, short), ((depth, SEND_ROWS, width), short)
+    side_shape = ((planes, SEND_ROWS, BLK_X), short)
+    image_shape = ((planes, window, span), full)
+    smem, vmem = (pl.BlockSpec(memory_space=space) for space in (pltpu.SMEM, pltpu.VMEM))
+    outs = [((cap, depth, BLK_Y, BLK_X), short)] * (tiles - 1) + [(sources.shape, jnp.int32), whole, whole, send_shape]
+    *packs, sources, moving_image, fixed_image, fixed_send = pl.pallas_call(
+        functools.partial(pack_kernel, tiles),
+        out_shape=[pltpu.VMEM(*out) for out in outs],
+        in_specs=[smem, vmem, vmem, vmem],
+        out_specs=[vmem] * len(outs),
+    )(sources, sources, moving_image, fixed_image)
+
+    trio = ("tile", "gz", "rep")
+
+    def number(t, g, r):
+        return (t * 2 + g) * 2 + r
+
+    swap = [(0, 1), (1, 0)]
+    straight, slant = [], []
+    for r in range(2):
+        for t in range(tiles):
+            for g in range(2):
+                to = t - 1 if (g + t) % 2 == 0 else t + 1
+                there = 0 <= to < tiles
+                straight.append((number(t, g, r), number(to, g, r) if there else number(t, g, 1 - r)))
+                slant.append((number(t, g, r), number(to if there else t, 1 - g, r)))
+
+    got = [
+        lax.ppermute(pack, "tile", [(t, t ^ step) for t in range(tiles)])
+        for step, pack in zip(range(1, tiles), packs)
+    ]
+    fixed_got = lax.ppermute(fixed_send, "gz", swap)
+    own, send = local_kernel(
+        functools.partial(unpack_kernel, tiles), [whole, send_shape], [sources, shifts, moving_image, *got]
+    )
+    warp_got = lax.ppermute(send, "gz", swap)
+    (fixed_side,) = local_kernel(side_kernel, [side_shape], [fixed_image, fixed_got])
+    fixed_near = lax.ppermute(fixed_side, "rep", swap)
+    boxes = [(count, planes, window, span) for count in (2, 3)]
+    fixed, fixed_boxes, band = local_kernel(
+        fixed_kernel,
+        [image_shape, (boxes[0], full), ((span, span), short)],
+        [fixed_image, fixed_got, fixed_near],
+        [pltpu.VMEM(boxes[0], full)],
+    )
+    (warp_side,) = local_kernel(side_kernel, [side_shape], [own, warp_got, fixed])
+    warp_near = lax.ppermute(warp_side, "rep", swap)
+    warped, rims = local_kernel(
+        warped_kernel,
+        [image_shape, ((2, planes * EDGE, span), short)],
+        [own, warp_got, warp_near, fixed],
+    )
+    rims = lax.ppermute(rims, trio, straight)
+    (warped_boxes,) = local_kernel(
+        cross_kernel, [(boxes[1], full)], [fixed, warped, band], [pltpu.VMEM(boxes[1], full)]
+    )
+
+    row_knots, col_knots = height // SPACING, width // SPACING
+    row_at = jnp.arange(window, dtype=jnp.int32)
+    table_y = spline_table(half * (height // 2) - EDGE, window, -2, row_knots + 4)
+    table_y = jnp.where(((row_at >= EDGE) & (row_at < window - EDGE))[:, None], table_y, 0.0).T
+    table_x = spline_table(side * BLK_X, span, side * col_knots, col_knots).T
+    (part,) = local_kernel(
+        functools.partial(main_kernel, tiles),
+        [((3, row_knots + 4, col_knots), full)],
+        [fixed, warped, fixed_boxes, warped_boxes, rims, band, table_y, table_x],
+        [
+            pltpu.VMEM((planes, window, span), full),
+            pltpu.VMEM((5, planes, 2 * EDGE, span), full),
+            pltpu.VMEM((3, planes, window, span), full),
+            pltpu.VMEM((3, window, span), full),
+        ],
+    )
+    across = lax.ppermute(part, "gz", swap)
+    part_slant = lax.ppermute(part, trio, slant)
+    part_straight = lax.ppermute(part, trio, straight)
+    below = jnp.where(half == 0, part_slant, part_straight)
+    above = jnp.where(half == 0, part_straight, part_slant)
+    below = jnp.where(me == tiles - 1, 0.0, below[:, :2])
+    above = jnp.where(me == 0, 0.0, above[:, row_knots + 2 :])
+    middle = part[:, 2 : row_knots + 2] + across[:, 2 : row_knots + 2]
+    return (middle + jnp.concatenate([above, below], axis=1))[:, None]
+
+
 def solution(mesh):
+    sizes = mesh.shape
+    tiles = sizes["tile"]
+    fast = sizes["gz"] == 2 and sizes["rep"] == 2 and tiles & (tiles - 1) == 0 and tiles > 1
     return jax.shard_map(
-        body,
+        functools.partial(fast_body, tiles) if fast else body,
         mesh=mesh,
         in_specs=(
             P(("slab", "gz"), "tile", "rep"),

time: 111 us -> 33.4 us (0.30)
  starting transfers between devices: 42.9 us -> 13.6 us
  blocking collectives: 23.4 us -> 0 us
  local copies, waits for them, and re-layouts: 13.3 us -> 0.76 us
  other arithmetic: 8.79 us -> 0.91 us
  Pallas kernels: 0 us -> 7.59 us
  between operations: 5.84 us -> 0.14 us
  waiting for transfers between devices: 13.4 us -> 10.2 us
  matrix products: 2.18 us -> 0 us
    ppermute x16 -> x11, starting transfers between devices: 42.9 us -> 13.6 us  [the longest x3 5.68 us: fast_body(): lax.ppermute(pack, 'tile', [(t, t ^ step) for t in range(tiles)])]
    all_gather x1 -> x0, blocking collectives: 17.4 us -> none  [body(): piece = lax.all_gather(moving_image, 'tile', axis=1, tiled=True)]
    pallas_call x0 -> x8, Pallas kernels: none -> 7.59 us  [the longest x7 6.39 us: local_kernel(): pl.pallas_call(kernel, out_shape=[pltpu.VMEM(shape, dtype) for shape, dty...]
    gather x10 -> x0, local copies, waits for them, and re-layouts: 7.16 us -> none  [the longest x8 4.71 us: body(): taken = jnp.take(columns_part, jnp.clip(wanted, 0, length - 1), axis=1)]
    psum x1 -> x0, blocking collectives: 6.01 us -> none  [body(): return lax.psum(owned_grad, 'gz')]
    ppermute x16 -> x11, waiting for transfers between devices: 13.4 us -> 10.2 us  [the longest x3 3.34 us: fast_body(): lax.ppermute(pack, 'tile', [(t, t ^ step) for t in range(tiles)])]
    another operation x6 -> x0, other arithmetic: 3.08 us -> none  [the longest x3 1.6 us: body(): jnp.stack((term_a, term_b, term_c)).astype(jnp.bfloat16)]
    dot_general x3 -> x0, matrix products: 2.18 us -> none  [the longest x1 1.05 us: contract(): along_x = jnp.einsum('czyx,xk->czyk', pieces, table_x, precision=highest)]
  transfers between devices with their start and end apart: 16 -> 11, of which waited for: 10 -> 7; matrix products, arithmetic and copies ran while one was open for 0% -> 3% of each run, Pallas kernels for 0% -> 8%
where the time goes in v4:
time: 33.4 us; the launch traced here: 33.2 us
  starting transfers between devices  13.6 us (41%)
  waiting for transfers between devices  10.2 us (31%)
  Pallas kernels  7.59 us (23%)
  other arithmetic  0.91 us (3%)
  local copies, waits for them, and re-layouts  0.76 us (2%)
    pallas_call x7, Pallas kernels, local_kernel(): pl.pallas_call(kernel, out_shape=[pltpu.VMEM(shape, dtype) for shape, dty...  6.39 us
    ppermute x3, starting transfers between devices, fast_body(): lax.ppermute(pack, 'tile', [(t, t ^ step) for t in range(tiles)])  5.68 us
    ppermute x1, starting transfers between devices, fast_body(): part_slant = lax.ppermute(part, trio, slant)  4.23 us
    ppermute x3, waiting for transfers between devices, fast_body(): lax.ppermute(pack, 'tile', [(t, t ^ step) for t in range(tiles)])  3.34 us
    ppermute x1, waiting for transfers between devices, fast_body(): across = lax.ppermute(part, 'gz', swap)  2.28 us
    ppermute x1, starting transfers between devices, fast_body(): fixed_got = lax.ppermute(fixed_send, 'gz', swap)  1.71 us
    ppermute x1, starting transfers between devices, fast_body(): warp_got = lax.ppermute(send, 'gz', swap)  1.56 us
    ppermute x1, waiting for transfers between devices, fast_body(): part_slant = lax.ppermute(part, trio, slant)  1.3 us
  transfers between devices with their start and end apart: 11, of which 7 were waited for; matrix products, arithmetic and copies ran while one was open for 3% of the time, Pallas kernels for 8%

profile of v4, /device:TPU:0, one launch (start us, length us, event | category | flops | bytes accessed | tf_op | source)
XLA Modules:
  0.0 33.2 jit_solution(18077670325428191862)
XLA Ops:
  0.0 1.2 %shard_map.46 = (bf16[4,4,16,128]{3,2,1,0:T(8,128)(2,1)S(1)}, bf16[4,4,16,128]{3,2,1,0:T(8,128)(2,1)S(1)}, bf16[4,4,16,128]{3,2,1,0:T(8,128)(2,1)S(1)}, s32[4,8]...) custom-call(s32[4,8]{1,0:T(4,128)} %bitcast.6, ...), custom_call_target="tpu_custom_call" | custom-call | tf_op jit(solution)/shard_map/pallas_call | solution.py:486
  1.2 3.1 %collective-permute-start.2 = (bf16[4,4,16,128]{3,2,1,0:T(8,128)(2,1)S(1)}, bf16[4,4,16,128]{3,2,1,0:T(8,128)(2,1)S(1)}, u32[]{:S(2)}, u32[]{:S(2)}) collective-permute-start(bf16[4,4,16,128]{3,2,1,0:T(8,128)(2,1)S(1)} %get-tuple-element.24), channel_id=1, source_target_pairs={{0,4},{4,0},{8,12},{12,8},{1,5},{5,1},{9,13},{13,9},{2,6},{6,2},{1... | collective-permute-start | bytes 196616 | tf_op jit(solution)/shard_map/ppermute | solution.py:509
  4.3 2.6 %collective-permute-start.3 = (bf16[4,4,16,128]{3,2,1,0:T(8,128)(2,1)S(1)}, bf16[4,4,16,128]{3,2,1,0:T(8,128)(2,1)S(1)}, u32[]{:S(2)}, u32[]{:S(2)}) collective-permute-start(bf16[4,4,16,128]{3,2,1,0:T(8,128)(2,1)S(1)} %get-tuple-element.25), channel_id=1, source_target_pairs={{0,8},{4,12},{8,0},{12,4},{1,9},{5,13},{9,1},{13,5},{2,10},{6,14},... | collective-permute-start | bytes 196616 | tf_op jit(solution)/shard_map/ppermute | solution.py:509
  6.9 0.0 collective-permute-start.4
  6.9 1.7 %collective-permute-start = (bf16[4,48,256]{2,1,0:T(8,128)(2,1)S(1)}, bf16[4,48,256]{2,1,0:T(8,128)(2,1)S(1)}, u32[]{:S(2)}, u32[]{:S(2)}) collective-permute-start(bf16[4,48,256]{2,1,0:T(8,128)(2,1)S(1)} %get-tuple-element.20), channel_id=1, source_target_pairs={{0,2},{2,0},{1,3},{3,1},{4,6},{6,4},{5,7},{7,5},{8,10},{10,8},{9,1... | collective-permute-start | bytes 294920 | tf_op jit(solution)/shard_map/ppermute | solution.py:512
  8.7 0.8 %copy.5.shift_ref = s32[8,2]{1,0:T(8,128)S(1)} copy(s32[8,2]{0,1:T(2,128)} %bitcast.8) | data formatting | bytes 128 | tf_op jit(solution)/shard_map/squeeze | solution.py:476
  9.5 0.1 select_add_fusion.table_x
  9.6 0.0 collective-permute-done.2.refs_0_
  9.6 1.9 %collective-permute-done.3.refs_1_ = bf16[4,4,16,128]{3,2,1,0:T(8,128)(2,1)S(1)} collective-permute-done((bf16[4,4,16,128]{3,2,1,0:T(8,128)(2,1)S(1)}, bf16[4,4,16,128]{3,2,1,0:T(8,128)(2,1)S(1)}, u32[]{:S(2)}, u32[]{:S(2)}) %collective-permute-start.3) | collective-permute-done | bytes 65568 | tf_op jit(solution)/shard_map/ppermute | solution.py:509
  11.6 1.4 %collective-permute-done.4.refs_2_ = bf16[4,4,16,128]{3,2,1,0:T(8,128)(2,1)S(1)} collective-permute-done((bf16[4,4,16,128]{3,2,1,0:T(8,128)(2,1)S(1)}, bf16[4,4,16,128]{3,2,1,0:T(8,128)(2,1)S(1)}, u32[]{:S(2)}, u32[]{:S(2)}) %collective-permute-start.4) | collective-permute-done | bytes 65568 | tf_op jit(solution)/shard_map/ppermute | solution.py:509
  13.0 0.4 %shard_map.49 = (bf16[4,64,256]{2,1,0:T(8,128)(2,1)S(1)}, bf16[4,48,256]{2,1,0:T(8,128)(2,1)S(1)}) custom-call(s32[4,8]{1,0:T(4,128)S(1)} %get-tuple-element.22.source_ref, s32[8,2]{1,0:T(8,128)S(1)} %copy.5.shift_ref, bf16[4,64,256]{2,1,0:T(8,128)(2,1)S(1)} %get-tuple-element.23.moving_ref, bf16[4,4,16,128]{3,2,1,0:T(8,128)(2,1)S(1)} %collective-permute-done.2.refs_0_, ...), custom_call_target="tpu_custom_call" | custom-call | tf_op jit(solution)/shard_map/pallas_call | solution.py:461
  13.3 1.6 %collective-permute-start.5 = (bf16[4,48,256]{2,1,0:T(8,128)(2,1)S(1)}, bf16[4,48,256]{2,1,0:T(8,128)(2,1)S(1)}, u32[]{:S(2)}, u32[]{:S(2)}) collective-permute-start(bf16[4,48,256]{2,1,0:T(8,128)(2,1)S(1)} %get-tuple-element.28), channel_id=1, source_target_pairs={{0,2},{2,0},{1,3},{3,1},{4,6},{6,4},{5,7},{7,5},{8,10},{10,8},{9,1... | collective-permute-start | bytes 294920 | tf_op jit(solution)/shard_map/ppermute | solution.py:516
  14.9 0.0 collective-permute-done.got_ref.got
  14.9 0.1 collective-permute-start.1
  15.0 1.3 %collective-permute-done.1.near_in = bf16[8,48,128]{2,1,0:T(8,128)(2,1)S(1)} collective-permute-done((bf16[8,48,128]{2,1,0:T(8,128)(2,1)S(1)}, bf16[8,48,128]{2,1,0:T(8,128)(2,1)S(1)}, u32[]{:S(2)}, u32[]{:S(2)}) %collective-permute-start.1) | collective-permute-done | bytes 98336 | tf_op jit(solution)/shard_map/ppermute | solution.py:518
  16.3 1.0 %shard_map.48 = (f32[8,40,384]{2,1,0:T(8,128)S(1)}, f32[2,8,40,384]{3,2,1,0:T(8,128)S(1)}, bf16[384,384]{1,0:T(8,128)(2,1)S(1)}) custom-call(bf16[4,64,256]{2,1,0:T(8,128)(2,1)S(1)} %get-tuple-element.19.own_ref.own, bf16[4,48,256]{2,1,0:T(8,128)(2,1)S(1)} %collective-permute-done.got_ref.got, bf16[8,48,128]{2,1,0:T(8,128)(2,1)S(1)} %collective-permute-done.1.near_in), custom_call_target="tpu_custom_call" | custom-call | tf_op jit(solution)/shard_map/pallas_call | solution.py:461
  17.3 0.7 %collective-permute-done.5.got_ref.got = bf16[4,48,256]{2,1,0:T(8,128)(2,1)S(1)} collective-permute-done((bf16[4,48,256]{2,1,0:T(8,128)(2,1)S(1)}, bf16[4,48,256]{2,1,0:T(8,128)(2,1)S(1)}, u32[]{:S(2)}, u32[]{:S(2)}) %collective-permute-start.5) | collective-permute-done | bytes 98336 | tf_op jit(solution)/shard_map/ppermute | solution.py:516
  18.0 0.1 collective-permute-start.6
  18.1 1.3 %collective-permute-done.6.near_in = bf16[8,48,128]{2,1,0:T(8,128)(2,1)S(1)} collective-permute-done((bf16[8,48,128]{2,1,0:T(8,128)(2,1)S(1)}, bf16[8,48,128]{2,1,0:T(8,128)(2,1)S(1)}, u32[]{:S(2)}, u32[]{:S(2)}) %collective-permute-start.6) | collective-permute-done | bytes 98336 | tf_op jit(solution)/shard_map/ppermute | solution.py:527
  19.4 0.2 shard_map.51
  19.6 0.2 collective-permute-start.7
  19.8 0.1 add_select_fusion.table_y
  19.9 1.2 %shard_map.52.warped_boxes = f32[3,8,40,384]{3,2,1,0:T(8,128)S(1)} custom-call(f32[8,40,384]{2,1,0:T(8,128)S(1)} %get-tuple-element.21.refs_0_.fixed, f32[8,40,384]{2,1,0:T(8,128)S(1)} %get-tuple-element.29.warped, bf16[384,384]{1,0:T(8,128)(2,1)S(1)} %get-tuple-element.31.band), custom_call_target="tpu_custom_call" | custom-call | tf_op jit(solution)/shard_map/pallas_call | solution.py:461
  21.1 0.0 collective-permute-done.7.rims
  21.1 3.6 %shard_map.53 = f32[3,8,16]{2,1,0:T(8,128)S(1)} custom-call(f32[8,40,384]{2,1,0:T(8,128)S(1)} %get-tuple-element.21.refs_0_.fixed, f32[8,40,384]{2,1,0:T(8,128)S(1)} %get-tuple-element.29.warped, f32[2,8,40,384]{3,2,1,0:T(8,128)S(1)} %get-tuple-element.30.fixed_boxes, f32[3,8,40,384]{3,2,1,0:T(8,128)S(1)} %shard_map.52.warped_boxes, ...), custom_call_target="tpu_custom_call" | custom-call | tf_op jit(solution)/shard_map/pallas_call | solution.py:461
  24.7 4.2 %collective-permute-start.10 = (f32[3,8,16]{2,1,0:T(8,128)S(1)}, f32[3,8,16]{2,1,0:T(8,128)S(1)}, u32[]{:S(2)}, u32[]{:S(2)}) collective-permute-start(f32[3,8,16]{2,1,0:T(8,128)S(1)} %shard_map.53), channel_id=1, source_target_pairs={{0,2},{2,4},{4,10},{6,0},{8,6},{10,12},{12,14},{14,8},{1,3},{3,5},... | collective-permute-start | bytes 4616 | tf_op jit(solution)/shard_map/ppermute | solution.py:555
  28.9 0.0 collective-permute-start.9
  28.9 0.1 collective-permute-start.8
  29.0 1.3 %collective-permute-done.10 = f32[3,8,16]{2,1,0:T(8,128)S(1)} collective-permute-done((f32[3,8,16]{2,1,0:T(8,128)S(1)}, f32[3,8,16]{2,1,0:T(8,128)S(1)}, u32[]{:S(2)}, u32[]{:S(2)}) %collective-permute-start.10) | collective-permute-done | bytes 1568 | tf_op jit(solution)/shard_map/ppermute | solution.py:555
  30.3 0.0 collective-permute-done.9
  30.3 2.3 %collective-permute-done.8 = f32[3,8,16]{2,1,0:T(8,128)S(1)} collective-permute-done((f32[3,8,16]{2,1,0:T(8,128)S(1)}, f32[3,8,16]{2,1,0:T(8,128)S(1)}, u32[]{:S(2)}, u32[]{:S(2)}) %collective-permute-start.8) | collective-permute-done | bytes 1568 | tf_op jit(solution)/shard_map/ppermute | solution.py:554
  32.6 0.6 %fusion.1 = f32[3,1,4,16]{3,2,1,0:T(4,128)} fusion(f32[3,8,16]{2,1,0:T(8,128)S(1)} %collective-permute-done.8, f32[3,8,16]{2,1,0:T(8,128)S(1)} %shard_map.53, f32[3,2,16]{2,1,0:T(2,128)S(1)} %get-tuple-element.34, f32[3,2,16]{2,1,0:T(2,128)S(1)} %get-tuple-element.33), kind=kLoop, calls=%fused_computation.3 | loop fusion | flops 576 | bytes 3072 | tf_op jit(solution)/shard_map/broadcast_in_dim | solution.py:562
  (14 shorter events, 0.2 us)
Async XLA Ops:
  1.2 8.4 %collective-permute-start.2 = (bf16[4,4,16,128]{3,2,1,0:T(8,128)(2,1)S(1)}, bf16[4,4,16,128]{3,2,1,0:T(8,128)(2,1)S(1)}, u32[]{:S(2)}, u32[]{:S(2)}) collective-permute-start(bf16[4,4,16,128]{3,2,1,0:T(8,128)(2,1)S(1)} %get-tuple-element.24), channel_id=1, source_target_pairs={{0,4},{4,0},{8,12},{12,8},{1,5},{5,1},{9,13},{13,9},{2,6},{6,2},{1... | collective-permute-start | bytes 196616 | tf_op jit(solution)/shard_map/ppermute | solution.py:509
  4.3 7.3 %collective-permute-start.3 = (bf16[4,4,16,128]{3,2,1,0:T(8,128)(2,1)S(1)}, bf16[4,4,16,128]{3,2,1,0:T(8,128)(2,1)S(1)}, u32[]{:S(2)}, u32[]{:S(2)}) collective-permute-start(bf16[4,4,16,128]{3,2,1,0:T(8,128)(2,1)S(1)} %get-tuple-element.25), channel_id=1, source_target_pairs={{0,8},{4,12},{8,0},{12,4},{1,9},{5,13},{9,1},{13,5},{2,10},{6,14},... | collective-permute-start | bytes 196616 | tf_op jit(solution)/shard_map/ppermute | solution.py:509
  6.9 6.1 %collective-permute-start.4 = (bf16[4,4,16,128]{3,2,1,0:T(8,128)(2,1)S(1)}, bf16[4,4,16,128]{3,2,1,0:T(8,128)(2,1)S(1)}, u32[]{:S(2)}, u32[]{:S(2)}) collective-permute-start(bf16[4,4,16,128]{3,2,1,0:T(8,128)(2,1)S(1)} %get-tuple-element.26), channel_id=1, source_target_pairs={{0,12},{4,8},{8,4},{12,0},{1,13},{5,9},{9,5},{13,1},{2,14},{6,10},... | collective-permute-start | bytes 196616 | tf_op jit(solution)/shard_map/ppermute | solution.py:509
  6.9 8.0 %collective-permute-start = (bf16[4,48,256]{2,1,0:T(8,128)(2,1)S(1)}, bf16[4,48,256]{2,1,0:T(8,128)(2,1)S(1)}, u32[]{:S(2)}, u32[]{:S(2)}) collective-permute-start(bf16[4,48,256]{2,1,0:T(8,128)(2,1)S(1)} %get-tuple-element.20), channel_id=1, source_target_pairs={{0,2},{2,0},{1,3},{3,1},{4,6},{6,4},{5,7},{7,5},{8,10},{10,8},{9,1... | collective-permute-start | bytes 294920 | tf_op jit(solution)/shard_map/ppermute | solution.py:512
  13.3 4.7 %collective-permute-start.5 = (bf16[4,48,256]{2,1,0:T(8,128)(2,1)S(1)}, bf16[4,48,256]{2,1,0:T(8,128)(2,1)S(1)}, u32[]{:S(2)}, u32[]{:S(2)}) collective-permute-start(bf16[4,48,256]{2,1,0:T(8,128)(2,1)S(1)} %get-tuple-element.28), channel_id=1, source_target_pairs={{0,2},{2,0},{1,3},{3,1},{4,6},{6,4},{5,7},{7,5},{8,10},{10,8},{9,1... | collective-permute-start | bytes 294920 | tf_op jit(solution)/shard_map/ppermute | solution.py:516
  14.9 1.4 %collective-permute-start.1 = (bf16[8,48,128]{2,1,0:T(8,128)(2,1)S(1)}, bf16[8,48,128]{2,1,0:T(8,128)(2,1)S(1)}, u32[]{:S(2)}, u32[]{:S(2)}) collective-permute-start(bf16[8,48,128]{2,1,0:T(8,128)(2,1)S(1)} %shard_map.47), channel_id=1, source_target_pairs={{0,1},{1,0},{2,3},{3,2},{4,5},{5,4},{6,7},{7,6},{8,9},{9,8},{10,11... | collective-permute-start | bytes 294920 | tf_op jit(solution)/shard_map/ppermute | solution.py:518
  18.0 1.4 %collective-permute-start.6 = (bf16[8,48,128]{2,1,0:T(8,128)(2,1)S(1)}, bf16[8,48,128]{2,1,0:T(8,128)(2,1)S(1)}, u32[]{:S(2)}, u32[]{:S(2)}) collective-permute-start(bf16[8,48,128]{2,1,0:T(8,128)(2,1)S(1)} %shard_map.50), channel_id=1, source_target_pairs={{0,1},{1,0},{2,3},{3,2},{4,5},{5,4},{6,7},{7,6},{8,9},{9,8},{10,11... | collective-permute-start | bytes 294920 | tf_op jit(solution)/shard_map/ppermute | solution.py:527
  19.6 1.5 %collective-permute-start.7 = (bf16[2,32,384]{2,1,0:T(8,128)(2,1)S(1)}, bf16[2,32,384]{2,1,0:T(8,128)(2,1)S(1)}, u32[]{:S(2)}, u32[]{:S(2)}) collective-permute-start(bf16[2,32,384]{2,1,0:T(8,128)(2,1)S(1)} %get-tuple-element.32), channel_id=1, source_target_pairs={{0,1},{2,6},{4,8},{6,2},{8,4},{10,14},{12,13},{14,10},{1,0},{3,7},... | collective-permute-start | bytes 147464 | tf_op jit(solution)/shard_map/ppermute | solution.py:533
  24.7 5.6 %collective-permute-start.10 = (f32[3,8,16]{2,1,0:T(8,128)S(1)}, f32[3,8,16]{2,1,0:T(8,128)S(1)}, u32[]{:S(2)}, u32[]{:S(2)}) collective-permute-start(f32[3,8,16]{2,1,0:T(8,128)S(1)} %shard_map.53), channel_id=1, source_target_pairs={{0,2},{2,4},{4,10},{6,0},{8,6},{10,12},{12,14},{14,8},{1,3},{3,5},... | collective-permute-start | bytes 4616 | tf_op jit(solution)/shard_map/ppermute | solution.py:555
  28.9 1.4 %collective-permute-start.9 = (f32[3,8,16]{2,1,0:T(8,128)S(1)}, f32[3,8,16]{2,1,0:T(8,128)S(1)}, u32[]{:S(2)}, u32[]{:S(2)}) collective-permute-start(f32[3,8,16]{2,1,0:T(8,128)S(1)} %shard_map.53), channel_id=1, source_target_pairs={{0,1},{2,6},{4,8},{6,2},{8,4},{10,14},{12,13},{14,10},{1,0},{3,7},... | collective-permute-start | bytes 4616 | tf_op jit(solution)/shard_map/ppermute | solution.py:556
  28.9 3.7 %collective-permute-start.8 = (f32[3,8,16]{2,1,0:T(8,128)S(1)}, f32[3,8,16]{2,1,0:T(8,128)S(1)}, u32[]{:S(2)}, u32[]{:S(2)}) collective-permute-start(f32[3,8,16]{2,1,0:T(8,128)S(1)} %shard_map.53), channel_id=1, source_target_pairs={{0,2},{2,0},{1,3},{3,1},{4,6},{6,4},{5,7},{7,5},{8,10},{10,8},{9,1... | collective-permute-start | bytes 4616 | tf_op jit(solution)/shard_map/ppermute | solution.py:554

commit v5 on v4

--- a/solution.py
+++ b/solution.py
@@ -181,8 +181,19 @@
 
 
 EDGE = 2 * RAD
-SEND_ROWS = 48
+KEEP_ROWS, SEND_ROWS = 48, 40
 KERNEL_BYTES = 24 << 20
+
+
+def far_first(tiles):
+    return sorted(range(1, tiles), key=lambda step: (step < 2, step))
+
+
+def send_window(half, image, out):
+    rows = out.shape[1]
+    value = image[...].astype(jnp.float32)
+    value = jnp.where(half == 1, value[:, :rows], value[:, value.shape[1] - rows :])
+    out[...] = value.astype(out.dtype)
 
 
 def pack_kernel(tiles, source_ref, source_in, moving_ref, fixed_ref, *out_refs):
@@ -192,13 +203,12 @@
     fixed_out[...] = fixed_ref[...]
     me = lax.axis_index("tile")
     half = lax.rem(me + lax.axis_index("gz"), 2)
-    start = pl.multiple_of((1 - half) * BLK_Y, BLK_Y)
-    send_out[...] = fixed_ref[:, pl.ds(start, SEND_ROWS), :]
+    send_window(half, fixed_ref, send_out)
     height, width = moving_ref.shape[1:]
     xblocks = width // BLK_X
     blocks = (height // BLK_Y) * xblocks
     cap = packs[0].shape[0]
-    for step in range(1, tiles):
+    for step, pack in zip(far_first(tiles), packs):
         other = lax.bitwise_xor(me, step)
         count = jnp.int32(0)
         chosen = [jnp.int32(0)] * cap
@@ -209,18 +219,18 @@
         for slot, block in enumerate(chosen):
             row = pl.multiple_of(block // xblocks * BLK_Y, BLK_Y)
             col = pl.multiple_of(lax.rem(block, xblocks) * BLK_X, BLK_X)
-            packs[step - 1][slot] = moving_ref[:, pl.ds(row, BLK_Y), pl.ds(col, BLK_X)]
+            pack[slot] = moving_ref[:, pl.ds(row, BLK_Y), pl.ds(col, BLK_X)]
 
 
 def unpack_kernel(tiles, source_ref, shift_ref, moving_ref, *refs):
-    recvs = refs[: tiles - 1]
+    recvs = dict(zip(far_first(tiles), refs))
     own_ref, send_ref = refs[tiles - 1 :]
     me = lax.axis_index("tile")
     half = lax.rem(me + lax.axis_index("gz"), 2)
     height, width = moving_ref.shape[1:]
     xblocks = width // BLK_X
     blocks = (height // BLK_Y) * xblocks
-    cap = recvs[0].shape[0]
+    cap = refs[0].shape[0]
     for block in range(blocks):
         row, col = (block // xblocks) * BLK_Y, (block % xblocks) * BLK_X
         source = source_ref[me, block]
@@ -231,15 +241,14 @@
         step = lax.bitwise_xor(source, me)
         value = moving_ref[:, row : row + BLK_Y, col : col + BLK_X].astype(jnp.float32)
         for other in range(1, tiles):
-            value = jnp.where(step == other, recvs[other - 1][slot].astype(jnp.float32), value)
+            value = jnp.where(step == other, recvs[other][slot].astype(jnp.float32), value)
         down = lax.rem(shift_ref[block, 0], BLK_Y)
         right = lax.rem(shift_ref[block, 1], BLK_X)
         value = pltpu.roll(value, right, 2)
         for bit in (1, 2, 4, 8):
             value = jnp.where(lax.bitwise_and(down, bit) != 0, pltpu.roll(value, bit, 1), value)
         own_ref[:, row : row + BLK_Y, col : col + BLK_X] = value.astype(own_ref.dtype)
-    start = pl.multiple_of((1 - half) * BLK_Y, BLK_Y)
-    send_ref[...] = own_ref[:, pl.ds(start, SEND_ROWS), :]
+    send_window(half, own_ref, send_ref)
 
 
 def side_kernel(own_ref, got_ref, *refs):
@@ -250,8 +259,10 @@
     col = pl.multiple_of((1 - lax.axis_index("rep")) * BLK_X, BLK_X)
     start = pl.multiple_of(half * BLK_Y, BLK_Y)
     for i in range(depth):
-        out_ref[group * depth + i] = own_ref[i, pl.ds(start, SEND_ROWS), pl.ds(col, BLK_X)]
-        out_ref[(1 - group) * depth + i] = got_ref[i, :, pl.ds(col, BLK_X)]
+        out_ref[group * depth + i] = own_ref[i, pl.ds(start, KEEP_ROWS), pl.ds(col, BLK_X)]
+        theirs = got_ref[i, :, pl.ds(col, BLK_X)].astype(jnp.float32)
+        theirs = jnp.concatenate([theirs, jnp.zeros((KEEP_ROWS - SEND_ROWS, BLK_X), jnp.float32)], axis=0)
+        out_ref[(1 - group) * depth + i] = theirs.astype(out_ref.dtype)
 
 
 def five(array, axis):
@@ -277,27 +288,37 @@
     levels = lax.broadcasted_iota(jnp.int32, (window, BLK_X), 0)
     inner = (levels >= jnp.where(half == 0, EDGE, 0)) & (levels < jnp.where(half == 0, window, window - EDGE))
     near = inner & (lanes >= low) & (lanes < high)
-    turn = jnp.where(half == 0, EDGE, SEND_ROWS - BLK_Y + EDGE)
-
-    def shift_in(piece):
+
+    def shift_in(piece, skip):
+        turn = jnp.where(half == 0, EDGE, piece.shape[0] - skip)
         return pltpu.roll(piece.astype(jnp.float32), turn, 0)[:window]
 
     for i in range(depth):
-        mine, theirs = group * depth + i, (1 - group) * depth + i
-        for plane, piece in ((mine, own[i, pl.ds(start, SEND_ROWS), :]), (theirs, got[i])):
-            piece = shift_in(piece)
+        mine, theirs = (group * depth + i, BLK_Y - EDGE), ((1 - group) * depth + i, EDGE)
+        for (plane, skip), piece in ((mine, own[i, pl.ds(start, KEEP_ROWS), :]), (theirs, got[i])):
+            piece = shift_in(piece, skip)
             for part in range(width // BLK_X):
                 col = pl.multiple_of(own_col + part * BLK_X, BLK_X)
                 value = piece[:, part * BLK_X : (part + 1) * BLK_X]
                 image[plane, :, pl.ds(col, BLK_X)] = jnp.where(inner, value, 0.0)
-        for plane in (mine, theirs):
-            image[plane, :, pl.ds(new_col, BLK_X)] = jnp.where(near, shift_in(near_in[plane]), 0.0)
+        for plane, skip in (mine, theirs):
+            image[plane, :, pl.ds(new_col, BLK_X)] = jnp.where(near, shift_in(near_in[plane], skip), 0.0)
 
 
 def fill_band(band):
     span = band.shape[0]
     across = lax.broadcasted_iota(jnp.int32, (span, span), 0) - lax.broadcasted_iota(jnp.int32, (span, span), 1)
     band[...] = jnp.where(jnp.abs(across) <= RAD, 1.0, 0.0).astype(band.dtype)
+
+
+def halves(value):
+    high = value.astype(jnp.bfloat16)
+    return high, (value - high.astype(jnp.float32)).astype(jnp.bfloat16)
+
+
+def table_halves(table):
+    high = lax.reduce_precision(table, exponent_bits=8, mantissa_bits=7)
+    return high.astype(jnp.bfloat16), (table - high).astype(jnp.bfloat16)
 
 
 def lane_sums(exact, products, band):
@@ -429,8 +450,7 @@
         for which, value in enumerate(lane_sums([], values, band)):
             terms[which, z] = value
 
-    for d in range(3):
-        sums[d] = jnp.zeros((window, span), jnp.float32)
+    sums[...] = jnp.zeros(sums.shape, jnp.float32)
     owned = (levels >= EDGE) & (levels < window - EDGE)
     for z in range(planes):
         box_a, box_b, box_c = (total(terms[which, k] for k in near_planes(z, planes)) for which in range(3))
@@ -441,19 +461,19 @@
         gain = jnp.where(owned, gain, 0.0) * weight
         ahead = images[z + 1] if z + 1 < planes else 0.0
         behind = images[z - 1] if z > 0 else 0.0
-        sums[0] += gain * (ahead - behind)
-        sums[1] += gain * (pltpu.roll(w, window - 1, 0) - pltpu.roll(w, 1, 0))
-        sums[2] += gain * (pltpu.roll(w, span - 1, 1) - pltpu.roll(w, 1, 1))
-
-    for d in range(3):
-        along_x = lax.dot_general(
-            sums[d], table_x[...], (((1,), (1,)), ((), ())),
-            precision=lax.Precision.HIGHEST, preferred_element_type=jnp.float32,
-        )
-        out_ref[d] = lax.dot_general(
-            table_y[...], along_x, (((1,), (0,)), ((), ())),
-            precision=lax.Precision.HIGHEST, preferred_element_type=jnp.float32,
-        )
+        sums[:window] += gain * (ahead - behind)
+        sums[1 * window : 2 * window] += gain * (pltpu.roll(w, window - 1, 0) - pltpu.roll(w, 1, 0))
+        sums[2 * window : 3 * window] += gain * (pltpu.roll(w, span - 1, 1) - pltpu.roll(w, 1, 1))
+
+    boxed = jnp.dot(
+        jnp.concatenate(halves(sums[...]), axis=0), table_x[...], preferred_element_type=jnp.float32
+    )
+    rows, count = sums.shape[0], out_ref.shape[1]
+    along_x = boxed[:rows] + pltpu.roll(boxed[:rows], boxed.shape[1] - count, 1) + boxed[rows:]
+    high, low = halves(along_x)
+    out_ref[...] = jnp.dot(
+        table_y[...], jnp.concatenate([high, high, low], axis=0), preferred_element_type=jnp.float32
+    )[:, :count]
 
 
 def local_kernel(kernel, outs, arrays, scratch=()):
@@ -479,7 +499,7 @@
     window, span = height // 2 + 2 * EDGE, width + BLK_X
     short, full = jnp.bfloat16, jnp.float32
     whole, send_shape = (fixed_image.shape, short), ((depth, SEND_ROWS, width), short)
-    side_shape = ((planes, SEND_ROWS, BLK_X), short)
+    side_shape = ((planes, KEEP_ROWS, BLK_X), short)
     image_shape = ((planes, window, span), full)
     smem, vmem = (pl.BlockSpec(memory_space=space) for space in (pltpu.SMEM, pltpu.VMEM))
     outs = [((cap, depth, BLK_Y, BLK_X), short)] * (tiles - 1) + [(sources.shape, jnp.int32), whole, whole, send_shape]
@@ -507,7 +527,7 @@
 
     got = [
         lax.ppermute(pack, "tile", [(t, t ^ step) for t in range(tiles)])
-        for step, pack in zip(range(1, tiles), packs)
+        for step, pack in zip(far_first(tiles), packs)
     ]
     fixed_got = lax.ppermute(fixed_send, "gz", swap)
     own, send = local_kernel(
@@ -539,18 +559,24 @@
     row_at = jnp.arange(window, dtype=jnp.int32)
     table_y = spline_table(half * (height // 2) - EDGE, window, -2, row_knots + 4)
     table_y = jnp.where(((row_at >= EDGE) & (row_at < window - EDGE))[:, None], table_y, 0.0).T
-    table_x = spline_table(side * BLK_X, span, side * col_knots, col_knots).T
+    stacked = 3 * window + -3 * window % 128
+    table_y = jnp.pad(jnp.kron(jnp.eye(3, dtype=full), table_y), ((0, 0), (0, stacked - 3 * window)))
+    high, low = table_halves(table_y)
+    table_y = jnp.concatenate([high, low, high], axis=1)
+    high, low = table_halves(spline_table(side * BLK_X, span, side * col_knots, col_knots))
+    table_x = jnp.pad(jnp.concatenate([high, low], axis=1), ((0, 0), (0, -2 * col_knots % 128)))
     (part,) = local_kernel(
         functools.partial(main_kernel, tiles),
-        [((3, row_knots + 4, col_knots), full)],
+        [((3 * (row_knots + 4), col_knots), full)],
         [fixed, warped, fixed_boxes, warped_boxes, rims, band, table_y, table_x],
         [
             pltpu.VMEM((planes, window, span), full),
             pltpu.VMEM((5, planes, 2 * EDGE, span), full),
             pltpu.VMEM((3, planes, window, span), full),
-            pltpu.VMEM((3, window, span), full),
+            pltpu.VMEM((stacked, span), full),
         ],
     )
+    part = part.reshape(3, row_knots + 4, col_knots)
     across = lax.ppermute(part, "gz", swap)
     part_slant = lax.ppermute(part, trio, slant)
     part_straight = lax.ppermute(part, trio, straight)

time: 33.4 us -> 31.4 us (0.940)
  waiting for transfers between devices: 10.2 us -> 7.52 us
  starting transfers between devices: 13.6 us -> 14.4 us
  Pallas kernels: 7.59 us -> 7.05 us
    ppermute x3, waiting for transfers between devices: 3.34 us -> 1.96 us  [fast_body(): lax.ppermute(pack, 'tile', [(t, t ^ step) for t in range(tiles)])]
    ppermute x1, starting transfers between devices: 0.1 us -> 1.18 us  [fast_body(): across = lax.ppermute(part, 'gz', swap)]
    ppermute x1, waiting for transfers between devices: 2.28 us -> 1.66 us  [fast_body(): across = lax.ppermute(part, 'gz', swap)]
    pallas_call x7, Pallas kernels: 6.39 us -> 5.84 us  [local_kernel(): pl.pallas_call(kernel, out_shape=[pltpu.VMEM(shape, dtype) for shape, dty...]
    ppermute x1, waiting for transfers between devices: 1.3 us -> 0.84 us  [fast_body(): part_slant = lax.ppermute(part, trio, slant)]
  transfers between devices with their start and end apart: 11 -> 11, of which waited for: 7 -> 7; matrix products, arithmetic and copies ran while one was open for 3% -> 5% of each run, Pallas kernels for 8% -> 8%
where the time goes in v5:
time: 31.4 us; the launch traced here: 31.1 us
  starting transfers between devices  14.4 us (46%)
  waiting for transfers between devices  7.52 us (24%)
  Pallas kernels  7.05 us (22%)
  other arithmetic  1.02 us (3%)
  local copies, waits for them, and re-layouts  0.99 us (3%)
    pallas_call x7, Pallas kernels, local_kernel(): pl.pallas_call(kernel, out_shape=[pltpu.VMEM(shape, dtype) for shape, dty...  5.84 us
    ppermute x3, starting transfers between devices, fast_body(): lax.ppermute(pack, 'tile', [(t, t ^ step) for t in range(tiles)])  5.68 us
    ppermute x1, starting transfers between devices, fast_body(): part_slant = lax.ppermute(part, trio, slant)  4.12 us
    ppermute x3, waiting for transfers between devices, fast_body(): lax.ppermute(pack, 'tile', [(t, t ^ step) for t in range(tiles)])  1.96 us
    ppermute x1, waiting for transfers between devices, fast_body(): across = lax.ppermute(part, 'gz', swap)  1.66 us
    ppermute x1, starting transfers between devices, fast_body(): warp_got = lax.ppermute(send, 'gz', swap)  1.55 us
    ppermute x1, starting transfers between devices, fast_body(): fixed_got = lax.ppermute(fixed_send, 'gz', swap)  1.49 us
    ppermute x1, waiting for transfers between devices, fast_body(): fixed_near = lax.ppermute(fixed_side, 'rep', swap)  1.28 us
  transfers between devices with their start and end apart: 11, of which 7 were waited for; matrix products, arithmetic and copies ran while one was open for 5% of the time, Pallas kernels for 8%

profile of v5, /device:TPU:0, one launch (start us, length us, event | category | flops | bytes accessed | tf_op | source)
XLA Modules:
  0.0 31.1 jit_solution(17045672036440387797)
XLA Ops:
  0.0 1.2 %shard_map.46 = (bf16[4,4,16,128]{3,2,1,0:T(8,128)(2,1)S(1)}, bf16[4,4,16,128]{3,2,1,0:T(8,128)(2,1)S(1)}, bf16[4,4,16,128]{3,2,1,0:T(8,128)(2,1)S(1)}, s32[4,8]...) custom-call(s32[4,8]{1,0:T(4,128)} %bitcast.9, ...), custom_call_target="tpu_custom_call" | custom-call | tf_op jit(solution)/shard_map/pallas_call | solution.py:506
  1.2 4.1 %collective-permute-start.2 = (bf16[4,4,16,128]{3,2,1,0:T(8,128)(2,1)S(1)}, bf16[4,4,16,128]{3,2,1,0:T(8,128)(2,1)S(1)}, u32[]{:S(2)}, u32[]{:S(2)}) collective-permute-start(bf16[4,4,16,128]{3,2,1,0:T(8,128)(2,1)S(1)} %get-tuple-element.24), channel_id=1, source_target_pairs={{0,8},{4,12},{8,0},{12,4},{1,9},{5,13},{9,1},{13,5},{2,10},{6,14},... | collective-permute-start | bytes 196616 | tf_op jit(solution)/shard_map/ppermute | solution.py:529
  5.3 1.3 %collective-permute-start.3 = (bf16[4,4,16,128]{3,2,1,0:T(8,128)(2,1)S(1)}, bf16[4,4,16,128]{3,2,1,0:T(8,128)(2,1)S(1)}, u32[]{:S(2)}, u32[]{:S(2)}) collective-permute-start(bf16[4,4,16,128]{3,2,1,0:T(8,128)(2,1)S(1)} %get-tuple-element.25), channel_id=1, source_target_pairs={{0,12},{4,8},{8,4},{12,0},{1,13},{5,9},{9,5},{13,1},{2,14},{6,10},... | collective-permute-start | bytes 196616 | tf_op jit(solution)/shard_map/ppermute | solution.py:529
  6.7 0.2 collective-permute-start.4
  6.9 1.5 %collective-permute-start = (bf16[4,40,256]{2,1,0:T(8,128)(2,1)S(1)}, bf16[4,40,256]{2,1,0:T(8,128)(2,1)S(1)}, u32[]{:S(2)}, u32[]{:S(2)}) collective-permute-start(bf16[4,40,256]{2,1,0:T(8,128)(2,1)S(1)} %get-tuple-element.20), channel_id=1, source_target_pairs={{0,2},{2,0},{1,3},{3,1},{4,6},{6,4},{5,7},{7,5},{8,10},{10,8},{9,1... | collective-permute-start | bytes 245768 | tf_op jit(solution)/shard_map/ppermute | solution.py:532
  8.6 0.1 add_select_fusion
  8.7 0.1 broadcast_multiply_fusion
  8.7 0.1 reduce-precision_convert_fusion
  8.8 0.8 %copy.7.shift_ref = s32[8,2]{1,0:T(8,128)S(1)} copy(s32[8,2]{0,1:T(2,128)} %bitcast.11) | data formatting | bytes 128 | tf_op jit(solution)/shard_map/squeeze | solution.py:496
  9.6 0.1 mul.213
  9.7 0.0 collective-permute-done.2.refs_0_
  9.7 1.9 %collective-permute-done.3.refs_1_ = bf16[4,4,16,128]{3,2,1,0:T(8,128)(2,1)S(1)} collective-permute-done((bf16[4,4,16,128]{3,2,1,0:T(8,128)(2,1)S(1)}, bf16[4,4,16,128]{3,2,1,0:T(8,128)(2,1)S(1)}, u32[]{:S(2)}, u32[]{:S(2)}) %collective-permute-start.3) | collective-permute-done | bytes 65568 | tf_op jit(solution)/shard_map/ppermute | solution.py:529
  11.5 0.1 collective-permute-done.4.refs_2_
  11.6 0.4 %shard_map.49 = (bf16[4,64,256]{2,1,0:T(8,128)(2,1)S(1)}, bf16[4,40,256]{2,1,0:T(8,128)(2,1)S(1)}) custom-call(s32[4,8]{1,0:T(4,128)S(1)} %get-tuple-element.22.source_ref, s32[8,2]{1,0:T(8,128)S(1)} %copy.7.shift_ref, bf16[4,64,256]{2,1,0:T(8,128)(2,1)S(1)} %get-tuple-element.23.moving_ref, bf16[4,4,16,128]{3,2,1,0:T(8,128)(2,1)S(1)} %collective-permute-done.2.refs_0_, ...), custom_call_target="tpu_custom_call" | custom-call | tf_op jit(solution)/shard_map/pallas_call | solution.py:481
  12.0 1.6 %collective-permute-start.5 = (bf16[4,40,256]{2,1,0:T(8,128)(2,1)S(1)}, bf16[4,40,256]{2,1,0:T(8,128)(2,1)S(1)}, u32[]{:S(2)}, u32[]{:S(2)}) collective-permute-start(bf16[4,40,256]{2,1,0:T(8,128)(2,1)S(1)} %get-tuple-element.28), channel_id=1, source_target_pairs={{0,2},{2,0},{1,3},{3,1},{4,6},{6,4},{5,7},{7,5},{8,10},{10,8},{9,1... | collective-permute-start | bytes 245768 | tf_op jit(solution)/shard_map/ppermute | solution.py:536
  13.6 0.0 collective-permute-done.got_ref.got
  13.6 0.1 collective-permute-start.1
  13.7 1.3 %collective-permute-done.1.near_in = bf16[8,48,128]{2,1,0:T(8,128)(2,1)S(1)} collective-permute-done((bf16[8,48,128]{2,1,0:T(8,128)(2,1)S(1)}, bf16[8,48,128]{2,1,0:T(8,128)(2,1)S(1)}, u32[]{:S(2)}, u32[]{:S(2)}) %collective-permute-start.1) | collective-permute-done | bytes 98336 | tf_op jit(solution)/shard_map/ppermute | solution.py:538
  15.0 1.0 %shard_map.48 = (f32[8,40,384]{2,1,0:T(8,128)S(1)}, f32[2,8,40,384]{3,2,1,0:T(8,128)S(1)}, bf16[384,384]{1,0:T(8,128)(2,1)S(1)}) custom-call(bf16[4,64,256]{2,1,0:T(8,128)(2,1)S(1)} %get-tuple-element.19.own_ref.own, bf16[4,40,256]{2,1,0:T(8,128)(2,1)S(1)} %collective-permute-done.got_ref.got, bf16[8,48,128]{2,1,0:T(8,128)(2,1)S(1)} %collective-permute-done.1.near_in), custom_call_target="tpu_custom_call" | custom-call | tf_op jit(solution)/shard_map/pallas_call | solution.py:481
  16.0 0.5 %collective-permute-done.5.got_ref.got = bf16[4,40,256]{2,1,0:T(8,128)(2,1)S(1)} collective-permute-done((bf16[4,40,256]{2,1,0:T(8,128)(2,1)S(1)}, bf16[4,40,256]{2,1,0:T(8,128)(2,1)S(1)}, u32[]{:S(2)}, u32[]{:S(2)}) %collective-permute-start.5) | collective-permute-done | bytes 81952 | tf_op jit(solution)/shard_map/ppermute | solution.py:536
  16.5 0.1 collective-permute-start.6
  16.6 1.3 %collective-permute-done.6.near_in = bf16[8,48,128]{2,1,0:T(8,128)(2,1)S(1)} collective-permute-done((bf16[8,48,128]{2,1,0:T(8,128)(2,1)S(1)}, bf16[8,48,128]{2,1,0:T(8,128)(2,1)S(1)}, u32[]{:S(2)}, u32[]{:S(2)}) %collective-permute-start.6) | collective-permute-done | bytes 98336 | tf_op jit(solution)/shard_map/ppermute | solution.py:547
  17.9 0.2 shard_map.51
  18.1 0.2 collective-permute-start.7
  18.3 0.1 copy.8
  18.5 1.1 %shard_map.52.warped_boxes = f32[3,8,40,384]{3,2,1,0:T(8,128)S(1)} custom-call(f32[8,40,384]{2,1,0:T(8,128)S(1)} %get-tuple-element.21.refs_0_.fixed, f32[8,40,384]{2,1,0:T(8,128)S(1)} %get-tuple-element.29.warped, bf16[384,384]{1,0:T(8,128)(2,1)S(1)} %get-tuple-element.31.band), custom_call_target="tpu_custom_call" | custom-call | tf_op jit(solution)/shard_map/pallas_call | solution.py:481
  19.7 0.0 collective-permute-done.7.rims
  19.7 3.0 %shard_map.53 = f32[24,16]{1,0:T(8,128)S(1)} custom-call(f32[8,40,384]{2,1,0:T(8,128)S(1)} %get-tuple-element.21.refs_0_.fixed, f32[8,40,384]{2,1,0:T(8,128)S(1)} %get-tuple-element.29.warped, f32[2,8,40,384]{3,2,1,0:T(8,128)S(1)} %get-tuple-element.30.fixed_boxes, f32[3,8,40,384]{3,2,1,0:T(8,128)S(1)} %shard_map.52.warped_boxes, ...), custom_call_target="tpu_custom_call" | custom-call | tf_op jit(solution)/shard_map/pallas_call | solution.py:481
  22.7 4.1 %collective-permute-start.10 = (f32[3,8,16]{2,1,0:T(8,128)S(1)}, f32[3,8,16]{2,1,0:T(8,128)S(1)}, u32[]{:S(2)}, u32[]{:S(2)}) collective-permute-start(f32[3,8,16]{2,1,0:T(8,128)S(1)} %bitcast.5), channel_id=1, source_target_pairs={{0,2},{2,4},{4,10},{6,0},{8,6},{10,12},{12,14},{14,8},{1,3},{3,5},... | collective-permute-start | bytes 4616 | tf_op jit(solution)/shard_map/ppermute | solution.py:581
  26.8 0.0 collective-permute-start.9
  26.8 1.2 %collective-permute-start.8 = (f32[3,8,16]{2,1,0:T(8,128)S(1)}, f32[3,8,16]{2,1,0:T(8,128)S(1)}, u32[]{:S(2)}, u32[]{:S(2)}) collective-permute-start(f32[3,8,16]{2,1,0:T(8,128)S(1)} %bitcast.7), channel_id=1, source_target_pairs={{0,2},{2,0},{1,3},{3,1},{4,6},{6,4},{5,7},{7,5},{8,10},{10,8},{9,1... | collective-permute-start | bytes 4616 | tf_op jit(solution)/shard_map/ppermute | solution.py:580
  28.0 0.8 %collective-permute-done.10 = f32[3,8,16]{2,1,0:T(8,128)S(1)} collective-permute-done((f32[3,8,16]{2,1,0:T(8,128)S(1)}, f32[3,8,16]{2,1,0:T(8,128)S(1)}, u32[]{:S(2)}, u32[]{:S(2)}) %collective-permute-start.10) | collective-permute-done | bytes 1568 | tf_op jit(solution)/shard_map/ppermute | solution.py:581
  28.8 0.0 collective-permute-done.9
  28.8 1.7 %collective-permute-done.8 = f32[3,8,16]{2,1,0:T(8,128)S(1)} collective-permute-done((f32[3,8,16]{2,1,0:T(8,128)S(1)}, f32[3,8,16]{2,1,0:T(8,128)S(1)}, u32[]{:S(2)}, u32[]{:S(2)}) %collective-permute-start.8) | collective-permute-done | bytes 1568 | tf_op jit(solution)/shard_map/ppermute | solution.py:580
  30.5 0.6 %fusion.3 = f32[3,1,4,16]{3,2,1,0:T(4,128)} fusion(f32[3,8,16]{2,1,0:T(8,128)S(1)} %collective-permute-done.8, f32[3,8,16]{2,1,0:T(8,128)S(1)} %bitcast.8, f32[3,2,16]{2,1,0:T(2,128)S(1)} %get-tuple-element.34, f32[3,2,16]{2,1,0:T(2,128)S(1)} %get-tuple-element.33), kind=kLoop, calls=%fused_computation.12 | loop fusion | flops 576 | bytes 3072 | tf_op jit(solution)/shard_map/broadcast_in_dim | solution.py:588
  (19 shorter events, 0.2 us)
Async XLA Ops:
  1.2 8.5 %collective-permute-start.2 = (bf16[4,4,16,128]{3,2,1,0:T(8,128)(2,1)S(1)}, bf16[4,4,16,128]{3,2,1,0:T(8,128)(2,1)S(1)}, u32[]{:S(2)}, u32[]{:S(2)}) collective-permute-start(bf16[4,4,16,128]{3,2,1,0:T(8,128)(2,1)S(1)} %get-tuple-element.24), channel_id=1, source_target_pairs={{0,8},{4,12},{8,0},{12,4},{1,9},{5,13},{9,1},{13,5},{2,10},{6,14},... | collective-permute-start | bytes 196616 | tf_op jit(solution)/shard_map/ppermute | solution.py:529
  5.3 6.2 %collective-permute-start.3 = (bf16[4,4,16,128]{3,2,1,0:T(8,128)(2,1)S(1)}, bf16[4,4,16,128]{3,2,1,0:T(8,128)(2,1)S(1)}, u32[]{:S(2)}, u32[]{:S(2)}) collective-permute-start(bf16[4,4,16,128]{3,2,1,0:T(8,128)(2,1)S(1)} %get-tuple-element.25), channel_id=1, source_target_pairs={{0,12},{4,8},{8,4},{12,0},{1,13},{5,9},{9,5},{13,1},{2,14},{6,10},... | collective-permute-start | bytes 196616 | tf_op jit(solution)/shard_map/ppermute | solution.py:529
  6.7 5.0 %collective-permute-start.4 = (bf16[4,4,16,128]{3,2,1,0:T(8,128)(2,1)S(1)}, bf16[4,4,16,128]{3,2,1,0:T(8,128)(2,1)S(1)}, u32[]{:S(2)}, u32[]{:S(2)}) collective-permute-start(bf16[4,4,16,128]{3,2,1,0:T(8,128)(2,1)S(1)} %get-tuple-element.26), channel_id=1, source_target_pairs={{0,4},{4,0},{8,12},{12,8},{1,5},{5,1},{9,13},{13,9},{2,6},{6,2},{1... | collective-permute-start | bytes 196616 | tf_op jit(solution)/shard_map/ppermute | solution.py:529
  6.9 6.7 %collective-permute-start = (bf16[4,40,256]{2,1,0:T(8,128)(2,1)S(1)}, bf16[4,40,256]{2,1,0:T(8,128)(2,1)S(1)}, u32[]{:S(2)}, u32[]{:S(2)}) collective-permute-start(bf16[4,40,256]{2,1,0:T(8,128)(2,1)S(1)} %get-tuple-element.20), channel_id=1, source_target_pairs={{0,2},{2,0},{1,3},{3,1},{4,6},{6,4},{5,7},{7,5},{8,10},{10,8},{9,1... | collective-permute-start | bytes 245768 | tf_op jit(solution)/shard_map/ppermute | solution.py:532
  12.0 4.5 %collective-permute-start.5 = (bf16[4,40,256]{2,1,0:T(8,128)(2,1)S(1)}, bf16[4,40,256]{2,1,0:T(8,128)(2,1)S(1)}, u32[]{:S(2)}, u32[]{:S(2)}) collective-permute-start(bf16[4,40,256]{2,1,0:T(8,128)(2,1)S(1)} %get-tuple-element.28), channel_id=1, source_target_pairs={{0,2},{2,0},{1,3},{3,1},{4,6},{6,4},{5,7},{7,5},{8,10},{10,8},{9,1... | collective-permute-start | bytes 245768 | tf_op jit(solution)/shard_map/ppermute | solution.py:536
  13.6 1.4 %collective-permute-start.1 = (bf16[8,48,128]{2,1,0:T(8,128)(2,1)S(1)}, bf16[8,48,128]{2,1,0:T(8,128)(2,1)S(1)}, u32[]{:S(2)}, u32[]{:S(2)}) collective-permute-start(bf16[8,48,128]{2,1,0:T(8,128)(2,1)S(1)} %shard_map.47), channel_id=1, source_target_pairs={{0,1},{1,0},{2,3},{3,2},{4,5},{5,4},{6,7},{7,6},{8,9},{9,8},{10,11... | collective-permute-start | bytes 294920 | tf_op jit(solution)/shard_map/ppermute | solution.py:538
  16.5 1.4 %collective-permute-start.6 = (bf16[8,48,128]{2,1,0:T(8,128)(2,1)S(1)}, bf16[8,48,128]{2,1,0:T(8,128)(2,1)S(1)}, u32[]{:S(2)}, u32[]{:S(2)}) collective-permute-start(bf16[8,48,128]{2,1,0:T(8,128)(2,1)S(1)} %shard_map.50), channel_id=1, source_target_pairs={{0,1},{1,0},{2,3},{3,2},{4,5},{5,4},{6,7},{7,6},{8,9},{9,8},{10,11... | collective-permute-start | bytes 294920 | tf_op jit(solution)/shard_map/ppermute | solution.py:547
  18.1 1.5 %collective-permute-start.7 = (bf16[2,32,384]{2,1,0:T(8,128)(2,1)S(1)}, bf16[2,32,384]{2,1,0:T(8,128)(2,1)S(1)}, u32[]{:S(2)}, u32[]{:S(2)}) collective-permute-start(bf16[2,32,384]{2,1,0:T(8,128)(2,1)S(1)} %get-tuple-element.32), channel_id=1, source_target_pairs={{0,1},{2,6},{4,8},{6,2},{8,4},{10,14},{12,13},{14,10},{1,0},{3,7},... | collective-permute-start | bytes 147464 | tf_op jit(solution)/shard_map/ppermute | solution.py:553
  22.7 6.1 %collective-permute-start.10 = (f32[3,8,16]{2,1,0:T(8,128)S(1)}, f32[3,8,16]{2,1,0:T(8,128)S(1)}, u32[]{:S(2)}, u32[]{:S(2)}) collective-permute-start(f32[3,8,16]{2,1,0:T(8,128)S(1)} %bitcast.5), channel_id=1, source_target_pairs={{0,2},{2,4},{4,10},{6,0},{8,6},{10,12},{12,14},{14,8},{1,3},{3,5},... | collective-permute-start | bytes 4616 | tf_op jit(solution)/shard_map/ppermute | solution.py:581
  26.8 2.0 %collective-permute-start.9 = (f32[3,8,16]{2,1,0:T(8,128)S(1)}, f32[3,8,16]{2,1,0:T(8,128)S(1)}, u32[]{:S(2)}, u32[]{:S(2)}) collective-permute-start(f32[3,8,16]{2,1,0:T(8,128)S(1)} %bitcast.6), channel_id=1, source_target_pairs={{0,1},{2,6},{4,8},{6,2},{8,4},{10,14},{12,13},{14,10},{1,0},{3,7},... | collective-permute-start | bytes 4616 | tf_op jit(solution)/shard_map/ppermute | solution.py:582
  26.8 3.7 %collective-permute-start.8 = (f32[3,8,16]{2,1,0:T(8,128)S(1)}, f32[3,8,16]{2,1,0:T(8,128)S(1)}, u32[]{:S(2)}, u32[]{:S(2)}) collective-permute-start(f32[3,8,16]{2,1,0:T(8,128)S(1)} %bitcast.7), channel_id=1, source_target_pairs={{0,2},{2,0},{1,3},{3,1},{4,6},{6,4},{5,7},{7,5},{8,10},{10,8},{9,1... | collective-permute-start | bytes 4616 | tf_op jit(solution)/shard_map/ppermute | solution.py:580

commit v6 on v5

--- a/solution.py
+++ b/solution.py
@@ -265,6 +265,38 @@
         out_ref[(1 - group) * depth + i] = theirs.astype(out_ref.dtype)
 
 
+def edge_kernel(own_ref, got_ref, fixed_ref, side_ref, rim_ref, far_ref, rims):
+    side_kernel(own_ref, got_ref, side_ref)
+    group, side = lax.axis_index("gz"), lax.axis_index("rep")
+    half = lax.rem(lax.axis_index("tile") + group, 2)
+    depth, height, width = own_ref.shape
+    tile = 2 * EDGE
+    upper = lax.broadcasted_iota(jnp.int32, (tile, width), 0) < EDGE
+    own_start = pl.multiple_of(half * (height - BLK_Y), BLK_Y)
+    own_col = pl.multiple_of(side * BLK_X, BLK_X)
+
+    def pair(low, high):
+        top = jnp.where(upper, low[:tile], pltpu.roll(high[:tile], EDGE, 0))
+        end = jnp.where(upper, pltpu.roll(low[-tile:], EDGE, 0), high[-tile:])
+        return jnp.where(half == 0, top, end)
+
+    for i in range(0, depth, 2):
+        mine = pl.multiple_of((group * depth + i) * EDGE, tile)
+        theirs = pl.multiple_of(((1 - group) * depth + i) * EDGE, tile)
+        rims[1, pl.ds(mine, tile), :] = pair(
+            *(own_ref[i + k, pl.ds(own_start, BLK_Y), :].astype(jnp.float32) for k in range(2))
+        )
+        rims[1, pl.ds(theirs, tile), :] = pair(*(got_ref[i + k].astype(jnp.float32) for k in range(2)))
+    for z in range(0, 2 * depth, 2):
+        low, high = (fixed_ref[z + k, :, pl.ds(own_col, width)] for k in range(2))
+        top = jnp.where(upper, pltpu.roll(low[:tile], EDGE, 0), high[:tile])
+        end = jnp.where(upper, low[-tile:], pltpu.roll(high[-tile:], EDGE, 0))
+        rims[0, z * EDGE : z * EDGE + tile, :] = jnp.where(half == 0, top, end)
+    rim_ref[...] = rims[...].astype(rim_ref.dtype)
+    far_col = pl.multiple_of((1 - side) * BLK_X, BLK_X)
+    far_ref[...] = rims[:, :, pl.ds(far_col, BLK_X)].astype(far_ref.dtype)
+
+
 def five(array, axis):
     size = array.shape[axis]
     pair = array + pltpu.roll(array, 1, axis)
@@ -363,19 +395,8 @@
     sum_planes(rows, boxes)
 
 
-def warped_kernel(own, got, near_in, fixed, image, rims):
+def warped_kernel(own, got, near_in, image):
     assemble(own, got, near_in, image)
-    half = lax.rem(lax.axis_index("tile") + lax.axis_index("gz"), 2)
-    planes, window, span = image.shape
-    upper = lax.broadcasted_iota(jnp.int32, (2 * EDGE, span), 0) < EDGE
-    for which, source in enumerate((fixed, image)):
-        tiles = []
-        for z in range(0, planes, 2):
-            low, high = source.at[z], source.at[z + 1]
-            top = jnp.where(upper, pltpu.roll(low[: 2 * EDGE], EDGE, 0), high[: 2 * EDGE])
-            end = jnp.where(upper, low[window - 2 * EDGE :], pltpu.roll(high[window - 2 * EDGE :], EDGE, 0))
-            tiles.append(jnp.where(half == 0, top, end))
-        rims[which] = jnp.concatenate(tiles, axis=0).astype(rims.dtype)
 
 
 def cross_kernel(fixed, warped, band, boxes, rows):
@@ -387,8 +408,8 @@
 
 
 def main_kernel(
-    tiles, fixed, warped, fixed_boxes, warped_boxes, rims, band, table_y, table_x,
-    out_ref, images, edges, terms, sums,
+    tiles, fixed, warped, fixed_boxes, warped_boxes, rims, far_rims, band, table_x,
+    out_ref, images, edges, terms, sums, whole_rims,
 ):
     side, me = lax.axis_index("rep"), lax.axis_index("tile")
     half = lax.rem(me + lax.axis_index("gz"), 2)
@@ -404,8 +425,16 @@
     inside = (lanes >= low_lane) & (lanes < high_lane) & (levels >= low_row) & (levels < high_row)
 
     outer = (first + last) != 0
-    rim_f = jnp.where(outer, 0.0, rims[0].astype(jnp.float32))
-    rim_w = jnp.where(outer, 0.0, rims[1].astype(jnp.float32))
+    width = rims.shape[2]
+    own_col = pl.multiple_of(side * BLK_X, BLK_X)
+    new_col = pl.multiple_of((1 - side) * width, BLK_X)
+    far_lanes = lax.broadcasted_iota(jnp.int32, far_rims.shape[1:], 1) + new_col
+    far = (far_lanes >= low_lane) & (far_lanes < high_lane)
+    for which in range(2):
+        whole_rims[which, :, pl.ds(own_col, width)] = rims[which].astype(jnp.float32)
+        whole_rims[which, :, pl.ds(new_col, BLK_X)] = jnp.where(far, far_rims[which].astype(jnp.float32), 0.0)
+    rim_f = jnp.where(outer, 0.0, whole_rims[0])
+    rim_w = jnp.where(outer, 0.0, whole_rims[1])
     rim_sums = lane_sums([rim_f, rim_w], [rim_f * rim_f, rim_w * rim_w, rim_f * rim_w], band)
     at = lax.broadcasted_iota(jnp.int32, (tile, span), 0)
     upper = at < EDGE
@@ -450,7 +479,8 @@
         for which, value in enumerate(lane_sums([], values, band)):
             terms[which, z] = value
 
-    sums[...] = jnp.zeros(sums.shape, jnp.float32)
+    for d in range(3):
+        sums[d] = jnp.zeros((window, span), jnp.float32)
     owned = (levels >= EDGE) & (levels < window - EDGE)
     for z in range(planes):
         box_a, box_b, box_c = (total(terms[which, k] for k in near_planes(z, planes)) for which in range(3))
@@ -461,19 +491,44 @@
         gain = jnp.where(owned, gain, 0.0) * weight
         ahead = images[z + 1] if z + 1 < planes else 0.0
         behind = images[z - 1] if z > 0 else 0.0
-        sums[:window] += gain * (ahead - behind)
-        sums[1 * window : 2 * window] += gain * (pltpu.roll(w, window - 1, 0) - pltpu.roll(w, 1, 0))
-        sums[2 * window : 3 * window] += gain * (pltpu.roll(w, span - 1, 1) - pltpu.roll(w, 1, 1))
-
+        sums[0] += gain * (ahead - behind)
+        sums[1] += gain * (pltpu.roll(w, window - 1, 0) - pltpu.roll(w, 1, 0))
+        sums[2] += gain * (pltpu.roll(w, span - 1, 1) - pltpu.roll(w, 1, 1))
+
+    knots = window // SPACING
+    at_row = lax.broadcasted_iota(jnp.int32, (window, BLK_X), 0) - EDGE
+    knot = lax.shift_right_arithmetic(at_row, 4)
+    u = (at_row - knot * SPACING).astype(jnp.float32) * (1.0 / SPACING)
+    square = u * u
+    cube = square * u
+    weights = (
+        (1.0 - u) * (1.0 - u) * (1.0 - u) * (1.0 / 6.0),
+        (3.0 * cube - 6.0 * square + 4.0) * (1.0 / 6.0),
+        (-3.0 * cube + 3.0 * square + 3.0 * u + 1.0) * (1.0 / 6.0),
+        cube * (1.0 / 6.0),
+    )
+    at_knot = lax.broadcasted_iota(jnp.int32, (tile, span), 0)
+    stack = []
+    columns = []
+    for target in range(knots + 3):
+        column = jnp.zeros((window, BLK_X), jnp.float32)
+        for offset in range(4):
+            column = jnp.where(knot == target - offset, weights[offset], column)
+        column = jnp.where((at_row >= 0) & (at_row < window - tile), column, 0.0)
+        columns.append(jnp.concatenate([column] * (span // BLK_X), axis=1))
+    for d in range(3):
+        found = jnp.zeros((tile, span), jnp.float32)
+        for target, column in enumerate(columns):
+            line = jnp.sum(sums[d] * column, axis=0, keepdims=True)
+            found = jnp.where(at_knot == target, line, found)
+        stack.append(jnp.where(half == 0, pltpu.roll(found, 1, 0), pltpu.roll(found, 1 + knots, 0)))
     boxed = jnp.dot(
-        jnp.concatenate(halves(sums[...]), axis=0), table_x[...], preferred_element_type=jnp.float32
-    )
-    rows, count = sums.shape[0], out_ref.shape[1]
+        jnp.concatenate(halves(jnp.concatenate(stack, axis=0)), axis=0), table_x[...],
+        preferred_element_type=jnp.float32,
+    )
+    rows, count = out_ref.shape
     along_x = boxed[:rows] + pltpu.roll(boxed[:rows], boxed.shape[1] - count, 1) + boxed[rows:]
-    high, low = halves(along_x)
-    out_ref[...] = jnp.dot(
-        table_y[...], jnp.concatenate([high, high, low], axis=0), preferred_element_type=jnp.float32
-    )[:, :count]
+    out_ref[...] = along_x[:, :count]
 
 
 def local_kernel(kernel, outs, arrays, scratch=()):
@@ -516,13 +571,14 @@
         return (t * 2 + g) * 2 + r
 
     swap = [(0, 1), (1, 0)]
-    straight, slant = [], []
+    straight, slant, crossed = [], [], []
     for r in range(2):
         for t in range(tiles):
             for g in range(2):
                 to = t - 1 if (g + t) % 2 == 0 else t + 1
                 there = 0 <= to < tiles
                 straight.append((number(t, g, r), number(to, g, r) if there else number(t, g, 1 - r)))
+                crossed.append((number(t, g, r), number(to if there else t, g, 1 - r)))
                 slant.append((number(t, g, r), number(to if there else t, 1 - g, r)))
 
     got = [
@@ -543,37 +599,34 @@
         [fixed_image, fixed_got, fixed_near],
         [pltpu.VMEM(boxes[0], full)],
     )
-    (warp_side,) = local_kernel(side_kernel, [side_shape], [own, warp_got, fixed])
+    rim_shape = (2, planes * EDGE, width)
+    warp_side, rims, far_rims = local_kernel(
+        edge_kernel,
+        [side_shape, (rim_shape, short), ((2, planes * EDGE, BLK_X), short)],
+        [own, warp_got, fixed],
+        [pltpu.VMEM(rim_shape, full)],
+    )
     warp_near = lax.ppermute(warp_side, "rep", swap)
-    warped, rims = local_kernel(
-        warped_kernel,
-        [image_shape, ((2, planes * EDGE, span), short)],
-        [own, warp_got, warp_near, fixed],
-    )
     rims = lax.ppermute(rims, trio, straight)
+    far_rims = lax.ppermute(far_rims, trio, crossed)
+    (warped,) = local_kernel(warped_kernel, [image_shape], [own, warp_got, warp_near])
     (warped_boxes,) = local_kernel(
         cross_kernel, [(boxes[1], full)], [fixed, warped, band], [pltpu.VMEM(boxes[1], full)]
     )
 
     row_knots, col_knots = height // SPACING, width // SPACING
-    row_at = jnp.arange(window, dtype=jnp.int32)
-    table_y = spline_table(half * (height // 2) - EDGE, window, -2, row_knots + 4)
-    table_y = jnp.where(((row_at >= EDGE) & (row_at < window - EDGE))[:, None], table_y, 0.0).T
-    stacked = 3 * window + -3 * window % 128
-    table_y = jnp.pad(jnp.kron(jnp.eye(3, dtype=full), table_y), ((0, 0), (0, stacked - 3 * window)))
-    high, low = table_halves(table_y)
-    table_y = jnp.concatenate([high, low, high], axis=1)
     high, low = table_halves(spline_table(side * BLK_X, span, side * col_knots, col_knots))
     table_x = jnp.pad(jnp.concatenate([high, low], axis=1), ((0, 0), (0, -2 * col_knots % 128)))
     (part,) = local_kernel(
         functools.partial(main_kernel, tiles),
         [((3 * (row_knots + 4), col_knots), full)],
-        [fixed, warped, fixed_boxes, warped_boxes, rims, band, table_y, table_x],
+        [fixed, warped, fixed_boxes, warped_boxes, rims, far_rims, band, table_x],
         [
             pltpu.VMEM((planes, window, span), full),
             pltpu.VMEM((5, planes, 2 * EDGE, span), full),
             pltpu.VMEM((3, planes, window, span), full),
-            pltpu.VMEM((stacked, span), full),
+            pltpu.VMEM((3, window, span), full),
+            pltpu.VMEM((2, planes * EDGE, span), full),
         ],
     )
     part = part.reshape(3, row_knots + 4, col_knots)

time: 31.4 us -> 30.2 us (0.962)
  waiting for transfers between devices: 7.52 us -> 6.84 us
    ppermute x1, starting transfers between devices: 4.12 us -> 2.62 us  [fast_body(): part_slant = lax.ppermute(part, trio, slant)]
    ppermute x1, starting transfers between devices: 1.18 us -> 2.3 us  [fast_body(): across = lax.ppermute(part, 'gz', swap)]
    ppermute x1, waiting for transfers between devices: 0.84 us -> 0.01 us  [fast_body(): part_slant = lax.ppermute(part, trio, slant)]
    ppermute x3, waiting for transfers between devices: 1.96 us -> 2.41 us  [fast_body(): lax.ppermute(pack, 'tile', [(t, t ^ step) for t in range(tiles)])]
  transfers between devices with their start and end apart: 11 -> 12, of which waited for: 7 -> 6; matrix products, arithmetic and copies ran while one was open for 5% -> 4% of each run, Pallas kernels for 8% -> 9%
where the time goes in v6:
time: 30.2 us; the launch traced here: 30.1 us
  starting transfers between devices  14.4 us (48%)
  Pallas kernels  7.09 us (23%)
  waiting for transfers between devices  6.84 us (23%)
  local copies, waits for them, and re-layouts  0.91 us (3%)
  other arithmetic  0.77 us (3%)
    pallas_call x7, Pallas kernels, local_kernel(): pl.pallas_call(kernel, out_shape=[pltpu.VMEM(shape, dtype) for shape, dty...  5.89 us
    ppermute x3, starting transfers between devices, fast_body(): lax.ppermute(pack, 'tile', [(t, t ^ step) for t in range(tiles)])  5.68 us
    ppermute x1, starting transfers between devices, fast_body(): part_slant = lax.ppermute(part, trio, slant)  2.62 us
    ppermute x3, waiting for transfers between devices, fast_body(): lax.ppermute(pack, 'tile', [(t, t ^ step) for t in range(tiles)])  2.41 us
    ppermute x1, starting transfers between devices, fast_body(): across = lax.ppermute(part, 'gz', swap)  2.3 us
    ppermute x1, waiting for transfers between devices, fast_body(): across = lax.ppermute(part, 'gz', swap)  1.65 us
    ppermute x1, starting transfers between devices, fast_body(): warp_got = lax.ppermute(send, 'gz', swap)  1.55 us
    ppermute x1, starting transfers between devices, fast_body(): fixed_got = lax.ppermute(fixed_send, 'gz', swap)  1.49 us
  transfers between devices with their start and end apart: 12, of which 6 were waited for; matrix products, arithmetic and copies ran while one was open for 4% of the time, Pallas kernels for 9%

profile of v6, /device:TPU:0, one launch (start us, length us, event | category | flops | bytes accessed | tf_op | source)
XLA Modules:
  0.0 30.1 jit_solution(14078258857369625977)
XLA Ops:
  0.0 1.2 %shard_map.46 = (bf16[4,4,16,128]{3,2,1,0:T(8,128)(2,1)S(1)}, bf16[4,4,16,128]{3,2,1,0:T(8,128)(2,1)S(1)}, bf16[4,4,16,128]{3,2,1,0:T(8,128)(2,1)S(1)}, s32[4,8]...) custom-call(s32[4,8]{1,0:T(4,128)} %bitcast.9, ...), custom_call_target="tpu_custom_call" | custom-call | tf_op jit(solution)/shard_map/pallas_call | solution.py:561
  1.2 4.1 %collective-permute-start.2 = (bf16[4,4,16,128]{3,2,1,0:T(8,128)(2,1)S(1)}, bf16[4,4,16,128]{3,2,1,0:T(8,128)(2,1)S(1)}, u32[]{:S(2)}, u32[]{:S(2)}) collective-permute-start(bf16[4,4,16,128]{3,2,1,0:T(8,128)(2,1)S(1)} %get-tuple-element.25), channel_id=1, source_target_pairs={{0,8},{4,12},{8,0},{12,4},{1,9},{5,13},{9,1},{13,5},{2,10},{6,14},... | collective-permute-start | bytes 196616 | tf_op jit(solution)/shard_map/ppermute | solution.py:585
  5.3 1.3 %collective-permute-start.3 = (bf16[4,4,16,128]{3,2,1,0:T(8,128)(2,1)S(1)}, bf16[4,4,16,128]{3,2,1,0:T(8,128)(2,1)S(1)}, u32[]{:S(2)}, u32[]{:S(2)}) collective-permute-start(bf16[4,4,16,128]{3,2,1,0:T(8,128)(2,1)S(1)} %get-tuple-element.26), channel_id=1, source_target_pairs={{0,12},{4,8},{8,4},{12,0},{1,13},{5,9},{9,5},{13,1},{2,14},{6,10},... | collective-permute-start | bytes 196616 | tf_op jit(solution)/shard_map/ppermute | solution.py:585
  6.7 0.2 collective-permute-start.4
  6.9 1.5 %collective-permute-start = (bf16[4,40,256]{2,1,0:T(8,128)(2,1)S(1)}, bf16[4,40,256]{2,1,0:T(8,128)(2,1)S(1)}, u32[]{:S(2)}, u32[]{:S(2)}) collective-permute-start(bf16[4,40,256]{2,1,0:T(8,128)(2,1)S(1)} %get-tuple-element.21), channel_id=1, source_target_pairs={{0,2},{2,0},{1,3},{3,1},{4,6},{6,4},{5,7},{7,5},{8,10},{10,8},{9,1... | collective-permute-start | bytes 245768 | tf_op jit(solution)/shard_map/ppermute | solution.py:588
  8.5 0.8 %copy.6.shift_ref = s32[8,2]{1,0:T(8,128)S(1)} copy(s32[8,2]{0,1:T(2,128)} %bitcast.11) | data formatting | bytes 128 | tf_op jit(solution)/shard_map/squeeze | solution.py:551
  9.2 0.0 collective-permute-done.2.refs_0_
  9.2 2.3 %collective-permute-done.3.refs_1_ = bf16[4,4,16,128]{3,2,1,0:T(8,128)(2,1)S(1)} collective-permute-done((bf16[4,4,16,128]{3,2,1,0:T(8,128)(2,1)S(1)}, bf16[4,4,16,128]{3,2,1,0:T(8,128)(2,1)S(1)}, u32[]{:S(2)}, u32[]{:S(2)}) %collective-permute-start.3) | collective-permute-done | bytes 65568 | tf_op jit(solution)/shard_map/ppermute | solution.py:585
  11.5 0.1 collective-permute-done.4.refs_2_
  11.6 0.4 %shard_map.49 = (bf16[4,64,256]{2,1,0:T(8,128)(2,1)S(1)}, bf16[4,40,256]{2,1,0:T(8,128)(2,1)S(1)}) custom-call(s32[4,8]{1,0:T(4,128)S(1)} %get-tuple-element.23.source_ref, s32[8,2]{1,0:T(8,128)S(1)} %copy.6.shift_ref, bf16[4,64,256]{2,1,0:T(8,128)(2,1)S(1)} %get-tuple-element.24.moving_ref, bf16[4,4,16,128]{3,2,1,0:T(8,128)(2,1)S(1)} %collective-permute-done.2.refs_0_, ...), custom_call_target="tpu_custom_call" | custom-call | tf_op jit(solution)/shard_map/pallas_call | solution.py:536
  12.0 1.6 %collective-permute-start.5 = (bf16[4,40,256]{2,1,0:T(8,128)(2,1)S(1)}, bf16[4,40,256]{2,1,0:T(8,128)(2,1)S(1)}, u32[]{:S(2)}, u32[]{:S(2)}) collective-permute-start(bf16[4,40,256]{2,1,0:T(8,128)(2,1)S(1)} %get-tuple-element.29), channel_id=1, source_target_pairs={{0,2},{2,0},{1,3},{3,1},{4,6},{6,4},{5,7},{7,5},{8,10},{10,8},{9,1... | collective-permute-start | bytes 245768 | tf_op jit(solution)/shard_map/ppermute | solution.py:592
  13.6 0.0 collective-permute-done.got_ref.got
  13.6 0.1 collective-permute-start.1
  13.7 0.1 reduce-precision_convert_fusion
  13.8 1.2 %collective-permute-done.1.near_in = bf16[8,48,128]{2,1,0:T(8,128)(2,1)S(1)} collective-permute-done((bf16[8,48,128]{2,1,0:T(8,128)(2,1)S(1)}, bf16[8,48,128]{2,1,0:T(8,128)(2,1)S(1)}, u32[]{:S(2)}, u32[]{:S(2)}) %collective-permute-start.1) | collective-permute-done | bytes 98336 | tf_op jit(solution)/shard_map/ppermute | solution.py:594
  15.0 1.0 %shard_map.48 = (f32[8,40,384]{2,1,0:T(8,128)S(1)}, f32[2,8,40,384]{3,2,1,0:T(8,128)S(1)}, bf16[384,384]{1,0:T(8,128)(2,1)S(1)}) custom-call(bf16[4,64,256]{2,1,0:T(8,128)(2,1)S(1)} %get-tuple-element.20.own_ref.own, bf16[4,40,256]{2,1,0:T(8,128)(2,1)S(1)} %collective-permute-done.got_ref.got, bf16[8,48,128]{2,1,0:T(8,128)(2,1)S(1)} %collective-permute-done.1.near_in), custom_call_target="tpu_custom_call" | custom-call | tf_op jit(solution)/shard_map/pallas_call | solution.py:536
  16.0 0.5 %collective-permute-done.5.got_ref.got = bf16[4,40,256]{2,1,0:T(8,128)(2,1)S(1)} collective-permute-done((bf16[4,40,256]{2,1,0:T(8,128)(2,1)S(1)}, bf16[4,40,256]{2,1,0:T(8,128)(2,1)S(1)}, u32[]{:S(2)}, u32[]{:S(2)}) %collective-permute-start.5) | collective-permute-done | bytes 81952 | tf_op jit(solution)/shard_map/ppermute | solution.py:592
  16.6 0.1 collective-permute-start.8
  16.6 0.5 %collective-permute-start.7 = (bf16[2,32,256]{2,1,0:T(8,128)(2,1)S(1)}, bf16[2,32,256]{2,1,0:T(8,128)(2,1)S(1)}, u32[]{:S(2)}, u32[]{:S(2)}) collective-permute-start(bf16[2,32,256]{2,1,0:T(8,128)(2,1)S(1)} %get-tuple-element.33), channel_id=1, source_target_pairs={{0,1},{2,6},{4,8},{6,2},{8,4},{10,14},{12,13},{14,10},{1,0},{3,7},... | collective-permute-start | bytes 98312 | tf_op jit(solution)/shard_map/ppermute | solution.py:610
  17.1 0.1 collective-permute-start.6
  17.2 0.1 copy.7
  17.4 1.1 %collective-permute-done.6.near_in = bf16[8,48,128]{2,1,0:T(8,128)(2,1)S(1)} collective-permute-done((bf16[8,48,128]{2,1,0:T(8,128)(2,1)S(1)}, bf16[8,48,128]{2,1,0:T(8,128)(2,1)S(1)}, u32[]{:S(2)}, u32[]{:S(2)}) %collective-permute-start.6) | collective-permute-done | bytes 98336 | tf_op jit(solution)/shard_map/ppermute | solution.py:609
  18.4 0.2 shard_map.51.warped
  18.7 1.2 %shard_map.52.warped_boxes = f32[3,8,40,384]{3,2,1,0:T(8,128)S(1)} custom-call(f32[8,40,384]{2,1,0:T(8,128)S(1)} %get-tuple-element.22.fixed_ref.fixed, f32[8,40,384]{2,1,0:T(8,128)S(1)} %shard_map.51.warped, bf16[384,384]{1,0:T(8,128)(2,1)S(1)} %get-tuple-element.32.band), custom_call_target="tpu_custom_call" | custom-call | tf_op jit(solution)/shard_map/pallas_call | solution.py:536
  19.8 0.0 collective-permute-done.8.far_rims
  19.8 0.0 collective-permute-done.7.rims
  19.8 3.0 %shard_map.53 = f32[24,16]{1,0:T(8,128)S(1)} custom-call(f32[8,40,384]{2,1,0:T(8,128)S(1)} %get-tuple-element.22.fixed_ref.fixed, f32[8,40,384]{2,1,0:T(8,128)S(1)} %shard_map.51.warped, f32[2,8,40,384]{3,2,1,0:T(8,128)S(1)} %get-tuple-element.31.fixed_boxes, f32[3,8,40,384]{3,2,1,0:T(8,128)S(1)} %shard_map.52.warped_boxes, ...), custom_call_target="tpu_custom_call" | custom-call | tf_op jit(solution)/shard_map/pallas_call | solution.py:536
  22.9 2.6 %collective-permute-start.11 = (f32[3,8,16]{2,1,0:T(8,128)S(1)}, f32[3,8,16]{2,1,0:T(8,128)S(1)}, u32[]{:S(2)}, u32[]{:S(2)}) collective-permute-start(f32[3,8,16]{2,1,0:T(8,128)S(1)} %bitcast.5), channel_id=1, source_target_pairs={{0,2},{2,4},{4,10},{6,0},{8,6},{10,12},{12,14},{14,8},{1,3},{3,5},... | collective-permute-start | bytes 4616 | tf_op jit(solution)/shard_map/ppermute | solution.py:634
  25.5 0.0 collective-permute-start.10
  25.5 2.3 %collective-permute-start.9 = (f32[3,8,16]{2,1,0:T(8,128)S(1)}, f32[3,8,16]{2,1,0:T(8,128)S(1)}, u32[]{:S(2)}, u32[]{:S(2)}) collective-permute-start(f32[3,8,16]{2,1,0:T(8,128)S(1)} %bitcast.7), channel_id=1, source_target_pairs={{0,2},{2,0},{1,3},{3,1},{4,6},{6,4},{5,7},{7,5},{8,10},{10,8},{9,1... | collective-permute-start | bytes 4616 | tf_op jit(solution)/shard_map/ppermute | solution.py:633
  27.8 0.0 collective-permute-done.11
  27.8 0.0 collective-permute-done.10
  27.8 1.7 %collective-permute-done.9 = f32[3,8,16]{2,1,0:T(8,128)S(1)} collective-permute-done((f32[3,8,16]{2,1,0:T(8,128)S(1)}, f32[3,8,16]{2,1,0:T(8,128)S(1)}, u32[]{:S(2)}, u32[]{:S(2)}) %collective-permute-start.9) | collective-permute-done | bytes 1568 | tf_op jit(solution)/shard_map/ppermute | solution.py:633
  29.5 0.6 %fusion.2 = f32[3,1,4,16]{3,2,1,0:T(4,128)} fusion(f32[3,8,16]{2,1,0:T(8,128)S(1)} %collective-permute-done.9, f32[3,8,16]{2,1,0:T(8,128)S(1)} %bitcast.8, f32[3,2,16]{2,1,0:T(2,128)S(1)} %get-tuple-element.36, f32[3,2,16]{2,1,0:T(2,128)S(1)} %get-tuple-element.35), kind=kLoop, calls=%fused_computation.7 | loop fusion | flops 576 | bytes 3072 | tf_op jit(solution)/shard_map/broadcast_in_dim | solution.py:641
  (10 shorter events, 0.2 us)
Async XLA Ops:
  1.2 8.0 %collective-permute-start.2 = (bf16[4,4,16,128]{3,2,1,0:T(8,128)(2,1)S(1)}, bf16[4,4,16,128]{3,2,1,0:T(8,128)(2,1)S(1)}, u32[]{:S(2)}, u32[]{:S(2)}) collective-permute-start(bf16[4,4,16,128]{3,2,1,0:T(8,128)(2,1)S(1)} %get-tuple-element.25), channel_id=1, source_target_pairs={{0,8},{4,12},{8,0},{12,4},{1,9},{5,13},{9,1},{13,5},{2,10},{6,14},... | collective-permute-start | bytes 196616 | tf_op jit(solution)/shard_map/ppermute | solution.py:585
  5.3 6.2 %collective-permute-start.3 = (bf16[4,4,16,128]{3,2,1,0:T(8,128)(2,1)S(1)}, bf16[4,4,16,128]{3,2,1,0:T(8,128)(2,1)S(1)}, u32[]{:S(2)}, u32[]{:S(2)}) collective-permute-start(bf16[4,4,16,128]{3,2,1,0:T(8,128)(2,1)S(1)} %get-tuple-element.26), channel_id=1, source_target_pairs={{0,12},{4,8},{8,4},{12,0},{1,13},{5,9},{9,5},{13,1},{2,14},{6,10},... | collective-permute-start | bytes 196616 | tf_op jit(solution)/shard_map/ppermute | solution.py:585
  6.7 5.0 %collective-permute-start.4 = (bf16[4,4,16,128]{3,2,1,0:T(8,128)(2,1)S(1)}, bf16[4,4,16,128]{3,2,1,0:T(8,128)(2,1)S(1)}, u32[]{:S(2)}, u32[]{:S(2)}) collective-permute-start(bf16[4,4,16,128]{3,2,1,0:T(8,128)(2,1)S(1)} %get-tuple-element.27), channel_id=1, source_target_pairs={{0,4},{4,0},{8,12},{12,8},{1,5},{5,1},{9,13},{13,9},{2,6},{6,2},{1... | collective-permute-start | bytes 196616 | tf_op jit(solution)/shard_map/ppermute | solution.py:585
  6.9 6.7 %collective-permute-start = (bf16[4,40,256]{2,1,0:T(8,128)(2,1)S(1)}, bf16[4,40,256]{2,1,0:T(8,128)(2,1)S(1)}, u32[]{:S(2)}, u32[]{:S(2)}) collective-permute-start(bf16[4,40,256]{2,1,0:T(8,128)(2,1)S(1)} %get-tuple-element.21), channel_id=1, source_target_pairs={{0,2},{2,0},{1,3},{3,1},{4,6},{6,4},{5,7},{7,5},{8,10},{10,8},{9,1... | collective-permute-start | bytes 245768 | tf_op jit(solution)/shard_map/ppermute | solution.py:588
  12.0 4.5 %collective-permute-start.5 = (bf16[4,40,256]{2,1,0:T(8,128)(2,1)S(1)}, bf16[4,40,256]{2,1,0:T(8,128)(2,1)S(1)}, u32[]{:S(2)}, u32[]{:S(2)}) collective-permute-start(bf16[4,40,256]{2,1,0:T(8,128)(2,1)S(1)} %get-tuple-element.29), channel_id=1, source_target_pairs={{0,2},{2,0},{1,3},{3,1},{4,6},{6,4},{5,7},{7,5},{8,10},{10,8},{9,1... | collective-permute-start | bytes 245768 | tf_op jit(solution)/shard_map/ppermute | solution.py:592
  13.6 1.4 %collective-permute-start.1 = (bf16[8,48,128]{2,1,0:T(8,128)(2,1)S(1)}, bf16[8,48,128]{2,1,0:T(8,128)(2,1)S(1)}, u32[]{:S(2)}, u32[]{:S(2)}) collective-permute-start(bf16[8,48,128]{2,1,0:T(8,128)(2,1)S(1)} %shard_map.47), channel_id=1, source_target_pairs={{0,1},{1,0},{2,3},{3,2},{4,5},{5,4},{6,7},{7,6},{8,9},{9,8},{10,11... | collective-permute-start | bytes 294920 | tf_op jit(solution)/shard_map/ppermute | solution.py:594
  16.6 3.3 %collective-permute-start.8 = (bf16[2,32,128]{2,1,0:T(8,128)(2,1)S(1)}, bf16[2,32,128]{2,1,0:T(8,128)(2,1)S(1)}, u32[]{:S(2)}, u32[]{:S(2)}) collective-permute-start(bf16[2,32,128]{2,1,0:T(8,128)(2,1)S(1)} %get-tuple-element.34), channel_id=1, source_target_pairs={{0,1},{2,7},{4,9},{6,3},{8,5},{10,15},{12,13},{14,11},{1,0},{3,6},... | collective-permute-start | bytes 49160 | tf_op jit(solution)/shard_map/ppermute | solution.py:611
  16.6 3.2 %collective-permute-start.7 = (bf16[2,32,256]{2,1,0:T(8,128)(2,1)S(1)}, bf16[2,32,256]{2,1,0:T(8,128)(2,1)S(1)}, u32[]{:S(2)}, u32[]{:S(2)}) collective-permute-start(bf16[2,32,256]{2,1,0:T(8,128)(2,1)S(1)} %get-tuple-element.33), channel_id=1, source_target_pairs={{0,1},{2,6},{4,8},{6,2},{8,4},{10,14},{12,13},{14,10},{1,0},{3,7},... | collective-permute-start | bytes 98312 | tf_op jit(solution)/shard_map/ppermute | solution.py:610
  17.1 1.3 %collective-permute-start.6 = (bf16[8,48,128]{2,1,0:T(8,128)(2,1)S(1)}, bf16[8,48,128]{2,1,0:T(8,128)(2,1)S(1)}, u32[]{:S(2)}, u32[]{:S(2)}) collective-permute-start(bf16[8,48,128]{2,1,0:T(8,128)(2,1)S(1)} %get-tuple-element.30), channel_id=1, source_target_pairs={{0,1},{1,0},{2,3},{3,2},{4,5},{5,4},{6,7},{7,6},{8,9},{9,8},{10,11... | collective-permute-start | bytes 294920 | tf_op jit(solution)/shard_map/ppermute | solution.py:609
  22.9 4.9 %collective-permute-start.11 = (f32[3,8,16]{2,1,0:T(8,128)S(1)}, f32[3,8,16]{2,1,0:T(8,128)S(1)}, u32[]{:S(2)}, u32[]{:S(2)}) collective-permute-start(f32[3,8,16]{2,1,0:T(8,128)S(1)} %bitcast.5), channel_id=1, source_target_pairs={{0,2},{2,4},{4,10},{6,0},{8,6},{10,12},{12,14},{14,8},{1,3},{3,5},... | collective-permute-start | bytes 4616 | tf_op jit(solution)/shard_map/ppermute | solution.py:634
  25.5 2.3 %collective-permute-start.10 = (f32[3,8,16]{2,1,0:T(8,128)S(1)}, f32[3,8,16]{2,1,0:T(8,128)S(1)}, u32[]{:S(2)}, u32[]{:S(2)}) collective-permute-start(f32[3,8,16]{2,1,0:T(8,128)S(1)} %bitcast.6), channel_id=1, source_target_pairs={{0,1},{2,6},{4,8},{6,2},{8,4},{10,14},{12,13},{14,10},{1,0},{3,7},... | collective-permute-start | bytes 4616 | tf_op jit(solution)/shard_map/ppermute | solution.py:635
  25.5 4.0 %collective-permute-start.9 = (f32[3,8,16]{2,1,0:T(8,128)S(1)}, f32[3,8,16]{2,1,0:T(8,128)S(1)}, u32[]{:S(2)}, u32[]{:S(2)}) collective-permute-start(f32[3,8,16]{2,1,0:T(8,128)S(1)} %bitcast.7), channel_id=1, source_target_pairs={{0,2},{2,0},{1,3},{3,1},{4,6},{6,4},{5,7},{7,5},{8,10},{10,8},{9,1... | collective-permute-start | bytes 4616 | tf_op jit(solution)/shard_map/ppermute | solution.py:633

commit v7 on v6

--- a/solution.py
+++ b/solution.py
@@ -355,15 +355,14 @@
 
 def lane_sums(exact, products, band):
     rows = (exact + products)[0].shape[0]
-    low = [value - value.astype(jnp.bfloat16).astype(jnp.float32) for value in products]
-    boxed = jnp.dot(
-        jnp.concatenate(exact + products + low, axis=0).astype(jnp.bfloat16), band[...],
-        preferred_element_type=jnp.float32,
-    )
-    pieces = [boxed[k * rows : (k + 1) * rows] for k in range(len(exact) + 2 * len(products))]
-    first = len(exact)
-    return pieces[:first] + [
-        pieces[first + k] + pieces[first + len(products) + k] for k in range(len(products))
+    skip = len(exact) * rows
+    value = jnp.concatenate(exact + products, axis=0)
+    high = value.astype(jnp.bfloat16)
+    low = (value - high.astype(jnp.float32))[skip:].astype(jnp.bfloat16)
+    boxed = jnp.dot(high, band[...], preferred_element_type=jnp.float32)
+    rest = boxed[skip:] + jnp.dot(low, band[...], preferred_element_type=jnp.float32)
+    return [boxed[k * rows : (k + 1) * rows] for k in range(len(exact))] + [
+        rest[k * rows : (k + 1) * rows] for k in range(len(products))
     ]
 
 

time: 30.2 us -> 30 us (level)
  transfers between devices with their start and end apart: 12 -> 12, of which waited for: 6 -> 6; matrix products, arithmetic and copies ran while one was open for 4% -> 4% of each run, Pallas kernels for 9% -> 10%
where the time goes in v7:
time: 30 us; the launch traced here: 29.9 us
  starting transfers between devices  14.3 us (48%)
  Pallas kernels  7.16 us (24%)
  waiting for transfers between devices  6.64 us (22%)
  local copies, waits for them, and re-layouts  0.91 us (3%)
  other arithmetic  0.77 us (3%)
    pallas_call x7, Pallas kernels, local_kernel(): pl.pallas_call(kernel, out_shape=[pltpu.VMEM(shape, dtype) for shape, dty...  5.96 us
    ppermute x3, starting transfers between devices, fast_body(): lax.ppermute(pack, 'tile', [(t, t ^ step) for t in range(tiles)])  5.68 us
    ppermute x1, starting transfers between devices, fast_body(): part_slant = lax.ppermute(part, trio, slant)  2.55 us
    ppermute x3, waiting for transfers between devices, fast_body(): lax.ppermute(pack, 'tile', [(t, t ^ step) for t in range(tiles)])  2.41 us
    ppermute x1, starting transfers between devices, fast_body(): across = lax.ppermute(part, 'gz', swap)  2.28 us
    ppermute x1, waiting for transfers between devices, fast_body(): across = lax.ppermute(part, 'gz', swap)  1.65 us
    ppermute x1, starting transfers between devices, fast_body(): warp_got = lax.ppermute(send, 'gz', swap)  1.55 us
    ppermute x1, starting transfers between devices, fast_body(): fixed_got = lax.ppermute(fixed_send, 'gz', swap)  1.49 us
  transfers between devices with their start and end apart: 12, of which 6 were waited for; matrix products, arithmetic and copies ran while one was open for 4% of the time, Pallas kernels for 10%

profile of v7, /device:TPU:0, one launch (start us, length us, event | category | flops | bytes accessed | tf_op | source)
XLA Modules:
  0.0 29.9 jit_solution(2046710033992877708)
XLA Ops:
  0.0 1.2 %shard_map.46 = (bf16[4,4,16,128]{3,2,1,0:T(8,128)(2,1)S(1)}, bf16[4,4,16,128]{3,2,1,0:T(8,128)(2,1)S(1)}, bf16[4,4,16,128]{3,2,1,0:T(8,128)(2,1)S(1)}, s32[4,8]...) custom-call(s32[4,8]{1,0:T(4,128)} %bitcast.9, ...), custom_call_target="tpu_custom_call" | custom-call | tf_op jit(solution)/shard_map/pallas_call | solution.py:560
  1.2 4.1 %collective-permute-start.2 = (bf16[4,4,16,128]{3,2,1,0:T(8,128)(2,1)S(1)}, bf16[4,4,16,128]{3,2,1,0:T(8,128)(2,1)S(1)}, u32[]{:S(2)}, u32[]{:S(2)}) collective-permute-start(bf16[4,4,16,128]{3,2,1,0:T(8,128)(2,1)S(1)} %get-tuple-element.25), channel_id=1, source_target_pairs={{0,8},{4,12},{8,0},{12,4},{1,9},{5,13},{9,1},{13,5},{2,10},{6,14},... | collective-permute-start | bytes 196616 | tf_op jit(solution)/shard_map/ppermute | solution.py:584
  5.3 1.3 %collective-permute-start.3 = (bf16[4,4,16,128]{3,2,1,0:T(8,128)(2,1)S(1)}, bf16[4,4,16,128]{3,2,1,0:T(8,128)(2,1)S(1)}, u32[]{:S(2)}, u32[]{:S(2)}) collective-permute-start(bf16[4,4,16,128]{3,2,1,0:T(8,128)(2,1)S(1)} %get-tuple-element.26), channel_id=1, source_target_pairs={{0,12},{4,8},{8,4},{12,0},{1,13},{5,9},{9,5},{13,1},{2,14},{6,10},... | collective-permute-start | bytes 196616 | tf_op jit(solution)/shard_map/ppermute | solution.py:584
  6.7 0.2 collective-permute-start.4
  6.9 1.5 %collective-permute-start = (bf16[4,40,256]{2,1,0:T(8,128)(2,1)S(1)}, bf16[4,40,256]{2,1,0:T(8,128)(2,1)S(1)}, u32[]{:S(2)}, u32[]{:S(2)}) collective-permute-start(bf16[4,40,256]{2,1,0:T(8,128)(2,1)S(1)} %get-tuple-element.21), channel_id=1, source_target_pairs={{0,2},{2,0},{1,3},{3,1},{4,6},{6,4},{5,7},{7,5},{8,10},{10,8},{9,1... | collective-permute-start | bytes 245768 | tf_op jit(solution)/shard_map/ppermute | solution.py:587
  8.5 0.8 %copy.6.shift_ref = s32[8,2]{1,0:T(8,128)S(1)} copy(s32[8,2]{0,1:T(2,128)} %bitcast.11) | data formatting | bytes 128 | tf_op jit(solution)/shard_map/squeeze | solution.py:550
  9.2 0.0 collective-permute-done.2.refs_0_
  9.2 2.3 %collective-permute-done.3.refs_1_ = bf16[4,4,16,128]{3,2,1,0:T(8,128)(2,1)S(1)} collective-permute-done((bf16[4,4,16,128]{3,2,1,0:T(8,128)(2,1)S(1)}, bf16[4,4,16,128]{3,2,1,0:T(8,128)(2,1)S(1)}, u32[]{:S(2)}, u32[]{:S(2)}) %collective-permute-start.3) | collective-permute-done | bytes 65568 | tf_op jit(solution)/shard_map/ppermute | solution.py:584
  11.5 0.1 collective-permute-done.4.refs_2_
  11.6 0.4 %shard_map.49 = (bf16[4,64,256]{2,1,0:T(8,128)(2,1)S(1)}, bf16[4,40,256]{2,1,0:T(8,128)(2,1)S(1)}) custom-call(s32[4,8]{1,0:T(4,128)S(1)} %get-tuple-element.23.source_ref, s32[8,2]{1,0:T(8,128)S(1)} %copy.6.shift_ref, bf16[4,64,256]{2,1,0:T(8,128)(2,1)S(1)} %get-tuple-element.24.moving_ref, bf16[4,4,16,128]{3,2,1,0:T(8,128)(2,1)S(1)} %collective-permute-done.2.refs_0_, ...), custom_call_target="tpu_custom_call" | custom-call | tf_op jit(solution)/shard_map/pallas_call | solution.py:535
  12.0 1.6 %collective-permute-start.5 = (bf16[4,40,256]{2,1,0:T(8,128)(2,1)S(1)}, bf16[4,40,256]{2,1,0:T(8,128)(2,1)S(1)}, u32[]{:S(2)}, u32[]{:S(2)}) collective-permute-start(bf16[4,40,256]{2,1,0:T(8,128)(2,1)S(1)} %get-tuple-element.29), channel_id=1, source_target_pairs={{0,2},{2,0},{1,3},{3,1},{4,6},{6,4},{5,7},{7,5},{8,10},{10,8},{9,1... | collective-permute-start | bytes 245768 | tf_op jit(solution)/shard_map/ppermute | solution.py:591
  13.6 0.0 collective-permute-done.got_ref.got
  13.6 0.1 collective-permute-start.1
  13.7 0.1 reduce-precision_convert_fusion
  13.8 1.2 %collective-permute-done.1.near_in = bf16[8,48,128]{2,1,0:T(8,128)(2,1)S(1)} collective-permute-done((bf16[8,48,128]{2,1,0:T(8,128)(2,1)S(1)}, bf16[8,48,128]{2,1,0:T(8,128)(2,1)S(1)}, u32[]{:S(2)}, u32[]{:S(2)}) %collective-permute-start.1) | collective-permute-done | bytes 98336 | tf_op jit(solution)/shard_map/ppermute | solution.py:593
  15.0 1.2 %shard_map.48 = (f32[8,40,384]{2,1,0:T(8,128)S(1)}, f32[2,8,40,384]{3,2,1,0:T(8,128)S(1)}, bf16[384,384]{1,0:T(8,128)(2,1)S(1)}) custom-call(bf16[4,64,256]{2,1,0:T(8,128)(2,1)S(1)} %get-tuple-element.20.own_ref.own, bf16[4,40,256]{2,1,0:T(8,128)(2,1)S(1)} %collective-permute-done.got_ref.got, bf16[8,48,128]{2,1,0:T(8,128)(2,1)S(1)} %collective-permute-done.1.near_in), custom_call_target="tpu_custom_call" | custom-call | tf_op jit(solution)/shard_map/pallas_call | solution.py:535
  16.2 0.3 %collective-permute-done.5.got_ref.got = bf16[4,40,256]{2,1,0:T(8,128)(2,1)S(1)} collective-permute-done((bf16[4,40,256]{2,1,0:T(8,128)(2,1)S(1)}, bf16[4,40,256]{2,1,0:T(8,128)(2,1)S(1)}, u32[]{:S(2)}, u32[]{:S(2)}) %collective-permute-start.5) | collective-permute-done | bytes 81952 | tf_op jit(solution)/shard_map/ppermute | solution.py:591
  16.6 0.1 collective-permute-start.8
  16.6 0.5 %collective-permute-start.7 = (bf16[2,32,256]{2,1,0:T(8,128)(2,1)S(1)}, bf16[2,32,256]{2,1,0:T(8,128)(2,1)S(1)}, u32[]{:S(2)}, u32[]{:S(2)}) collective-permute-start(bf16[2,32,256]{2,1,0:T(8,128)(2,1)S(1)} %get-tuple-element.33), channel_id=1, source_target_pairs={{0,1},{2,6},{4,8},{6,2},{8,4},{10,14},{12,13},{14,10},{1,0},{3,7},... | collective-permute-start | bytes 98312 | tf_op jit(solution)/shard_map/ppermute | solution.py:609
  17.1 0.1 collective-permute-start.6
  17.2 0.1 copy.7
  17.4 1.1 %collective-permute-done.6.near_in = bf16[8,48,128]{2,1,0:T(8,128)(2,1)S(1)} collective-permute-done((bf16[8,48,128]{2,1,0:T(8,128)(2,1)S(1)}, bf16[8,48,128]{2,1,0:T(8,128)(2,1)S(1)}, u32[]{:S(2)}, u32[]{:S(2)}) %collective-permute-start.6) | collective-permute-done | bytes 98336 | tf_op jit(solution)/shard_map/ppermute | solution.py:608
  18.4 0.2 shard_map.51.warped
  18.7 1.2 %shard_map.52.warped_boxes = f32[3,8,40,384]{3,2,1,0:T(8,128)S(1)} custom-call(f32[8,40,384]{2,1,0:T(8,128)S(1)} %get-tuple-element.22.fixed_ref.fixed, f32[8,40,384]{2,1,0:T(8,128)S(1)} %shard_map.51.warped, bf16[384,384]{1,0:T(8,128)(2,1)S(1)} %get-tuple-element.32.band), custom_call_target="tpu_custom_call" | custom-call | tf_op jit(solution)/shard_map/pallas_call | solution.py:535
  19.9 0.0 collective-permute-done.8.far_rims
  19.9 0.0 collective-permute-done.7.rims
  19.9 2.8 %shard_map.53 = f32[24,16]{1,0:T(8,128)S(1)} custom-call(f32[8,40,384]{2,1,0:T(8,128)S(1)} %get-tuple-element.22.fixed_ref.fixed, f32[8,40,384]{2,1,0:T(8,128)S(1)} %shard_map.51.warped, f32[2,8,40,384]{3,2,1,0:T(8,128)S(1)} %get-tuple-element.31.fixed_boxes, f32[3,8,40,384]{3,2,1,0:T(8,128)S(1)} %shard_map.52.warped_boxes, ...), custom_call_target="tpu_custom_call" | custom-call | tf_op jit(solution)/shard_map/pallas_call | solution.py:535
  22.8 2.5 %collective-permute-start.11 = (f32[3,8,16]{2,1,0:T(8,128)S(1)}, f32[3,8,16]{2,1,0:T(8,128)S(1)}, u32[]{:S(2)}, u32[]{:S(2)}) collective-permute-start(f32[3,8,16]{2,1,0:T(8,128)S(1)} %bitcast.5), channel_id=1, source_target_pairs={{0,2},{2,4},{4,10},{6,0},{8,6},{10,12},{12,14},{14,8},{1,3},{3,5},... | collective-permute-start | bytes 4616 | tf_op jit(solution)/shard_map/ppermute | solution.py:633
  25.3 0.0 collective-permute-start.10
  25.3 2.3 %collective-permute-start.9 = (f32[3,8,16]{2,1,0:T(8,128)S(1)}, f32[3,8,16]{2,1,0:T(8,128)S(1)}, u32[]{:S(2)}, u32[]{:S(2)}) collective-permute-start(f32[3,8,16]{2,1,0:T(8,128)S(1)} %bitcast.7), channel_id=1, source_target_pairs={{0,2},{2,0},{1,3},{3,1},{4,6},{6,4},{5,7},{7,5},{8,10},{10,8},{9,1... | collective-permute-start | bytes 4616 | tf_op jit(solution)/shard_map/ppermute | solution.py:632
  27.6 0.0 collective-permute-done.11
  27.6 0.0 collective-permute-done.10
  27.6 1.7 %collective-permute-done.9 = f32[3,8,16]{2,1,0:T(8,128)S(1)} collective-permute-done((f32[3,8,16]{2,1,0:T(8,128)S(1)}, f32[3,8,16]{2,1,0:T(8,128)S(1)}, u32[]{:S(2)}, u32[]{:S(2)}) %collective-permute-start.9) | collective-permute-done | bytes 1568 | tf_op jit(solution)/shard_map/ppermute | solution.py:632
  29.3 0.6 %fusion.2 = f32[3,1,4,16]{3,2,1,0:T(4,128)} fusion(f32[3,8,16]{2,1,0:T(8,128)S(1)} %collective-permute-done.9, f32[3,8,16]{2,1,0:T(8,128)S(1)} %bitcast.8, f32[3,2,16]{2,1,0:T(2,128)S(1)} %get-tuple-element.36, f32[3,2,16]{2,1,0:T(2,128)S(1)} %get-tuple-element.35), kind=kLoop, calls=%fused_computation.7 | loop fusion | flops 576 | bytes 3072 | tf_op jit(solution)/shard_map/broadcast_in_dim | solution.py:640
  (10 shorter events, 0.2 us)
Async XLA Ops:
  1.2 8.0 %collective-permute-start.2 = (bf16[4,4,16,128]{3,2,1,0:T(8,128)(2,1)S(1)}, bf16[4,4,16,128]{3,2,1,0:T(8,128)(2,1)S(1)}, u32[]{:S(2)}, u32[]{:S(2)}) collective-permute-start(bf16[4,4,16,128]{3,2,1,0:T(8,128)(2,1)S(1)} %get-tuple-element.25), channel_id=1, source_target_pairs={{0,8},{4,12},{8,0},{12,4},{1,9},{5,13},{9,1},{13,5},{2,10},{6,14},... | collective-permute-start | bytes 196616 | tf_op jit(solution)/shard_map/ppermute | solution.py:584
  5.3 6.2 %collective-permute-start.3 = (bf16[4,4,16,128]{3,2,1,0:T(8,128)(2,1)S(1)}, bf16[4,4,16,128]{3,2,1,0:T(8,128)(2,1)S(1)}, u32[]{:S(2)}, u32[]{:S(2)}) collective-permute-start(bf16[4,4,16,128]{3,2,1,0:T(8,128)(2,1)S(1)} %get-tuple-element.26), channel_id=1, source_target_pairs={{0,12},{4,8},{8,4},{12,0},{1,13},{5,9},{9,5},{13,1},{2,14},{6,10},... | collective-permute-start | bytes 196616 | tf_op jit(solution)/shard_map/ppermute | solution.py:584
  6.7 5.0 %collective-permute-start.4 = (bf16[4,4,16,128]{3,2,1,0:T(8,128)(2,1)S(1)}, bf16[4,4,16,128]{3,2,1,0:T(8,128)(2,1)S(1)}, u32[]{:S(2)}, u32[]{:S(2)}) collective-permute-start(bf16[4,4,16,128]{3,2,1,0:T(8,128)(2,1)S(1)} %get-tuple-element.27), channel_id=1, source_target_pairs={{0,4},{4,0},{8,12},{12,8},{1,5},{5,1},{9,13},{13,9},{2,6},{6,2},{1... | collective-permute-start | bytes 196616 | tf_op jit(solution)/shard_map/ppermute | solution.py:584
  6.9 6.7 %collective-permute-start = (bf16[4,40,256]{2,1,0:T(8,128)(2,1)S(1)}, bf16[4,40,256]{2,1,0:T(8,128)(2,1)S(1)}, u32[]{:S(2)}, u32[]{:S(2)}) collective-permute-start(bf16[4,40,256]{2,1,0:T(8,128)(2,1)S(1)} %get-tuple-element.21), channel_id=1, source_target_pairs={{0,2},{2,0},{1,3},{3,1},{4,6},{6,4},{5,7},{7,5},{8,10},{10,8},{9,1... | collective-permute-start | bytes 245768 | tf_op jit(solution)/shard_map/ppermute | solution.py:587
  12.0 4.5 %collective-permute-start.5 = (bf16[4,40,256]{2,1,0:T(8,128)(2,1)S(1)}, bf16[4,40,256]{2,1,0:T(8,128)(2,1)S(1)}, u32[]{:S(2)}, u32[]{:S(2)}) collective-permute-start(bf16[4,40,256]{2,1,0:T(8,128)(2,1)S(1)} %get-tuple-element.29), channel_id=1, source_target_pairs={{0,2},{2,0},{1,3},{3,1},{4,6},{6,4},{5,7},{7,5},{8,10},{10,8},{9,1... | collective-permute-start | bytes 245768 | tf_op jit(solution)/shard_map/ppermute | solution.py:591
  13.6 1.4 %collective-permute-start.1 = (bf16[8,48,128]{2,1,0:T(8,128)(2,1)S(1)}, bf16[8,48,128]{2,1,0:T(8,128)(2,1)S(1)}, u32[]{:S(2)}, u32[]{:S(2)}) collective-permute-start(bf16[8,48,128]{2,1,0:T(8,128)(2,1)S(1)} %shard_map.47), channel_id=1, source_target_pairs={{0,1},{1,0},{2,3},{3,2},{4,5},{5,4},{6,7},{7,6},{8,9},{9,8},{10,11... | collective-permute-start | bytes 294920 | tf_op jit(solution)/shard_map/ppermute | solution.py:593
  16.6 3.3 %collective-permute-start.8 = (bf16[2,32,128]{2,1,0:T(8,128)(2,1)S(1)}, bf16[2,32,128]{2,1,0:T(8,128)(2,1)S(1)}, u32[]{:S(2)}, u32[]{:S(2)}) collective-permute-start(bf16[2,32,128]{2,1,0:T(8,128)(2,1)S(1)} %get-tuple-element.34), channel_id=1, source_target_pairs={{0,1},{2,7},{4,9},{6,3},{8,5},{10,15},{12,13},{14,11},{1,0},{3,6},... | collective-permute-start | bytes 49160 | tf_op jit(solution)/shard_map/ppermute | solution.py:610
  16.6 3.3 %collective-permute-start.7 = (bf16[2,32,256]{2,1,0:T(8,128)(2,1)S(1)}, bf16[2,32,256]{2,1,0:T(8,128)(2,1)S(1)}, u32[]{:S(2)}, u32[]{:S(2)}) collective-permute-start(bf16[2,32,256]{2,1,0:T(8,128)(2,1)S(1)} %get-tuple-element.33), channel_id=1, source_target_pairs={{0,1},{2,6},{4,8},{6,2},{8,4},{10,14},{12,13},{14,10},{1,0},{3,7},... | collective-permute-start | bytes 98312 | tf_op jit(solution)/shard_map/ppermute | solution.py:609
  17.1 1.3 %collective-permute-start.6 = (bf16[8,48,128]{2,1,0:T(8,128)(2,1)S(1)}, bf16[8,48,128]{2,1,0:T(8,128)(2,1)S(1)}, u32[]{:S(2)}, u32[]{:S(2)}) collective-permute-start(bf16[8,48,128]{2,1,0:T(8,128)(2,1)S(1)} %get-tuple-element.30), channel_id=1, source_target_pairs={{0,1},{1,0},{2,3},{3,2},{4,5},{5,4},{6,7},{7,6},{8,9},{9,8},{10,11... | collective-permute-start | bytes 294920 | tf_op jit(solution)/shard_map/ppermute | solution.py:608
  22.8 4.8 %collective-permute-start.11 = (f32[3,8,16]{2,1,0:T(8,128)S(1)}, f32[3,8,16]{2,1,0:T(8,128)S(1)}, u32[]{:S(2)}, u32[]{:S(2)}) collective-permute-start(f32[3,8,16]{2,1,0:T(8,128)S(1)} %bitcast.5), channel_id=1, source_target_pairs={{0,2},{2,4},{4,10},{6,0},{8,6},{10,12},{12,14},{14,8},{1,3},{3,5},... | collective-permute-start | bytes 4616 | tf_op jit(solution)/shard_map/ppermute | solution.py:633
  25.3 2.3 %collective-permute-start.10 = (f32[3,8,16]{2,1,0:T(8,128)S(1)}, f32[3,8,16]{2,1,0:T(8,128)S(1)}, u32[]{:S(2)}, u32[]{:S(2)}) collective-permute-start(f32[3,8,16]{2,1,0:T(8,128)S(1)} %bitcast.6), channel_id=1, source_target_pairs={{0,1},{2,6},{4,8},{6,2},{8,4},{10,14},{12,13},{14,10},{1,0},{3,7},... | collective-permute-start | bytes 4616 | tf_op jit(solution)/shard_map/ppermute | solution.py:634
  25.3 3.9 %collective-permute-start.9 = (f32[3,8,16]{2,1,0:T(8,128)S(1)}, f32[3,8,16]{2,1,0:T(8,128)S(1)}, u32[]{:S(2)}, u32[]{:S(2)}) collective-permute-start(f32[3,8,16]{2,1,0:T(8,128)S(1)} %bitcast.7), channel_id=1, source_target_pairs={{0,2},{2,0},{1,3},{3,1},{4,6},{6,4},{5,7},{7,5},{8,10},{10,8},{9,1... | collective-permute-start | bytes 4616 | tf_op jit(solution)/shard_map/ppermute | solution.py:632

commit v8 on v6

--- a/solution.py
+++ b/solution.py
@@ -476,8 +476,12 @@
         term_b = -(ratio * ratio) * var_f
         term_c = -(term_a * sum_f + 2.0 * term_b * sum_w) * (1.0 / volume)
         values = [five(jnp.where(inside, value, 0.0), 0) for value in (term_a, term_b, term_c)]
-        for which, value in enumerate(lane_sums([], values, band)):
-            terms[which, z] = value
+        high, low = halves(jnp.concatenate(values, axis=0))
+        boxed = jnp.dot(high, band[...], preferred_element_type=jnp.float32) + jnp.dot(
+            low, band[...], preferred_element_type=jnp.float32
+        )
+        for which in range(3):
+            terms[which, z] = boxed[which * window : (which + 1) * window]
 
     for d in range(3):
         sums[d] = jnp.zeros((window, span), jnp.float32)

time: 30.2 us -> 30.1 us (level)
  no operation moved by 1% of the time
where the time goes in v8:
time: 30.1 us; the launch traced here: 29.9 us
  starting transfers between devices  14.4 us (48%)
  Pallas kernels  6.95 us (23%)
  waiting for transfers between devices  6.84 us (23%)
  local copies, waits for them, and re-layouts  0.91 us (3%)
  other arithmetic  0.77 us (3%)
    pallas_call x7, Pallas kernels, local_kernel(): pl.pallas_call(kernel, out_shape=[pltpu.VMEM(shape, dtype) for shape, dty...  5.74 us
    ppermute x3, starting transfers between devices, fast_body(): lax.ppermute(pack, 'tile', [(t, t ^ step) for t in range(tiles)])  5.68 us
    ppermute x1, starting transfers between devices, fast_body(): part_slant = lax.ppermute(part, trio, slant)  2.62 us
    ppermute x3, waiting for transfers between devices, fast_body(): lax.ppermute(pack, 'tile', [(t, t ^ step) for t in range(tiles)])  2.41 us
    ppermute x1, starting transfers between devices, fast_body(): across = lax.ppermute(part, 'gz', swap)  2.3 us
    ppermute x1, waiting for transfers between devices, fast_body(): across = lax.ppermute(part, 'gz', swap)  1.65 us
    ppermute x1, starting transfers between devices, fast_body(): warp_got = lax.ppermute(send, 'gz', swap)  1.55 us
    ppermute x1, starting transfers between devices, fast_body(): fixed_got = lax.ppermute(fixed_send, 'gz', swap)  1.49 us
  transfers between devices with their start and end apart: 12, of which 6 were waited for; matrix products, arithmetic and copies ran while one was open for 4% of the time, Pallas kernels for 9%

profile of v8, /device:TPU:0, one launch (start us, length us, event | category | flops | bytes accessed | tf_op | source)
XLA Modules:
  0.0 29.9 jit_solution(10196303169560799033)
XLA Ops:
  0.0 1.2 %shard_map.46 = (bf16[4,4,16,128]{3,2,1,0:T(8,128)(2,1)S(1)}, bf16[4,4,16,128]{3,2,1,0:T(8,128)(2,1)S(1)}, bf16[4,4,16,128]{3,2,1,0:T(8,128)(2,1)S(1)}, s32[4,8]...) custom-call(s32[4,8]{1,0:T(4,128)} %bitcast.9, ...), custom_call_target="tpu_custom_call" | custom-call | tf_op jit(solution)/shard_map/pallas_call | solution.py:565
  1.2 4.1 %collective-permute-start.2 = (bf16[4,4,16,128]{3,2,1,0:T(8,128)(2,1)S(1)}, bf16[4,4,16,128]{3,2,1,0:T(8,128)(2,1)S(1)}, u32[]{:S(2)}, u32[]{:S(2)}) collective-permute-start(bf16[4,4,16,128]{3,2,1,0:T(8,128)(2,1)S(1)} %get-tuple-element.25), channel_id=1, source_target_pairs={{0,8},{4,12},{8,0},{12,4},{1,9},{5,13},{9,1},{13,5},{2,10},{6,14},... | collective-permute-start | bytes 196616 | tf_op jit(solution)/shard_map/ppermute | solution.py:589
  5.3 1.3 %collective-permute-start.3 = (bf16[4,4,16,128]{3,2,1,0:T(8,128)(2,1)S(1)}, bf16[4,4,16,128]{3,2,1,0:T(8,128)(2,1)S(1)}, u32[]{:S(2)}, u32[]{:S(2)}) collective-permute-start(bf16[4,4,16,128]{3,2,1,0:T(8,128)(2,1)S(1)} %get-tuple-element.26), channel_id=1, source_target_pairs={{0,12},{4,8},{8,4},{12,0},{1,13},{5,9},{9,5},{13,1},{2,14},{6,10},... | collective-permute-start | bytes 196616 | tf_op jit(solution)/shard_map/ppermute | solution.py:589
  6.7 0.2 collective-permute-start.4
  6.9 1.5 %collective-permute-start = (bf16[4,40,256]{2,1,0:T(8,128)(2,1)S(1)}, bf16[4,40,256]{2,1,0:T(8,128)(2,1)S(1)}, u32[]{:S(2)}, u32[]{:S(2)}) collective-permute-start(bf16[4,40,256]{2,1,0:T(8,128)(2,1)S(1)} %get-tuple-element.21), channel_id=1, source_target_pairs={{0,2},{2,0},{1,3},{3,1},{4,6},{6,4},{5,7},{7,5},{8,10},{10,8},{9,1... | collective-permute-start | bytes 245768 | tf_op jit(solution)/shard_map/ppermute | solution.py:592
  8.5 0.8 %copy.6.shift_ref = s32[8,2]{1,0:T(8,128)S(1)} copy(s32[8,2]{0,1:T(2,128)} %bitcast.11) | data formatting | bytes 128 | tf_op jit(solution)/shard_map/squeeze | solution.py:555
  9.2 0.0 collective-permute-done.2.refs_0_
  9.2 2.3 %collective-permute-done.3.refs_1_ = bf16[4,4,16,128]{3,2,1,0:T(8,128)(2,1)S(1)} collective-permute-done((bf16[4,4,16,128]{3,2,1,0:T(8,128)(2,1)S(1)}, bf16[4,4,16,128]{3,2,1,0:T(8,128)(2,1)S(1)}, u32[]{:S(2)}, u32[]{:S(2)}) %collective-permute-start.3) | collective-permute-done | bytes 65568 | tf_op jit(solution)/shard_map/ppermute | solution.py:589
  11.5 0.1 collective-permute-done.4.refs_2_
  11.6 0.4 %shard_map.49 = (bf16[4,64,256]{2,1,0:T(8,128)(2,1)S(1)}, bf16[4,40,256]{2,1,0:T(8,128)(2,1)S(1)}) custom-call(s32[4,8]{1,0:T(4,128)S(1)} %get-tuple-element.23.source_ref, s32[8,2]{1,0:T(8,128)S(1)} %copy.6.shift_ref, bf16[4,64,256]{2,1,0:T(8,128)(2,1)S(1)} %get-tuple-element.24.moving_ref, bf16[4,4,16,128]{3,2,1,0:T(8,128)(2,1)S(1)} %collective-permute-done.2.refs_0_, ...), custom_call_target="tpu_custom_call" | custom-call | tf_op jit(solution)/shard_map/pallas_call | solution.py:540
  12.0 1.6 %collective-permute-start.5 = (bf16[4,40,256]{2,1,0:T(8,128)(2,1)S(1)}, bf16[4,40,256]{2,1,0:T(8,128)(2,1)S(1)}, u32[]{:S(2)}, u32[]{:S(2)}) collective-permute-start(bf16[4,40,256]{2,1,0:T(8,128)(2,1)S(1)} %get-tuple-element.29), channel_id=1, source_target_pairs={{0,2},{2,0},{1,3},{3,1},{4,6},{6,4},{5,7},{7,5},{8,10},{10,8},{9,1... | collective-permute-start | bytes 245768 | tf_op jit(solution)/shard_map/ppermute | solution.py:596
  13.6 0.0 collective-permute-done.got_ref.got
  13.6 0.1 collective-permute-start.1
  13.7 0.1 reduce-precision_convert_fusion
  13.8 1.2 %collective-permute-done.1.near_in = bf16[8,48,128]{2,1,0:T(8,128)(2,1)S(1)} collective-permute-done((bf16[8,48,128]{2,1,0:T(8,128)(2,1)S(1)}, bf16[8,48,128]{2,1,0:T(8,128)(2,1)S(1)}, u32[]{:S(2)}, u32[]{:S(2)}) %collective-permute-start.1) | collective-permute-done | bytes 98336 | tf_op jit(solution)/shard_map/ppermute | solution.py:598
  15.0 1.0 %shard_map.48 = (f32[8,40,384]{2,1,0:T(8,128)S(1)}, f32[2,8,40,384]{3,2,1,0:T(8,128)S(1)}, bf16[384,384]{1,0:T(8,128)(2,1)S(1)}) custom-call(bf16[4,64,256]{2,1,0:T(8,128)(2,1)S(1)} %get-tuple-element.20.own_ref.own, bf16[4,40,256]{2,1,0:T(8,128)(2,1)S(1)} %collective-permute-done.got_ref.got, bf16[8,48,128]{2,1,0:T(8,128)(2,1)S(1)} %collective-permute-done.1.near_in), custom_call_target="tpu_custom_call" | custom-call | tf_op jit(solution)/shard_map/pallas_call | solution.py:540
  16.0 0.5 %collective-permute-done.5.got_ref.got = bf16[4,40,256]{2,1,0:T(8,128)(2,1)S(1)} collective-permute-done((bf16[4,40,256]{2,1,0:T(8,128)(2,1)S(1)}, bf16[4,40,256]{2,1,0:T(8,128)(2,1)S(1)}, u32[]{:S(2)}, u32[]{:S(2)}) %collective-permute-start.5) | collective-permute-done | bytes 81952 | tf_op jit(solution)/shard_map/ppermute | solution.py:596
  16.6 0.1 collective-permute-start.8
  16.6 0.5 %collective-permute-start.7 = (bf16[2,32,256]{2,1,0:T(8,128)(2,1)S(1)}, bf16[2,32,256]{2,1,0:T(8,128)(2,1)S(1)}, u32[]{:S(2)}, u32[]{:S(2)}) collective-permute-start(bf16[2,32,256]{2,1,0:T(8,128)(2,1)S(1)} %get-tuple-element.33), channel_id=1, source_target_pairs={{0,1},{2,6},{4,8},{6,2},{8,4},{10,14},{12,13},{14,10},{1,0},{3,7},... | collective-permute-start | bytes 98312 | tf_op jit(solution)/shard_map/ppermute | solution.py:614
  17.1 0.1 collective-permute-start.6
  17.2 0.1 copy.7
  17.4 1.1 %collective-permute-done.6.near_in = bf16[8,48,128]{2,1,0:T(8,128)(2,1)S(1)} collective-permute-done((bf16[8,48,128]{2,1,0:T(8,128)(2,1)S(1)}, bf16[8,48,128]{2,1,0:T(8,128)(2,1)S(1)}, u32[]{:S(2)}, u32[]{:S(2)}) %collective-permute-start.6) | collective-permute-done | bytes 98336 | tf_op jit(solution)/shard_map/ppermute | solution.py:613
  18.4 0.2 shard_map.51.warped
  18.7 1.2 %shard_map.52.warped_boxes = f32[3,8,40,384]{3,2,1,0:T(8,128)S(1)} custom-call(f32[8,40,384]{2,1,0:T(8,128)S(1)} %get-tuple-element.22.fixed_ref.fixed, f32[8,40,384]{2,1,0:T(8,128)S(1)} %shard_map.51.warped, bf16[384,384]{1,0:T(8,128)(2,1)S(1)} %get-tuple-element.32.band), custom_call_target="tpu_custom_call" | custom-call | tf_op jit(solution)/shard_map/pallas_call | solution.py:540
  19.8 0.0 collective-permute-done.8.far_rims
  19.8 0.0 collective-permute-done.7.rims
  19.8 2.9 %shard_map.53 = f32[24,16]{1,0:T(8,128)S(1)} custom-call(f32[8,40,384]{2,1,0:T(8,128)S(1)} %get-tuple-element.22.fixed_ref.fixed, f32[8,40,384]{2,1,0:T(8,128)S(1)} %shard_map.51.warped, f32[2,8,40,384]{3,2,1,0:T(8,128)S(1)} %get-tuple-element.31.fixed_boxes, f32[3,8,40,384]{3,2,1,0:T(8,128)S(1)} %shard_map.52.warped_boxes, ...), custom_call_target="tpu_custom_call" | custom-call | tf_op jit(solution)/shard_map/pallas_call | solution.py:540
  22.7 2.6 %collective-permute-start.11 = (f32[3,8,16]{2,1,0:T(8,128)S(1)}, f32[3,8,16]{2,1,0:T(8,128)S(1)}, u32[]{:S(2)}, u32[]{:S(2)}) collective-permute-start(f32[3,8,16]{2,1,0:T(8,128)S(1)} %bitcast.5), channel_id=1, source_target_pairs={{0,2},{2,4},{4,10},{6,0},{8,6},{10,12},{12,14},{14,8},{1,3},{3,5},... | collective-permute-start | bytes 4616 | tf_op jit(solution)/shard_map/ppermute | solution.py:638
  25.3 0.0 collective-permute-start.10
  25.3 2.3 %collective-permute-start.9 = (f32[3,8,16]{2,1,0:T(8,128)S(1)}, f32[3,8,16]{2,1,0:T(8,128)S(1)}, u32[]{:S(2)}, u32[]{:S(2)}) collective-permute-start(f32[3,8,16]{2,1,0:T(8,128)S(1)} %bitcast.7), channel_id=1, source_target_pairs={{0,2},{2,0},{1,3},{3,1},{4,6},{6,4},{5,7},{7,5},{8,10},{10,8},{9,1... | collective-permute-start | bytes 4616 | tf_op jit(solution)/shard_map/ppermute | solution.py:637
  27.6 0.0 collective-permute-done.11
  27.7 0.0 collective-permute-done.10
  27.7 1.7 %collective-permute-done.9 = f32[3,8,16]{2,1,0:T(8,128)S(1)} collective-permute-done((f32[3,8,16]{2,1,0:T(8,128)S(1)}, f32[3,8,16]{2,1,0:T(8,128)S(1)}, u32[]{:S(2)}, u32[]{:S(2)}) %collective-permute-start.9) | collective-permute-done | bytes 1568 | tf_op jit(solution)/shard_map/ppermute | solution.py:637
  29.3 0.6 %fusion.2 = f32[3,1,4,16]{3,2,1,0:T(4,128)} fusion(f32[3,8,16]{2,1,0:T(8,128)S(1)} %collective-permute-done.9, f32[3,8,16]{2,1,0:T(8,128)S(1)} %bitcast.8, f32[3,2,16]{2,1,0:T(2,128)S(1)} %get-tuple-element.36, f32[3,2,16]{2,1,0:T(2,128)S(1)} %get-tuple-element.35), kind=kLoop, calls=%fused_computation.7 | loop fusion | flops 576 | bytes 3072 | tf_op jit(solution)/shard_map/broadcast_in_dim | solution.py:645
  (10 shorter events, 0.2 us)
Async XLA Ops:
  1.2 8.0 %collective-permute-start.2 = (bf16[4,4,16,128]{3,2,1,0:T(8,128)(2,1)S(1)}, bf16[4,4,16,128]{3,2,1,0:T(8,128)(2,1)S(1)}, u32[]{:S(2)}, u32[]{:S(2)}) collective-permute-start(bf16[4,4,16,128]{3,2,1,0:T(8,128)(2,1)S(1)} %get-tuple-element.25), channel_id=1, source_target_pairs={{0,8},{4,12},{8,0},{12,4},{1,9},{5,13},{9,1},{13,5},{2,10},{6,14},... | collective-permute-start | bytes 196616 | tf_op jit(solution)/shard_map/ppermute | solution.py:589
  5.3 6.2 %collective-permute-start.3 = (bf16[4,4,16,128]{3,2,1,0:T(8,128)(2,1)S(1)}, bf16[4,4,16,128]{3,2,1,0:T(8,128)(2,1)S(1)}, u32[]{:S(2)}, u32[]{:S(2)}) collective-permute-start(bf16[4,4,16,128]{3,2,1,0:T(8,128)(2,1)S(1)} %get-tuple-element.26), channel_id=1, source_target_pairs={{0,12},{4,8},{8,4},{12,0},{1,13},{5,9},{9,5},{13,1},{2,14},{6,10},... | collective-permute-start | bytes 196616 | tf_op jit(solution)/shard_map/ppermute | solution.py:589
  6.7 5.0 %collective-permute-start.4 = (bf16[4,4,16,128]{3,2,1,0:T(8,128)(2,1)S(1)}, bf16[4,4,16,128]{3,2,1,0:T(8,128)(2,1)S(1)}, u32[]{:S(2)}, u32[]{:S(2)}) collective-permute-start(bf16[4,4,16,128]{3,2,1,0:T(8,128)(2,1)S(1)} %get-tuple-element.27), channel_id=1, source_target_pairs={{0,4},{4,0},{8,12},{12,8},{1,5},{5,1},{9,13},{13,9},{2,6},{6,2},{1... | collective-permute-start | bytes 196616 | tf_op jit(solution)/shard_map/ppermute | solution.py:589
  6.9 6.7 %collective-permute-start = (bf16[4,40,256]{2,1,0:T(8,128)(2,1)S(1)}, bf16[4,40,256]{2,1,0:T(8,128)(2,1)S(1)}, u32[]{:S(2)}, u32[]{:S(2)}) collective-permute-start(bf16[4,40,256]{2,1,0:T(8,128)(2,1)S(1)} %get-tuple-element.21), channel_id=1, source_target_pairs={{0,2},{2,0},{1,3},{3,1},{4,6},{6,4},{5,7},{7,5},{8,10},{10,8},{9,1... | collective-permute-start | bytes 245768 | tf_op jit(solution)/shard_map/ppermute | solution.py:592
  12.0 4.5 %collective-permute-start.5 = (bf16[4,40,256]{2,1,0:T(8,128)(2,1)S(1)}, bf16[4,40,256]{2,1,0:T(8,128)(2,1)S(1)}, u32[]{:S(2)}, u32[]{:S(2)}) collective-permute-start(bf16[4,40,256]{2,1,0:T(8,128)(2,1)S(1)} %get-tuple-element.29), channel_id=1, source_target_pairs={{0,2},{2,0},{1,3},{3,1},{4,6},{6,4},{5,7},{7,5},{8,10},{10,8},{9,1... | collective-permute-start | bytes 245768 | tf_op jit(solution)/shard_map/ppermute | solution.py:596
  13.6 1.4 %collective-permute-start.1 = (bf16[8,48,128]{2,1,0:T(8,128)(2,1)S(1)}, bf16[8,48,128]{2,1,0:T(8,128)(2,1)S(1)}, u32[]{:S(2)}, u32[]{:S(2)}) collective-permute-start(bf16[8,48,128]{2,1,0:T(8,128)(2,1)S(1)} %shard_map.47), channel_id=1, source_target_pairs={{0,1},{1,0},{2,3},{3,2},{4,5},{5,4},{6,7},{7,6},{8,9},{9,8},{10,11... | collective-permute-start | bytes 294920 | tf_op jit(solution)/shard_map/ppermute | solution.py:598
  16.6 3.3 %collective-permute-start.8 = (bf16[2,32,128]{2,1,0:T(8,128)(2,1)S(1)}, bf16[2,32,128]{2,1,0:T(8,128)(2,1)S(1)}, u32[]{:S(2)}, u32[]{:S(2)}) collective-permute-start(bf16[2,32,128]{2,1,0:T(8,128)(2,1)S(1)} %get-tuple-element.34), channel_id=1, source_target_pairs={{0,1},{2,7},{4,9},{6,3},{8,5},{10,15},{12,13},{14,11},{1,0},{3,6},... | collective-permute-start | bytes 49160 | tf_op jit(solution)/shard_map/ppermute | solution.py:615
  16.6 3.2 %collective-permute-start.7 = (bf16[2,32,256]{2,1,0:T(8,128)(2,1)S(1)}, bf16[2,32,256]{2,1,0:T(8,128)(2,1)S(1)}, u32[]{:S(2)}, u32[]{:S(2)}) collective-permute-start(bf16[2,32,256]{2,1,0:T(8,128)(2,1)S(1)} %get-tuple-element.33), channel_id=1, source_target_pairs={{0,1},{2,6},{4,8},{6,2},{8,4},{10,14},{12,13},{14,10},{1,0},{3,7},... | collective-permute-start | bytes 98312 | tf_op jit(solution)/shard_map/ppermute | solution.py:614
  17.1 1.3 %collective-permute-start.6 = (bf16[8,48,128]{2,1,0:T(8,128)(2,1)S(1)}, bf16[8,48,128]{2,1,0:T(8,128)(2,1)S(1)}, u32[]{:S(2)}, u32[]{:S(2)}) collective-permute-start(bf16[8,48,128]{2,1,0:T(8,128)(2,1)S(1)} %get-tuple-element.30), channel_id=1, source_target_pairs={{0,1},{1,0},{2,3},{3,2},{4,5},{5,4},{6,7},{7,6},{8,9},{9,8},{10,11... | collective-permute-start | bytes 294920 | tf_op jit(solution)/shard_map/ppermute | solution.py:613
  22.7 4.9 %collective-permute-start.11 = (f32[3,8,16]{2,1,0:T(8,128)S(1)}, f32[3,8,16]{2,1,0:T(8,128)S(1)}, u32[]{:S(2)}, u32[]{:S(2)}) collective-permute-start(f32[3,8,16]{2,1,0:T(8,128)S(1)} %bitcast.5), channel_id=1, source_target_pairs={{0,2},{2,4},{4,10},{6,0},{8,6},{10,12},{12,14},{14,8},{1,3},{3,5},... | collective-permute-start | bytes 4616 | tf_op jit(solution)/shard_map/ppermute | solution.py:638
  25.3 2.3 %collective-permute-start.10 = (f32[3,8,16]{2,1,0:T(8,128)S(1)}, f32[3,8,16]{2,1,0:T(8,128)S(1)}, u32[]{:S(2)}, u32[]{:S(2)}) collective-permute-start(f32[3,8,16]{2,1,0:T(8,128)S(1)} %bitcast.6), channel_id=1, source_target_pairs={{0,1},{2,6},{4,8},{6,2},{8,4},{10,14},{12,13},{14,10},{1,0},{3,7},... | collective-permute-start | bytes 4616 | tf_op jit(solution)/shard_map/ppermute | solution.py:639
  25.3 4.0 %collective-permute-start.9 = (f32[3,8,16]{2,1,0:T(8,128)S(1)}, f32[3,8,16]{2,1,0:T(8,128)S(1)}, u32[]{:S(2)}, u32[]{:S(2)}) collective-permute-start(f32[3,8,16]{2,1,0:T(8,128)S(1)} %bitcast.7), channel_id=1, source_target_pairs={{0,2},{2,0},{1,3},{3,1},{4,6},{6,4},{5,7},{7,5},{8,10},{10,8},{9,1... | collective-permute-start | bytes 4616 | tf_op jit(solution)/shard_map/ppermute | solution.py:637
